TPU v7x, 32 devices: a whole 2x2x4 slice. The times are simulated.
32 devices in a mesh: dp: 8 (over z, core), mp: 4 (over y, x).
Axes of the slice: x: 2, y: 2, z: 4, core: 2. Of those that a mesh axis runs over, the one named last changes fastest.
Arguments:
- prefix_input: bfloat16 [6528, 2048], P('dp'), may hold values from -6 to 6
- action_input: bfloat16 [16, 50, 32], P('dp'), may hold values from -6 to 6
- valid_dims: int32 [16], P('dp'), may hold values from 0 to 18, as said below
- slot_item: int32 [16], P('dp'), may hold values from -1 to 7, as said below
- segments: int32 [8, 816], P('dp'), may hold values from 0 to 3, never falling along the last dimension, each value on 1 to 408 neighbouring positions
- pre_gain_attn: bfloat16 [2048], P('dp'), may hold values from 0.099609375 to 1.8984375
- pre_query: bfloat16 [2048, 2048], P('dp', 'mp'), may hold values from -0.125 to 0.125
- pre_key: bfloat16 [2048, 256], P('dp'), may hold values from -0.125 to 0.125
- pre_value: bfloat16 [2048, 256], P('dp'), may hold values from -0.125 to 0.125
- pre_output: bfloat16 [2048, 2048], P('mp', 'dp'), may hold values from -2 to 2
- pre_gain_ffn: bfloat16 [2048], P('dp'), may hold values from 0.099609375 to 1.8984375
- pre_gate: bfloat16 [2048, 16384], P('dp', 'mp'), may hold values from -0.125 to 0.125
- pre_up: bfloat16 [2048, 16384], P('dp', 'mp'), may hold values from -0.125 to 0.125
- pre_down: bfloat16 [16384, 2048], P('mp', 'dp'), may hold values from -0.046875 to 0.046875
- act_embed: bfloat16 [32, 1024], P(None, 'dp'), may hold values from -1.5 to 1.5
- act_gain_attn: bfloat16 [1024], P('dp'), may hold values from 0.099609375 to 1.8984375
- act_query: bfloat16 [1024, 2048], P('dp', 'mp'), may hold values from -0.1875 to 0.1875
- act_key: bfloat16 [1024, 256], P('dp'), may hold values from -0.1875 to 0.1875
- act_value: bfloat16 [1024, 256], P('dp'), may hold values from -0.1875 to 0.1875
- act_output: bfloat16 [2048, 1024], P('mp', 'dp'), may hold values from -2 to 2
- act_gain_ffn: bfloat16 [1024], P('dp'), may hold values from 0.099609375 to 1.8984375
- act_gate: bfloat16 [1024, 4096], P('dp', 'mp'), may hold values from -0.1875 to 0.1875
- act_up: bfloat16 [1024, 4096], P('dp', 'mp'), may hold values from -0.1875 to 0.1875
- act_down: bfloat16 [4096, 1024], P('mp', 'dp'), may hold values from -0.09375 to 0.09375
- prefix_cotangent: bfloat16 [6528, 2048], P('dp'), may hold values from -6 to 6
- action_cotangent: bfloat16 [16, 50, 1024], P('dp'), may hold values from -6 to 6
Outputs:
- prefix_output: bfloat16 [6528, 2048], P('dp')
- action_output: bfloat16 [16, 50, 1024], P('dp')
- prefix_grad: float32 [6528, 2048], P('dp')
- action_grad: float32 [16, 50, 32], P('dp')
- grad_pre_gain_attn: float32 [2048], P('dp')
- grad_pre_query: float32 [2048, 2048], P('dp', 'mp')
- grad_pre_key: float32 [2048, 256], P('dp')
- grad_pre_value: float32 [2048, 256], P('dp')
- grad_pre_output: float32 [2048, 2048], P('mp', 'dp')
- grad_pre_gain_ffn: float32 [2048], P('dp')
- grad_pre_gate: float32 [2048, 16384], P('dp', 'mp')
- grad_pre_up: float32 [2048, 16384], P('dp', 'mp')
- grad_pre_down: float32 [16384, 2048], P('mp', 'dp')
- grad_act_embed: float32 [32, 1024], P(None, 'dp')
- grad_act_gain_attn: float32 [1024], P('dp')
- grad_act_query: float32 [1024, 2048], P('dp', 'mp')
- grad_act_key: float32 [1024, 256], P('dp')
- grad_act_value: float32 [1024, 256], P('dp')
- grad_act_output: float32 [2048, 1024], P('mp', 'dp')
- grad_act_gain_ffn: float32 [1024], P('dp')
- grad_act_gate: float32 [1024, 4096], P('dp', 'mp')
- grad_act_up: float32 [1024, 4096], P('dp', 'mp')
- grad_act_down: float32 [4096, 1024], P('mp', 'dp')
Inputs may be any that keep to these rules, and one draw needn't show every extreme that they name: `slot_item`: each of the 8 items stands in exactly one slot; -1 marks an empty slot; on each index of dp either all 2 slots are filled or none, and half of the indices are filled. `valid_dims`: 0 on empty slots, 7 or more on filled ones. `segments`: never falling along an item's prefix.
All inputs are finite; a program needn't handle non-finite values.
Results may differ from a plain program's by a relative error of at most 0.02.
Values may be sent and summed in bfloat16 or wider, within the bound.
A program may use at most 320 MiB of HBM per device.

v0:
```python
import jax
import jax.numpy as jnp
from jax import lax
from jax.sharding import PartitionSpec as P

HD = 256


EPS = 1e-06


def rms_gain(values, gain):
    return values * lax.rsqrt(jnp.mean(values * values, axis=-1, keepdims=True) + EPS) * gain


def glu_value(gate, upward):
    return jax.nn.gelu(gate, approximate=True) * upward


def dot_plain(left, right):
    return jnp.dot(left, right, preferred_element_type=jnp.float32)


def dot_left(left, right):
    return lax.dot_general(
        left, right, (((0,), (0,)), ((), ())), preferred_element_type=jnp.float32
    )


def dot_right(left, right):
    return lax.dot_general(
        left, right, (((1,), (1,)), ((), ())), preferred_element_type=jnp.float32
    )


def attend_forward(query, keys, values, allowed, scale):
    scores = jnp.einsum("blhd,bmd->bhlm", query, keys, preferred_element_type=jnp.float32) * scale
    masked = jnp.where(allowed[:, None], scores, -1e30)
    top = jnp.max(masked, axis=-1, keepdims=True)
    logsum = top + jnp.log(jnp.sum(jnp.exp(masked - top), axis=-1, keepdims=True))
    probs = jnp.exp(masked - logsum).astype(jnp.bfloat16)
    mixed = jnp.einsum("bhlm,bmd->blhd", probs, values, preferred_element_type=jnp.float32)
    return (mixed.astype(jnp.bfloat16), logsum)


def attend_backward(query, keys, values, allowed, logsum, grad_mixed, scale):
    scores = jnp.einsum("blhd,bmd->bhlm", query, keys, preferred_element_type=jnp.float32) * scale
    masked = jnp.where(allowed[:, None], scores, -1e30)
    probs = jnp.exp(masked - logsum)
    grad_probs = jnp.einsum(
        "blhd,bmd->bhlm", grad_mixed, values, preferred_element_type=jnp.float32
    )
    centred = grad_probs - jnp.sum(probs * grad_probs, axis=-1, keepdims=True)
    grad_scores = (probs * centred).astype(jnp.bfloat16)
    grad_query = (
        jnp.einsum("bhlm,bmd->blhd", grad_scores, keys, preferred_element_type=jnp.float32) * scale
    )
    grad_keys = (
        jnp.einsum("bhlm,blhd->bmd", grad_scores, query, preferred_element_type=jnp.float32) * scale
    )
    grad_values = jnp.einsum(
        "bhlm,blhd->bmd", probs.astype(jnp.bfloat16), grad_mixed, preferred_element_type=jnp.float32
    )
    return (grad_query, grad_keys, grad_values)


def ffn_forward(second, gain, w_gate, w_up, w_down):
    normed = rms_gain(second, gain.astype(jnp.float32)).astype(jnp.bfloat16)
    gate = dot_plain(normed, w_gate)
    upward = dot_plain(normed, w_up)
    hidden = glu_value(gate, upward).astype(jnp.bfloat16)
    return (normed, gate, upward, hidden, dot_plain(hidden, w_down))


def ffn_backward(normed, gate, upward, hidden, w_gate, w_up, w_down, grad_out):
    grad_hidden = dot_right(grad_out, w_down)
    unused, pull = jax.vjp(glu_value, gate, upward)
    grad_gate, grad_upward = pull(grad_hidden)
    grad_gate = grad_gate.astype(jnp.bfloat16)
    grad_upward = grad_upward.astype(jnp.bfloat16)
    grad_normed = dot_right(grad_gate, w_gate) + dot_right(grad_upward, w_up)
    return (
        grad_normed,
        dot_left(normed, grad_gate),
        dot_left(normed, grad_upward),
        dot_left(hidden, grad_out),
    )


def norm_backward(values, gain, grad_out):
    unused, pull = jax.vjp(rms_gain, values, gain.astype(jnp.float32))
    return pull(grad_out)


def local(
    prefix_input,
    action_input,
    valid_dims,
    slot_item,
    segments,
    pre_gain_attn,
    pre_query,
    pre_key,
    pre_value,
    pre_output,
    pre_gain_ffn,
    pre_gate,
    pre_up,
    pre_down,
    act_embed,
    act_gain_attn,
    act_query,
    act_key,
    act_value,
    act_output,
    act_gain_ffn,
    act_gate,
    act_up,
    act_down,
    prefix_cotangent,
    action_cotangent,
):
    fetched = (
        lax.all_gather(pre_gain_attn, "dp", axis=0, tiled=True),
        lax.all_gather(pre_query, "dp", axis=0, tiled=True),
        lax.all_gather(pre_key, "dp", axis=0, tiled=True),
        lax.all_gather(pre_value, "dp", axis=0, tiled=True),
        lax.all_gather(pre_output, "dp", axis=1, tiled=True),
        lax.all_gather(pre_gain_ffn, "dp", axis=0, tiled=True),
        lax.all_gather(pre_gate, "dp", axis=0, tiled=True),
        lax.all_gather(pre_up, "dp", axis=0, tiled=True),
        lax.all_gather(pre_down, "dp", axis=1, tiled=True),
        lax.all_gather(act_embed, "dp", axis=1, tiled=True),
        lax.all_gather(act_gain_attn, "dp", axis=0, tiled=True),
        lax.all_gather(act_query, "dp", axis=0, tiled=True),
        lax.all_gather(act_key, "dp", axis=0, tiled=True),
        lax.all_gather(act_value, "dp", axis=0, tiled=True),
        lax.all_gather(act_output, "dp", axis=1, tiled=True),
        lax.all_gather(act_gain_ffn, "dp", axis=0, tiled=True),
        lax.all_gather(act_gate, "dp", axis=0, tiled=True),
        lax.all_gather(act_up, "dp", axis=0, tiled=True),
        lax.all_gather(act_down, "dp", axis=1, tiled=True),
    )
    (
        p_gain_one,
        p_query,
        p_key,
        p_value,
        p_out,
        p_gain_two,
        p_gate,
        p_up,
        p_down,
        a_embed,
        a_gain_one,
        a_query,
        a_key,
        a_value,
        a_out,
        a_gain_two,
        a_gate,
        a_up,
        a_down,
    ) = fetched
    row_count = prefix_input.shape[0]
    items_dev, length = segments.shape
    slot_count, steps, dims_count = action_input.shape
    act_rows = slot_count * steps
    head_count = p_query.shape[1] // HD
    scale = HD ** (-0.5)
    x_pre = prefix_input.astype(jnp.float32)
    h1_pre = rms_gain(x_pre, p_gain_one.astype(jnp.float32)).astype(jnp.bfloat16)
    q_pre = dot_plain(h1_pre, p_query).astype(jnp.bfloat16)
    wkv_pre = jnp.concatenate([p_key, p_value], axis=1)
    kv_pre = dot_plain(h1_pre, wkv_pre).astype(jnp.bfloat16).reshape(items_dev, length, 2 * HD)
    allowed_pre = segments[:, :, None] >= segments[:, None, :]
    q_pre4 = q_pre.reshape(items_dev, length, head_count, HD)
    mixed_pre, logsum_pre = attend_forward(
        q_pre4, kv_pre[..., :HD], kv_pre[..., HD:], allowed_pre, scale
    )
    live = slot_item >= 0
    dims_mask = lax.broadcasted_iota(jnp.int32, (slot_count, dims_count), 1) < valid_dims[:, None]
    masked_in = (action_input * dims_mask[:, None, :].astype(jnp.bfloat16)).reshape(
        act_rows, dims_count
    )
    x_act = dot_plain(masked_in, a_embed)
    h1_act = rms_gain(x_act, a_gain_one.astype(jnp.float32)).astype(jnp.bfloat16)
    q_act = dot_plain(h1_act, a_query).astype(jnp.bfloat16)
    wkv_act = jnp.concatenate([a_key, a_value], axis=1)
    kv_act = dot_plain(h1_act, wkv_act).astype(jnp.bfloat16).reshape(slot_count, steps, 2 * HD)
    piece = lax.all_gather(kv_pre, "dp", axis=0, tiled=True)
    count = piece.shape[0]
    match = (slot_item[:, None] == lax.broadcasted_iota(jnp.int32, (1, count), 1)).astype(
        jnp.bfloat16
    )
    kv_slots = jnp.einsum("cn,npk->cpk", match, piece, preferred_element_type=jnp.float32).astype(
        jnp.bfloat16
    )
    kv_all = jnp.concatenate([kv_slots, kv_act], axis=1)
    allowed_act = jnp.ones((slot_count, steps, length + steps), dtype=bool)
    q_act4 = q_act.reshape(slot_count, steps, head_count, HD)
    mixed_act, logsum_act = attend_forward(
        q_act4, kv_all[..., :HD], kv_all[..., HD:], allowed_act, scale
    )
    flat_pre = mixed_pre.reshape(row_count, head_count * HD)
    flat_act = mixed_act.reshape(act_rows, head_count * HD)
    y_pre, y_act = lax.psum((dot_plain(flat_pre, p_out), dot_plain(flat_act, a_out)), "mp")
    x2_pre = x_pre + y_pre
    x2_act = x_act + y_act
    h2_pre, gate_pre, up_pre, hid_pre, z_pre_part = ffn_forward(
        x2_pre, p_gain_two, p_gate, p_up, p_down
    )
    h2_act, gate_act, up_act, hid_act, z_act_part = ffn_forward(
        x2_act, a_gain_two, a_gate, a_up, a_down
    )
    z_pre, z_act = (
        lax.psum(z_pre_part.astype(jnp.bfloat16), "mp").astype(jnp.float32),
        lax.psum(z_act_part.astype(jnp.bfloat16), "mp").astype(jnp.float32),
    )
    prefix_output = (x2_pre + z_pre).astype(jnp.bfloat16)
    action_output = (x2_act + z_act).astype(jnp.bfloat16).reshape(slot_count, steps, x_act.shape[1])
    again = (
        lax.all_gather(pre_gain_attn, "dp", axis=0, tiled=True),
        lax.all_gather(pre_query, "dp", axis=0, tiled=True),
        lax.all_gather(pre_key, "dp", axis=0, tiled=True),
        lax.all_gather(pre_value, "dp", axis=0, tiled=True),
        lax.all_gather(pre_output, "dp", axis=1, tiled=True),
        lax.all_gather(pre_gain_ffn, "dp", axis=0, tiled=True),
        lax.all_gather(pre_gate, "dp", axis=0, tiled=True),
        lax.all_gather(pre_up, "dp", axis=0, tiled=True),
        lax.all_gather(pre_down, "dp", axis=1, tiled=True),
        lax.all_gather(act_embed, "dp", axis=1, tiled=True),
        lax.all_gather(act_gain_attn, "dp", axis=0, tiled=True),
        lax.all_gather(act_query, "dp", axis=0, tiled=True),
        lax.all_gather(act_key, "dp", axis=0, tiled=True),
        lax.all_gather(act_value, "dp", axis=0, tiled=True),
        lax.all_gather(act_output, "dp", axis=1, tiled=True),
        lax.all_gather(act_gain_ffn, "dp", axis=0, tiled=True),
        lax.all_gather(act_gate, "dp", axis=0, tiled=True),
        lax.all_gather(act_up, "dp", axis=0, tiled=True),
        lax.all_gather(act_down, "dp", axis=1, tiled=True),
    )
    (
        b_gain_one,
        b_query,
        b_key,
        b_value,
        b_out,
        b_gain_two,
        b_gate,
        b_up,
        b_down,
        c_embed,
        c_gain_one,
        c_query,
        c_key,
        c_value,
        c_out,
        c_gain_two,
        c_gate,
        c_up,
        c_down,
    ) = again
    grad_z_act = (action_cotangent * live[:, None, None].astype(jnp.bfloat16)).reshape(
        act_rows, x_act.shape[1]
    )
    gh2_pre, g_gate_pre, g_up_pre, g_down_pre = ffn_backward(
        h2_pre, gate_pre, up_pre, hid_pre, b_gate, b_up, b_down, prefix_cotangent
    )
    gh2_act, g_gate_act, g_up_act, g_down_act = ffn_backward(
        h2_act, gate_act, up_act, hid_act, c_gate, c_up, c_down, grad_z_act
    )
    gh2_pre, gh2_act = lax.psum((gh2_pre, gh2_act), "mp")
    gx2n_pre, g_gain_two_pre = norm_backward(x2_pre, b_gain_two, gh2_pre)
    gx2n_act, g_gain_two_act = norm_backward(x2_act, c_gain_two, gh2_act)
    gx2_pre = prefix_cotangent.astype(jnp.float32) + gx2n_pre
    gx2_act = grad_z_act.astype(jnp.float32) + gx2n_act
    gy_pre = gx2_pre.astype(jnp.bfloat16)
    gy_act = gx2_act.astype(jnp.bfloat16)
    g_out_pre = dot_left(flat_pre, gy_pre)
    g_out_act = dot_left(flat_act, gy_act)
    gmix_pre = (
        dot_right(gy_pre, b_out).astype(jnp.bfloat16).reshape(items_dev, length, head_count, HD)
    )
    gmix_act = (
        dot_right(gy_act, c_out).astype(jnp.bfloat16).reshape(slot_count, steps, head_count, HD)
    )
    gq_pre, gk_pre, gv_pre = attend_backward(
        q_pre4, kv_pre[..., :HD], kv_pre[..., HD:], allowed_pre, logsum_pre, gmix_pre, scale
    )
    gq_act, gk_all, gv_all = attend_backward(
        q_act4, kv_all[..., :HD], kv_all[..., HD:], allowed_act, logsum_act, gmix_act, scale
    )
    gkv_all = jnp.concatenate([gk_all, gv_all], axis=-1)
    gkv_slots = gkv_all[:, :length]
    gkv_own = gkv_all[:, length:].reshape(act_rows, 2 * HD)
    match = (
        lax.broadcasted_iota(jnp.int32, (row_count * lax.axis_size("dp") // length, 1), 0)
        == slot_item[None, :]
    ).astype(jnp.float32)
    picked = jnp.einsum(
        "nc,cpk->npk",
        match,
        gkv_slots,
        precision=lax.Precision.HIGHEST,
        preferred_element_type=jnp.float32,
    )
    gkv_back = lax.psum_scatter(
        picked.reshape(row_count * lax.axis_size("dp"), 2 * HD).astype(jnp.bfloat16),
        "dp",
        scatter_dimension=0,
        tiled=True,
    ).astype(jnp.float32)
    gkv_pre_part = jnp.concatenate([gk_pre, gv_pre], axis=-1).reshape(row_count, 2 * HD) + gkv_back
    gqb_pre = gq_pre.reshape(row_count, head_count * HD).astype(jnp.bfloat16)
    gqb_act = gq_act.reshape(act_rows, head_count * HD).astype(jnp.bfloat16)
    gh1q_pre, gkv_pre, gh1q_act, gkv_act = lax.psum(
        (dot_right(gqb_pre, b_query), gkv_pre_part, dot_right(gqb_act, c_query), gkv_own), "mp"
    )
    gkvb_pre = gkv_pre.astype(jnp.bfloat16)
    gkvb_act = gkv_act.astype(jnp.bfloat16)
    wkv_pre_back = jnp.concatenate([b_key, b_value], axis=1)
    wkv_act_back = jnp.concatenate([c_key, c_value], axis=1)
    gh1_pre = gh1q_pre + dot_right(gkvb_pre, wkv_pre_back)
    gh1_act = gh1q_act + dot_right(gkvb_act, wkv_act_back)
    g_query_pre = dot_left(h1_pre, gqb_pre)
    g_query_act = dot_left(h1_act, gqb_act)
    g_kv_pre = dot_left(h1_pre, gkvb_pre)
    g_kv_act = dot_left(h1_act, gkvb_act)
    gxn_pre, g_gain_one_pre = norm_backward(x_pre, b_gain_one, gh1_pre)
    gxn_act, g_gain_one_act = norm_backward(x_act, c_gain_one, gh1_act)
    prefix_grad = gx2_pre + gxn_pre
    gxa = (gx2_act + gxn_act).astype(jnp.bfloat16)
    g_embed = dot_left(masked_in, gxa)
    action_grad = dot_right(gxa, c_embed).reshape(slot_count, steps, dims_count) * dims_mask[
        :, None, :
    ].astype(jnp.float32)
    summed = (
        lax.psum_scatter(
            g_gain_one_pre.astype(jnp.bfloat16), "dp", scatter_dimension=0, tiled=True
        ).astype(jnp.float32),
        lax.psum_scatter(
            g_query_pre.astype(jnp.bfloat16), "dp", scatter_dimension=0, tiled=True
        ).astype(jnp.float32),
        lax.psum_scatter(
            g_kv_pre[:, :HD].astype(jnp.bfloat16), "dp", scatter_dimension=0, tiled=True
        ).astype(jnp.float32),
        lax.psum_scatter(
            g_kv_pre[:, HD:].astype(jnp.bfloat16), "dp", scatter_dimension=0, tiled=True
        ).astype(jnp.float32),
        lax.psum_scatter(
            g_out_pre.astype(jnp.bfloat16), "dp", scatter_dimension=1, tiled=True
        ).astype(jnp.float32),
        lax.psum_scatter(
            g_gain_two_pre.astype(jnp.bfloat16), "dp", scatter_dimension=0, tiled=True
        ).astype(jnp.float32),
        lax.psum_scatter(
            g_gate_pre.astype(jnp.bfloat16), "dp", scatter_dimension=0, tiled=True
        ).astype(jnp.float32),
        lax.psum_scatter(
            g_up_pre.astype(jnp.bfloat16), "dp", scatter_dimension=0, tiled=True
        ).astype(jnp.float32),
        lax.psum_scatter(
            g_down_pre.astype(jnp.bfloat16), "dp", scatter_dimension=1, tiled=True
        ).astype(jnp.float32),
        lax.psum_scatter(
            g_embed.astype(jnp.bfloat16), "dp", scatter_dimension=1, tiled=True
        ).astype(jnp.float32),
        lax.psum_scatter(
            g_gain_one_act.astype(jnp.bfloat16), "dp", scatter_dimension=0, tiled=True
        ).astype(jnp.float32),
        lax.psum_scatter(
            g_query_act.astype(jnp.bfloat16), "dp", scatter_dimension=0, tiled=True
        ).astype(jnp.float32),
        lax.psum_scatter(
            g_kv_act[:, :HD].astype(jnp.bfloat16), "dp", scatter_dimension=0, tiled=True
        ).astype(jnp.float32),
        lax.psum_scatter(
            g_kv_act[:, HD:].astype(jnp.bfloat16), "dp", scatter_dimension=0, tiled=True
        ).astype(jnp.float32),
        lax.psum_scatter(
            g_out_act.astype(jnp.bfloat16), "dp", scatter_dimension=1, tiled=True
        ).astype(jnp.float32),
        lax.psum_scatter(
            g_gain_two_act.astype(jnp.bfloat16), "dp", scatter_dimension=0, tiled=True
        ).astype(jnp.float32),
        lax.psum_scatter(
            g_gate_act.astype(jnp.bfloat16), "dp", scatter_dimension=0, tiled=True
        ).astype(jnp.float32),
        lax.psum_scatter(
            g_up_act.astype(jnp.bfloat16), "dp", scatter_dimension=0, tiled=True
        ).astype(jnp.float32),
        lax.psum_scatter(
            g_down_act.astype(jnp.bfloat16), "dp", scatter_dimension=1, tiled=True
        ).astype(jnp.float32),
    )
    return (prefix_output, action_output, prefix_grad, action_grad) + tuple(summed)


def solution(mesh):
    return jax.shard_map(
        local,
        mesh=mesh,
        in_specs=(
            P("dp", None),
            P("dp", None, None),
            P("dp"),
            P("dp"),
            P("dp", None),
            P("dp"),
            P("dp", "mp"),
            P("dp", None),
            P("dp", None),
            P("mp", "dp"),
            P("dp"),
            P("dp", "mp"),
            P("dp", "mp"),
            P("mp", "dp"),
            P(None, "dp"),
            P("dp"),
            P("dp", "mp"),
            P("dp", None),
            P("dp", None),
            P("mp", "dp"),
            P("dp"),
            P("dp", "mp"),
            P("dp", "mp"),
            P("mp", "dp"),
            P("dp", None),
            P("dp", None, None),
        ),
        out_specs=(
            P("dp", None),
            P("dp", None, None),
            P("dp", None),
            P("dp", None, None),
            P("dp"),
            P("dp", "mp"),
            P("dp", None),
            P("dp", None),
            P("mp", "dp"),
            P("dp"),
            P("dp", "mp"),
            P("dp", "mp"),
            P("mp", "dp"),
            P(None, "dp"),
            P("dp"),
            P("dp", "mp"),
            P("dp", None),
            P("dp", None),
            P("mp", "dp"),
            P("dp"),
            P("dp", "mp"),
            P("dp", "mp"),
            P("mp", "dp"),
        ),
        check_vma=False,
    )
```

profile of v0, /device:TPU:0, one launch (start us, length us, event | category | flops | bytes accessed | tf_op | source)
XLA Modules:
  0.0 2514.6 jit_solution(5934202626278470101)
XLA Ops:
  36.8 21.0 all-gather.21.cloned.1.call-done
  156.3 62.0 %all-gather.43.cloned.1.call-done = bf16[6528,512]{1,0:T(8,128)(2,1)} async-done(((bf16[816,512]{1,0:T(8,128)(2,1)}), bf16[6528,512]{1,0:T(8,128)(2,1)}) %all-gather.43.cloned.1.call-update) | async-done | bytes 6684688 | tf_op jit(solution)/shard_map/all_gather | solution.py:191
  272.5 125.7 %all-reduce.20.cloned.1.call-done = (f32[816,2048]{1,0:T(8,128)}, f32[100,1024]{1,0:T(8,128)}) async-done(((f32[816,2048]{1,0:T(8,128)}, f32[100,1024]{1,0:T(8,128)}), (f32[816,2048]{1,0:T(8,128)}, f32[100,1024]{1,0:T(8,128)})) %all-reduce.20.cloned.1.call-update) | async-done | bytes 7094288 | tf_op jit(solution)/shard_map/psum | solution.py:207
  407.4 21.9 all-gather.37.cloned.1.call-done
  431.6 27.9 %all-gather.39.cloned.1.call-done = bf16[1024,1024]{1,0:T(8,128)(2,1)} async-done(((bf16[128,1024]{1,0:T(8,128)(2,1)}), bf16[1024,1024]{1,0:T(8,128)(2,1)}) %all-gather.39.cloned.1.call-update) | async-done | bytes 2097168 | tf_op jit(solution)/shard_map/all_gather | solution.py:141
  462.2 29.2 %all-gather.41.cloned.1.call-done = bf16[1024,1024]{1,0:T(8,128)(2,1)} async-done(((bf16[1024,128]{1,0:T(8,128)(2,1)}), bf16[1024,1024]{1,0:T(8,128)(2,1)}) %all-gather.41.cloned.1.call-update) | async-done | bytes 2097168 | tf_op jit(solution)/shard_map/all_gather | solution.py:142
  501.5 141.5 %all-gather.27.cloned.1.call-done = bf16[2048,4096]{1,0:T(8,128)(2,1)} async-done(((bf16[256,4096]{1,0:T(8,128)(2,1)}), bf16[2048,4096]{1,0:T(8,128)(2,1)}) %all-gather.27.cloned.1.call-update) | async-done | bytes 16777232 | tf_op jit(solution)/shard_map/all_gather | solution.py:130
  663.4 130.6 %all-gather.29.cloned.1.call-done = bf16[2048,4096]{1,0:T(8,128)(2,1)} async-done(((bf16[256,4096]{1,0:T(8,128)(2,1)}), bf16[2048,4096]{1,0:T(8,128)(2,1)}) %all-gather.29.cloned.1.call-update) | async-done | bytes 16777232 | tf_op jit(solution)/shard_map/all_gather | solution.py:131
  794.0 21.2 fusion.109
  815.2 130.3 %all-gather.31.cloned.1.call-done = bf16[4096,2048]{1,0:T(8,128)(2,1)} async-done(((bf16[4096,256]{1,0:T(8,128)(2,1)}), bf16[4096,2048]{1,0:T(8,128)(2,1)}) %all-gather.31.cloned.1.call-update) | async-done | bytes 16777232 | tf_op jit(solution)/shard_map/all_gather | solution.py:132
  945.6 34.1 %multiply_convert_fusion = (bf16[816,4096]{1,0:T(8,128)(2,1)}, bf16[816,4096]{1,0:T(8,128)(2,1)}, bf16[816,4096]{1,0:T(8,128)(2,1)}) fusion(f32[816,4096]{1,0:T(8,128)} %fusion.108, f32[816,4096]{1,0:T(8,128)} %fusion.109, bf16[816,2048]{1,0:T(8,128)(2,1)S(1)} %copy-done.28, bf16[4096,2048]{1,0:T(8,128)(2,1)} %all-gather.31.cloned.1.call-done), kind=kOutput, calls=%fused_computation.12 | convolution fusion | flops 13777108992 | bytes 66912256 | tf_op jit(solution)/shard_map/dot_general | solution.py:31
  999.7 22.5 convolution_add_fusion
  1024.9 20.7 convolution_convert_fusion.4
  1045.8 127.2 %all-reduce.18.cloned.1.call-done = (f32[816,2048]{1,0:T(8,128)}, f32[100,1024]{1,0:T(8,128)}) async-done(((f32[816,2048]{1,0:T(8,128)}, f32[100,1024]{1,0:T(8,128)}), (f32[816,2048]{1,0:T(8,128)}, f32[100,1024]{1,0:T(8,128)})) %all-reduce.18.cloned.1.call-update) | async-done | bytes 7094288 | tf_op jit(solution)/shard_map/psum | solution.py:273
  1174.7 97.2 %all-reduce.22.cloned.1.call-done = (bf16[816,2048]{1,0:T(8,128)(2,1)}, bf16[100,1024]{1,0:T(8,128)(2,1)}) async-done(((bf16[816,2048]{1,0:T(8,128)(2,1)}, bf16[100,1024]{1,0:T(8,128)(2,1)}), (bf16[816,2048]{1,0:T(8,128)(2,1)}, bf16[100,1024]{1,0:T(8,128)(2,1)})) %all-reduce.22.cloned.1.call-update) | async-done | bytes 3547152 | tf_op jit(solution)/shard_map/psum | solution.py:217
  1278.7 21.7 convolution_convert_fusion.3
  1382.7 121.1 %all-reduce.23 = (bf16[816,512]{1,0:T(8,128)(2,1)}, bf16[100,512]{1,0:T(8,128)(2,1)}) all-reduce(f32[816,512]{1,0:T(8,128)} %fusion.29, f32[100,512]{1,0:T(8,128)} %reshape.340), channel_id=1, replica_groups=mesh['dp'=8,'mp'=4] {'mp'}, use_global_device_ids=true, to_apply=%region_20.21 | all-reduce | flops 468992 | bytes 2813952 | tf_op jit(solution)/shard_map/psum | solution.py:317
  1503.7 81.1 %all-reduce.16.cloned.1.call-done = (f32[816,2048]{1,0:T(8,128)}, f32[100,1024]{1,0:T(8,128)}) async-done(((f32[816,2048]{1,0:T(8,128)}, f32[100,1024]{1,0:T(8,128)}), (f32[816,2048]{1,0:T(8,128)}, f32[100,1024]{1,0:T(8,128)})) %all-reduce.16.cloned.1.call-update) | async-done | bytes 7094288 | tf_op jit(solution)/shard_map/psum | solution.py:317
  1604.5 24.2 convolution_convert_fusion.2
  1629.0 24.3 convolution_convert_fusion.1
  1653.6 24.2 convolution_convert_fusion
  1702.0 28.1 %reduce-scatter.51.cloned.1.call-done = bf16[128,512]{1,0:T(8,128)(2,1)} async-done(((bf16[1024,512]{1,0:T(8,128)(2,1)}), bf16[128,512]{1,0:T(8,128)(2,1)}) %reduce-scatter.51.cloned.1.call-update) | async-done | bytes 131088
  1733.4 29.7 %reduce-scatter.39.cloned.1.call-done = bf16[128,512]{1,0:T(8,128)(2,1)} async-done(((bf16[1024,512]{1,0:T(8,128)(2,1)}), bf16[128,512]{1,0:T(8,128)(2,1)}) %reduce-scatter.39.cloned.1.call-update) | async-done | bytes 131088 | tf_op jit(solution)/shard_map/reduce_scatter | solution.py:372
  1764.7 34.5 %reduce-scatter.25.cloned.1.call-done = bf16[256,512]{1,0:T(8,128)(2,1)} async-done(((bf16[2048,512]{1,0:T(8,128)(2,1)}), bf16[256,512]{1,0:T(8,128)(2,1)}) %reduce-scatter.25.cloned.1.call-update) | async-done | bytes 262160 | tf_op jit(solution)/shard_map/reduce_scatter | solution.py:342
  1801.0 34.8 %reduce-scatter.31.cloned.1.call-done = bf16[512,256]{1,0:T(8,128)(2,1)} async-done(((bf16[512,2048]{1,0:T(8,128)(2,1)}), bf16[512,256]{1,0:T(8,128)(2,1)}) %reduce-scatter.31.cloned.1.call-update) | async-done | bytes 262160 | tf_op jit(solution)/shard_map/reduce_scatter | solution.py:351
  1849.2 27.4 %all-reduce.8 = (bf16[2048]{0:T(1024)(128)(2,1)S(1)}, bf16[2048]{0:T(1024)(128)(2,1)S(1)}, bf16[1024]{0:T(1024)(128)(2,1)S(1)}, bf16[1024]{0:T(1024)(128)(2,1)S(1)}) all-reduce(bf16[2048]{0:T(1024)(128)(2,1)S(1)} %get-tuple-element.94, bf16[2048]{0:T(1024)(128)(2,1)S(1)} %copy-done.72, ...), channel_id=4, replica_groups=mesh['dp'=8,'mp'=4] {'dp'}, use_global_device_ids=true, to_apply=%region_26.27.clone | all-reduce | flops 6144 | bytes 24576
  1900.4 29.8 %reduce-scatter.43.cloned.1.call-done = bf16[128,256]{1,0:T(8,128)(2,1)} async-done(((bf16[1024,256]{1,0:T(8,128)(2,1)}), bf16[128,256]{1,0:T(8,128)(2,1)}) %reduce-scatter.43.cloned.1.call-update) | async-done | bytes 65552 | tf_op jit(solution)/shard_map/reduce_scatter | solution.py:378
  1931.7 31.5 %reduce-scatter.27.cloned.1.call-done = bf16[256,256]{1,0:T(8,128)(2,1)} async-done(((bf16[2048,256]{1,0:T(8,128)(2,1)}), bf16[256,256]{1,0:T(8,128)(2,1)}) %reduce-scatter.27.cloned.1.call-update) | async-done | bytes 131088 | tf_op jit(solution)/shard_map/reduce_scatter | solution.py:345
  1964.8 31.9 %reduce-scatter.29.cloned.1.call-done = bf16[256,256]{1,0:T(8,128)(2,1)} async-done(((bf16[2048,256]{1,0:T(8,128)(2,1)}), bf16[256,256]{1,0:T(8,128)(2,1)}) %reduce-scatter.29.cloned.1.call-update) | async-done | bytes 131088 | tf_op jit(solution)/shard_map/reduce_scatter | solution.py:348
  1998.4 167.3 %reduce-scatter.33.cloned.1.call-done = bf16[256,4096]{1,0:T(8,128)(2,1)} async-done(((bf16[2048,4096]{1,0:T(8,128)(2,1)}), bf16[256,4096]{1,0:T(8,128)(2,1)}) %reduce-scatter.33.cloned.1.call-update) | async-done | bytes 2097168 | tf_op jit(solution)/shard_map/reduce_scatter | solution.py:357
  2169.7 165.0 %reduce-scatter.35.cloned.1.call-done = bf16[256,4096]{1,0:T(8,128)(2,1)} async-done(((bf16[2048,4096]{1,0:T(8,128)(2,1)}), bf16[256,4096]{1,0:T(8,128)(2,1)}) %reduce-scatter.35.cloned.1.call-update) | async-done | bytes 2097168 | tf_op jit(solution)/shard_map/reduce_scatter | solution.py:360
  2338.8 164.8 %reduce-scatter.37.cloned.1.call-done = bf16[4096,256]{1,0:T(8,128)(2,1)} async-done(((bf16[4096,2048]{1,0:T(8,128)(2,1)}), bf16[4096,256]{1,0:T(8,128)(2,1)}) %reduce-scatter.37.cloned.1.call-update) | async-done | bytes 2097168 | tf_op jit(solution)/shard_map/reduce_scatter | solution.py:363
  (427 shorter events, 443.0 us)
Async XLA Ops:
  7.9 49.8 %all-gather.21.cloned.1.call-start = ((), (), s32[]{:S(2)}) async-start(), calls=%async_computation.17 | async-start | bytes 1179648 | tf_op jit(solution)/shard_map/all_gather | solution.py:127
  8.7 120.6 %all-gather.33.cloned.1.call-start = ((), (), s32[]{:S(2)}) async-start(), calls=%async_computation.23 | async-start | bytes 1179648 | tf_op jit(solution)/shard_map/all_gather | solution.py:135
  9.4 123.7 %all-gather.23.cloned.1.call-start = ((), (), s32[]{:S(2)}) async-start(), calls=%async_computation.18 | async-start | bytes 2359296 | tf_op jit(solution)/shard_map/all_gather | solution.py:125
  10.0 139.7 %all-gather.25.cloned.1.call-start = ((), (), s32[]{:S(2)}) async-start(), calls=%async_computation.19 | async-start | bytes 2359296 | tf_op jit(solution)/shard_map/all_gather | solution.py:128
  10.6 207.7 %all-gather.43.cloned.1.call-start = ((), (), s32[]{:S(2)}) async-start(), calls=%async_computation.41 | async-start | bytes 7520256 | tf_op jit(solution)/shard_map/all_gather | solution.py:191
  64.6 177.9 %all-gather.35.cloned.1.call-start = ((), (), s32[]{:S(2)}) async-start(), calls=%async_computation.24 | async-start | bytes 1179648 | tf_op jit(solution)/shard_map/all_gather | solution.py:138
  65.4 332.9 %all-reduce.20.cloned.1.call-start = ((), (), s32[]{:S(2)}) async-start(), calls=%async_computation.47 | async-start | bytes 14221312 | tf_op jit(solution)/shard_map/psum | solution.py:207
  244.8 184.5 %all-gather.37.cloned.1.call-start = ((), (), s32[]{:S(2)}) async-start(), calls=%async_computation.25 | async-start | bytes 2359296 | tf_op jit(solution)/shard_map/all_gather | solution.py:140
  245.6 213.9 %all-gather.39.cloned.1.call-start = ((), (), s32[]{:S(2)}) async-start(), calls=%async_computation.26 | async-start | bytes 2359296 | tf_op jit(solution)/shard_map/all_gather | solution.py:141
  246.1 245.3 %all-gather.41.cloned.1.call-start = ((), (), s32[]{:S(2)}) async-start(), calls=%async_computation.27 | async-start | bytes 2359296 | tf_op jit(solution)/shard_map/all_gather | solution.py:142
  246.9 396.2 %all-gather.27.cloned.1.call-start = ((), (), s32[]{:S(2)}) async-start(), calls=%async_computation.20 | async-start | bytes 18874368 | tf_op jit(solution)/shard_map/all_gather | solution.py:130
  247.5 546.6 %all-gather.29.cloned.1.call-start = ((), (), s32[]{:S(2)}) async-start(), calls=%async_computation.21 | async-start | bytes 18874368 | tf_op jit(solution)/shard_map/all_gather | solution.py:131
  248.2 697.3 %all-gather.31.cloned.1.call-start = ((), (), s32[]{:S(2)}) async-start(), calls=%async_computation.22 | async-start | bytes 18874368 | tf_op jit(solution)/shard_map/all_gather | solution.py:132
  248.8 924.1 %all-reduce.18.cloned.1.call-start = ((), (), s32[]{:S(2)}) async-start(), calls=%async_computation.46 | async-start | bytes 14221312 | tf_op jit(solution)/shard_map/psum | solution.py:273
  1022.2 249.7 %all-reduce.22.cloned.1.call-start = ((), (), s32[]{:S(2)}) async-start(), calls=%async_computation.48 | async-start | bytes 7110656 | tf_op jit(solution)/shard_map/psum | solution.py:217
  1045.7 333.9 %reduce-scatter.23.cloned.1.call-start = ((), (), s32[]{:S(2)}) async-start(), calls=%async_computation.28 | async-start | bytes 7520256 | tf_op jit(solution)/shard_map/reduce_scatter | solution.py:308
  1305.8 279.1 %all-reduce.16.cloned.1.call-start = ((), (), s32[]{:S(2)}) async-start(), calls=%async_computation.45 | async-start | bytes 14221312 | tf_op jit(solution)/shard_map/psum | solution.py:317
  1337.0 343.5 %reduce-scatter.53.cloned.1.call-start = ((), (), s32[]{:S(2)}) async-start(), calls=%async_computation.44 | async-start | bytes 2359296
  1341.2 342.9 %reduce-scatter.45.cloned.1.call-start = ((), (), s32[]{:S(2)}) async-start(), calls=%async_computation.39 | async-start | bytes 2359296 | tf_op jit(solution)/shard_map/reduce_scatter | solution.py:387
  1343.4 353.3 %reduce-scatter.47.cloned.1.call-start = ((), (), s32[]{:S(2)}) async-start(), calls=%async_computation.40 | async-start | bytes 2359296 | tf_op jit(solution)/shard_map/reduce_scatter | solution.py:390
  1346.7 383.3 %reduce-scatter.51.cloned.1.call-start = ((), (), s32[]{:S(2)}) async-start(), calls=%async_computation.43 | async-start | bytes 1179648
  1351.6 411.4 %reduce-scatter.39.cloned.1.call-start = ((), (), s32[]{:S(2)}) async-start(), calls=%async_computation.36 | async-start | bytes 1179648 | tf_op jit(solution)/shard_map/reduce_scatter | solution.py:372
  1354.1 445.1 %reduce-scatter.25.cloned.1.call-start = ((), (), s32[]{:S(2)}) async-start(), calls=%async_computation.29 | async-start | bytes 2359296 | tf_op jit(solution)/shard_map/reduce_scatter | solution.py:342
  1359.3 476.5 %reduce-scatter.31.cloned.1.call-start = ((), (), s32[]{:S(2)}) async-start(), calls=%async_computation.32 | async-start | bytes 2359296 | tf_op jit(solution)/shard_map/reduce_scatter | solution.py:351
  1366.3 519.9 %reduce-scatter.49.cloned.1.call-start = ((), (), s32[]{:S(2)}) async-start(), calls=%async_computation.42 | async-start | bytes 294912
  1595.6 303.3 %reduce-scatter.41.cloned.1.call-start = ((), (), s32[]{:S(2)}) async-start(), calls=%async_computation.37 | async-start | bytes 589824 | tf_op jit(solution)/shard_map/reduce_scatter | solution.py:375
  1597.9 332.3 %reduce-scatter.43.cloned.1.call-start = ((), (), s32[]{:S(2)}) async-start(), calls=%async_computation.38 | async-start | bytes 589824 | tf_op jit(solution)/shard_map/reduce_scatter | solution.py:378
  1598.6 364.6 %reduce-scatter.27.cloned.1.call-start = ((), (), s32[]{:S(2)}) async-start(), calls=%async_computation.30 | async-start | bytes 1179648 | tf_op jit(solution)/shard_map/reduce_scatter | solution.py:345
  1603.9 392.8 %reduce-scatter.29.cloned.1.call-start = ((), (), s32[]{:S(2)}) async-start(), calls=%async_computation.31 | async-start | bytes 1179648 | tf_op jit(solution)/shard_map/reduce_scatter | solution.py:348
  1604.5 561.1 %reduce-scatter.33.cloned.1.call-start = ((), (), s32[]{:S(2)}) async-start(), calls=%async_computation.33 | async-start | bytes 18874368 | tf_op jit(solution)/shard_map/reduce_scatter | solution.py:357
  1628.7 706.0 %reduce-scatter.35.cloned.1.call-start = ((), (), s32[]{:S(2)}) async-start(), calls=%async_computation.34 | async-start | bytes 18874368 | tf_op jit(solution)/shard_map/reduce_scatter | solution.py:360
  1653.3 850.4 %reduce-scatter.37.cloned.1.call-start = ((), (), s32[]{:S(2)}) async-start(), calls=%async_computation.35 | async-start | bytes 18874368 | tf_op jit(solution)/shard_map/reduce_scatter | solution.py:363
  (101 other events, 3845.0 us)
Sparse Core Ops, SparseCore 0:
  9.6 24.8 all-gather.18
  59.4 21.9 all-gather.32
  82.9 34.9 all-gather.22
  119.3 30.3 all-gather.24
  151.2 67.0 all-gather.42
  219.9 22.5 all-gather.34
  247.3 150.9 all-reduce.19
  399.9 29.4 all-gather.36
  430.8 28.5 all-gather.38
  461.0 30.3 all-gather.40
  492.8 150.1 all-gather.26
  644.7 149.3 all-gather.28
  795.5 150.0 all-gather.30
  1022.3 150.5 all-reduce.17
  1177.2 94.6 all-reduce.21
  1305.9 73.6 reduce-scatter.22
  1383.6 201.1 all-reduce.15
  1587.1 36.0 reduce-scatter.52
  1625.3 34.4 reduce-scatter.44
  1662.2 34.5 reduce-scatter.46
  1699.0 31.0 reduce-scatter.50
  1732.3 30.6 reduce-scatter.38
  1765.2 33.9 reduce-scatter.24
  1801.5 34.2 reduce-scatter.30
  1838.5 29.0 reduce-scatter.48
  1869.7 29.1 reduce-scatter.40
  1901.1 29.0 reduce-scatter.42
  1932.6 30.5 reduce-scatter.26
  1966.0 30.6 reduce-scatter.28
  1999.2 166.3 reduce-scatter.32
  2168.1 166.6 reduce-scatter.34
  2337.1 166.5 reduce-scatter.36
  (1 shorter events, 21.5 us)
where the time goes:
time: 2520 us; the launch traced here: 2510 us
  waiting for transfers between devices  1770 us (70%)
  matrix products  345 us (14%)
  blocking collectives  237 us (9%)
  other arithmetic  92.5 us (4%)
  local copies, waits for them, and re-layouts  52.9 us (2%)
    reduce_scatter x1, waiting for transfers between devices, local(): lax.psum_scatter(g_gate_pre.astype(jnp.bfloat16), 'dp', scatter_dimension...  167 us
    reduce_scatter x1, waiting for transfers between devices, local(): lax.psum_scatter(g_up_pre.astype(jnp.bfloat16), 'dp', scatter_dimension=0...  165 us
    reduce_scatter x1, waiting for transfers between devices, local(): lax.psum_scatter(g_down_pre.astype(jnp.bfloat16), 'dp', scatter_dimension...  165 us
    all_gather x1, waiting for transfers between devices, local(): lax.all_gather(pre_gate, 'dp', axis=0, tiled=True)  142 us
    all_gather x1, waiting for transfers between devices, local(): lax.all_gather(pre_up, 'dp', axis=0, tiled=True)  131 us
    all_gather x1, waiting for transfers between devices, local(): lax.all_gather(pre_down, 'dp', axis=1, tiled=True)  130 us
    psum x1, waiting for transfers between devices, local(): gh2_pre, gh2_act = lax.psum((gh2_pre, gh2_act), 'mp')  127 us
    psum x1, waiting for transfers between devices, local(): lax.psum((dot_plain(flat_pre, p_out), dot_plain(flat_act, a_out)), 'mp')  126 us
  transfers between devices with their start and end apart: 33, of which 28 were waited for; matrix products, arithmetic and copies ran while one was open for 15% of the time, Pallas kernels for 0%

commit v1 on v0

v1 whole, which is shorter than its diff:
```python
import functools

import jax
import jax.numpy as jnp
from jax import lax
from jax.experimental import pallas as pl
from jax.experimental.pallas import tpu as pltpu
from jax.sharding import PartitionSpec as P

HD = 256
EPS = 1e-06
BF = jnp.bfloat16
F32 = jnp.float32


def rms_gain(values, gain):
    return values * lax.rsqrt(jnp.mean(values * values, axis=-1, keepdims=True) + EPS) * gain


def norm_backward(values, gain, grad_out):
    unused, pull = jax.vjp(rms_gain, values, gain)
    return pull(grad_out)


def glu_value(gate, upward):
    return jax.nn.gelu(gate, approximate=True) * upward


def dot_plain(left, right):
    return jnp.dot(left, right, preferred_element_type=F32)


def dot_left(left, right):
    return lax.dot_general(left, right, (((0,), (0,)), ((), ())), preferred_element_type=F32)


def dot_right(left, right):
    return lax.dot_general(left, right, (((1,), (1,)), ((), ())), preferred_element_type=F32)


def round_up(value, step):
    return -(-value // step) * step


def swap_mp(block, step):
    size = lax.axis_size("mp")
    return lax.ppermute(block, "mp", [(i, i ^ step) for i in range(size)])


def swap_core(block):
    size = lax.axis_size("dp")
    return lax.ppermute(block, "dp", [(i, i ^ 1) for i in range(size)])


def send_dp(block, step):
    size = lax.axis_size("dp")
    return lax.ppermute(block, "dp", [(i, (i + step) % size) for i in range(size)])


def pair_sum(parts):
    size, me = lax.axis_size("dp"), lax.axis_index("dp")
    parts = parts.reshape((size // 2, 2) + parts.shape[1:])
    here = lax.rem(me, 2)
    kept = lax.dynamic_index_in_dim(parts, here, 1, False)
    got = swap_core(lax.dynamic_index_in_dim(parts, 1 - here, 1, False))
    return (kept.astype(F32) + got.astype(F32)).astype(BF)


def reduce_dp(parts):
    size, me = lax.axis_size("dp"), lax.axis_index("dp")
    half = size // 2
    both = pair_sum(parts)
    total = 0.0
    for s in range(half):
        chip = lax.rem(me // 2 + s, half)
        block = lax.dynamic_index_in_dim(both, chip, 0, False)
        total = total + (send_dp(block, 2 * s) if s else block).astype(F32)
    return total


def gather_mp(block, axis):
    size = lax.axis_size("mp")
    return jnp.concatenate([block] + [swap_mp(block, s) for s in range(1, size)], axis=axis)


def reduce_mp(matrix, axis):
    size = lax.axis_size("mp")
    parts = jnp.split(matrix, size, axis=axis)
    total = parts[0].astype(F32)
    for s in range(1, size):
        total = total + swap_mp(parts[s].astype(BF), s).astype(F32)
    return total


def pick_mp(blocks, place):
    at = lax.axis_index("mp") ^ place
    block = blocks[0]
    for s in range(1, len(blocks)):
        block = jnp.where(at == s, blocks[s], block)
    return block


def own_order(array):
    col = lax.axis_index("mp")
    return jnp.stack(
        [lax.dynamic_index_in_dim(array, col ^ s, 0, False) for s in range(array.shape[0])]
    )


def pack(prefix, action):
    wider = ((0, 0), (0, prefix.shape[1] - action.shape[1]))
    return jnp.concatenate([prefix, jnp.pad(action, wider)], axis=0)


def unpack(block, rows, width):
    return block[:rows], block[rows:, :width]


MESH = pl.DeviceIdType.MESH
HBM = pl.BlockSpec(memory_space=pl.ANY)


def peers(n, m):
    me, col = lax.axis_index("dp"), lax.axis_index("mp")
    column = [(lax.rem(me + s, n), col) for s in range(1, n)]
    return column + [(me, col ^ s) for s in range(1, m)]


def greet(devices):
    barrier = pltpu.get_barrier_semaphore()
    for device in devices:
        pl.semaphore_signal(barrier, inc=1, device_id=device, device_id_type=MESH)
    pl.semaphore_wait(barrier, len(devices))


def remote(src, dst, sent, arrived, device):
    return pltpu.make_async_remote_copy(
        src_ref=src,
        dst_ref=dst,
        send_sem=sent,
        recv_sem=arrived,
        device_id=device,
        device_id_type=MESH,
    )


def at(start, size):
    return pl.ds(pl.multiple_of(start * size, size), size)


class Line:
    def __init__(self, own, place, sems, row):
        self.n = lax.axis_size("dp")
        self.me, self.col = lax.axis_index("dp"), lax.axis_index("mp")
        self.own, self.place, self.row = own, place, row
        self.sent, self.arrived, self.local = sems
        self.chips = self.n // 2
        self.chip = self.me // 2

    def copy(self, way, k):
        step = (2, -2)[way]
        origin = lax.rem(self.me - step * (k - 1) + 2 * self.n, self.n)
        source = self.own if k == 1 else self.place(origin)
        target = (lax.rem(self.me + step + self.n, self.n), self.col)
        slot = way * self.chips + k
        return remote(
            source,
            self.place(origin),
            self.sent.at[self.row, slot],
            self.arrived.at[self.row, slot],
            target,
        )

    def across(self, way, k):
        step = (2, -2)[way]
        origin = lax.rem(self.me - step * k + 2 * self.n, self.n)
        source = self.own if k == 0 else self.place(origin)
        slot = (2 + way) * self.chips + k
        return remote(
            source,
            self.place(origin),
            self.sent.at[self.row, slot],
            self.arrived.at[self.row, slot],
            (self.me ^ 1, self.col),
        )

    def sends(self, way, k):
        beyond = self.chip < self.chips - 1 if way == 0 else self.chip > 0
        return beyond & self.receives(way, k - 1)

    def receives(self, way, k):
        if k == 0:
            return self.chip >= 0
        return self.chip >= k if way == 0 else self.chip < self.chips - k

    def start(self):
        self.keep = pltpu.make_async_copy(self.own, self.place(self.me), self.local.at[self.row])
        self.keep.start()
        for way in (0, 1):
            pl.when(self.sends(way, 1))(self.copy(way, 1).start)
        self.across(0, 0).start()

    def step(self, k):
        for way in (0, 1):

            @pl.when(self.receives(way, k))
            def _(way=way):
                self.copy(way, k).wait_recv()
                self.across(way, k).start()

            if k < self.chips - 1:
                pl.when(self.sends(way, k + 1))(self.copy(way, k + 1).start)

    def finish(self):
        self.keep.wait()
        self.across(0, 0).wait()
        for way in (0, 1):
            for k in range(1, self.chips):
                pl.when(self.sends(way, k))(self.copy(way, k).wait_send)
                pl.when(self.receives(way, k))(self.across(way, k).wait)


def line_sems(count, n):
    return [
        pltpu.SemaphoreType.DMA((count, 2 * n)),
        pltpu.SemaphoreType.DMA((count, 2 * n)),
        pltpu.SemaphoreType.DMA((count,)),
    ]


def gather_kernel(n, m, count, places, shares, *refs):
    sources, results = refs[:count], refs[count : 2 * count]
    sent, arrived, local, share_sent, share_arrived = refs[2 * count :]
    me, col = lax.axis_index("dp"), lax.axis_index("mp")
    greet(peers(n, m))
    lines = []
    for a in range(count):
        place = functools.partial(places[a], results[a])
        lines.append(Line(sources[a], place, (sent, arrived, local), a))
        lines[-1].start()
    for k in range(1, n // 2):
        for line in lines:
            line.step(k)
    for line in lines:
        line.finish()

    def passed(x, a, s):
        whole = results[a].at[col]
        return remote(
            whole, whole, share_sent.at[x, s], share_arrived.at[x, s], (me, col ^ s)
        )

    copies = [passed(x, a, s) for x, a in enumerate(shares) for s in range(1, m)]
    for c in copies:
        c.start()
    for c in copies:
        c.wait()


def gather_all(arrays, shapes, places, shares, collective_id):
    n, m = lax.axis_size("dp"), lax.axis_size("mp")
    count = len(arrays)
    return pl.pallas_call(
        functools.partial(gather_kernel, n, m, count, places, shares),
        out_shape=[jax.ShapeDtypeStruct(s, a.dtype) for s, a in zip(shapes, arrays)],
        in_specs=[HBM] * count,
        out_specs=[HBM] * count,
        scratch_shapes=line_sems(count, n)
        + [pltpu.SemaphoreType.DMA((max(len(shares), 1), m))] * 2,
        compiler_params=pltpu.CompilerParams(collective_id=collective_id, has_side_effects=True),
        name="gather_all",
    )(*arrays)


def by_rows(size):
    return lambda ref, i: ref.at[at(i, size)]


def by_columns(size):
    return lambda ref, i: ref.at[:, at(i, size)]


def by_lead(ref, i):
    return ref.at[i]


def by_share(size):
    return lambda ref, i: ref.at[lax.axis_index("mp"), at(i, size)]


def deal_kernel(n, m, kinds, lines_count, *refs):
    count = len(kinds)
    total = count + lines_count
    sources, results = refs[:total], refs[total : 2 * total]
    sems = refs[2 * total :]
    deal_sent, deal_arrived, local = sems[:3]
    x_sent, x_arrived, y_sent, y_arrived = sems[3:7]
    xy_sent, xy_arrived, yx_sent, yx_arrived = sems[7:11]
    all_sent, all_arrived = sems[11:13]
    line_sent, line_arrived, line_local = sems[13:16]
    me, col = lax.axis_index("dp"), lax.axis_index("mp")
    greet(peers(n, m))
    beside_x, beside_y = (me, col ^ 1), (me, col ^ 2)

    def source(t, i):
        ref = sources[t]
        if kinds[t] == 2:
            return ref.at[i]
        if kinds[t] == 0:
            return ref.at[:, at(i, ref.shape[1] // n)]
        return ref.at[at(i, ref.shape[0] // n)]

    def region(t, i, place, part=None):
        ref = results[t]
        if kinds[t] == 2:
            if part is None:
                return ref.at[place, i]
            few = ref.shape[2] // 2
            return ref.at[place, i, pl.ds(part * few, few)]
        if kinds[t] == 0:
            rows, width = ref.shape[0] // n, ref.shape[1] // m
            row = i * rows
            columns = pl.ds(place * width, width)
        else:
            rows, width = ref.shape[0] // m, ref.shape[1] // n
            row = place * rows
            columns = at(i, width)
        if part is None:
            return ref.at[pl.ds(pl.multiple_of(row, rows), rows), columns]
        few = rows // 2
        return ref.at[pl.ds(pl.multiple_of(row + part * few, few), few), columns]

    def origin(s):
        return lax.rem(me - s + n, n)

    def deal(t, s):
        target = lax.rem(me + s, n)
        return remote(
            source(t, target), region(t, me, 0), deal_sent.at[t, s], deal_arrived.at[t, s],
            (target, col),
        )

    def keep(t):
        return pltpu.make_async_copy(source(t, me), region(t, me, 0), local.at[t])

    def pass_x(t, s):
        i = origin(s)
        return remote(
            region(t, i, 0), region(t, i, 1), x_sent.at[t, s], x_arrived.at[t, s], beside_x
        )

    def pass_y(t, s):
        i = origin(s)
        return remote(
            region(t, i, 0), region(t, i, 2), y_sent.at[t, s], y_arrived.at[t, s], beside_y
        )

    def pass_xy(t, s):
        i = origin(s)
        return remote(
            region(t, i, 1, 0), region(t, i, 3, 0), xy_sent.at[t, s], xy_arrived.at[t, s], beside_y
        )

    def pass_yx(t, s):
        i = origin(s)
        return remote(
            region(t, i, 2, 1), region(t, i, 3, 1), yx_sent.at[t, s], yx_arrived.at[t, s], beside_x
        )

    def pass_all(t, s, k):
        i = origin(s)
        slot = s * m + k
        return remote(
            region(t, i, 0), region(t, i, k), all_sent.at[t, slot], all_arrived.at[t, slot],
            (me, col ^ k),
        )

    def hand_on(t, s):
        if m == 4:
            pass_x(t, s).start()
            pass_y(t, s).start()
        else:
            for k in range(1, m):
                pass_all(t, s, k).start()

    def each(first, body):
        lax.fori_loop(first, n, lambda s, c: (body(s), c)[1], 0)

    def begin(t):
        keep(t).start()
        each(1, lambda s: deal(t, s).start())

    def arrive(t):
        keep(t).wait()
        hand_on(t, 0)

        def body(s):
            deal(t, s).wait_recv()
            hand_on(t, s)

        each(1, body)

    def relay(t):
        if m != 4:
            return

        def body(s):
            pass_x(t, s).wait_recv()
            pass_xy(t, s).start()
            pass_y(t, s).wait_recv()
            pass_yx(t, s).start()

        each(0, body)

    def finish(t):
        each(1, lambda s: deal(t, s).wait_send())

        def body(s):
            if m != 4:
                for k in range(1, m):
                    pass_all(t, s, k).wait()
                return
            pass_x(t, s).wait_send()
            pass_y(t, s).wait_send()
            pass_xy(t, s).wait()
            pass_yx(t, s).wait()

        each(0, body)

    lines = []
    for a in range(lines_count):
        ref = results[count + a]
        place = functools.partial(by_rows(ref.shape[0] // n), ref)
        lines.append(Line(sources[count + a], place, (line_sent, line_arrived, line_local), a))
    begin(0)
    begin(1)
    for t in range(count):
        arrive(t)
        if t + 2 < count:
            begin(t + 2)
        if t + 2 == count - 1:
            for line in lines:
                line.start()
        if t:
            relay(t - 1)
    relay(count - 1)
    for k in range(1, n // 2):
        for line in lines:
            line.step(k)
    for line in lines:
        line.finish()
    for t in range(count):
        finish(t)


def deal_all(weights, kinds, arrays, collective_id):
    n, m = lax.axis_size("dp"), lax.axis_size("mp")
    count, total = len(weights), len(weights) + len(arrays)
    shapes = []
    for w, kind in zip(weights, kinds):
        r, c = w.shape[-2:]
        if kind == 2:
            shapes.append((m,) + w.shape)
        else:
            shapes.append((n * r, m * (c // n)) if kind == 0 else (m * (r // n), n * c))
    shapes += [(n * a.shape[0], a.shape[1]) for a in arrays]
    pair = [pltpu.SemaphoreType.DMA((count, n))] * 2
    return pl.pallas_call(
        functools.partial(deal_kernel, n, m, kinds, len(arrays)),
        out_shape=[jax.ShapeDtypeStruct(s, BF) for s in shapes],
        in_specs=[HBM] * total,
        out_specs=[HBM] * total,
        scratch_shapes=pair
        + [pltpu.SemaphoreType.DMA((count,))]
        + pair * 4
        + [pltpu.SemaphoreType.DMA((count, n * m if m != 4 else 1))] * 2
        + line_sems(max(len(arrays), 1), n),
        compiler_params=pltpu.CompilerParams(collective_id=collective_id, has_side_effects=True),
        name="deal_all",
    )(*weights, *arrays)


def return_kernel(n, kinds, *refs):
    count = len(kinds)
    sources, results = refs[:count], refs[count : 2 * count]
    sent, arrived, local = refs[2 * count :]
    me, col = lax.axis_index("dp"), lax.axis_index("mp")
    greet(peers(n, 1))

    def source(t, i):
        ref = sources[t]
        if kinds[t] == 0:
            return ref.at[at(i, ref.shape[0] // n)]
        if kinds[t] == 1:
            return ref.at[:, at(i, ref.shape[1] // n)]
        return ref if kinds[t] == 3 else ref.at[i // 2 if kinds[t] == 2 else i]

    def place(t):
        ref = results[t]
        if kinds[t] == 0:
            return ref.at[:, at(me, ref.shape[1] // n)]
        if kinds[t] == 1:
            return ref.at[at(me, ref.shape[0] // n)]
        return ref.at[me // 2] if kinds[t] == 2 else ref.at[me]

    def move(t, s):
        target = lax.rem(me + s, n)
        return remote(
            source(t, target), place(t), sent.at[t, s], arrived.at[t, s], (target, col)
        )

    def keep(t):
        return pltpu.make_async_copy(source(t, me), place(t), local.at[t])

    def each(t, do):
        if kinds[t] == 2:
            lax.fori_loop(1, n // 2, lambda s, c: (do(t, 2 * s), c)[1], 0)
        else:
            lax.fori_loop(1, n, lambda s, c: (do(t, s), c)[1], 0)

    for t in range(count):
        keep(t).start()
        each(t, lambda t, s: move(t, s).start())
    for t in range(count):
        keep(t).wait()
        each(t, lambda t, s: move(t, s).wait())


def return_all(arrays, kinds, collective_id):
    n = lax.axis_size("dp")
    count = len(arrays)
    shapes = []
    for a, kind in zip(arrays, kinds):
        if kind == 0:
            shapes.append((a.shape[0] // n, a.shape[1] * n))
        elif kind == 1:
            shapes.append((a.shape[0] * n, a.shape[1] // n))
        else:
            shapes.append((n,) + a.shape if kind == 3 else a.shape)
    return pl.pallas_call(
        functools.partial(return_kernel, n, kinds),
        out_shape=[jax.ShapeDtypeStruct(s, a.dtype) for s, a in zip(shapes, arrays)],
        in_specs=[HBM] * count,
        out_specs=[HBM] * count,
        scratch_shapes=[
            pltpu.SemaphoreType.DMA((count, n)),
            pltpu.SemaphoreType.DMA((count, n)),
            pltpu.SemaphoreType.DMA((count,)),
        ],
        compiler_params=pltpu.CompilerParams(collective_id=collective_id, has_side_effects=True),
        name="return_all",
    )(*arrays)


def local(
    prefix_input,
    action_input,
    valid_dims,
    slot_item,
    segments,
    pre_gain_attn,
    pre_query,
    pre_key,
    pre_value,
    pre_output,
    pre_gain_ffn,
    pre_gate,
    pre_up,
    pre_down,
    act_embed,
    act_gain_attn,
    act_query,
    act_key,
    act_value,
    act_output,
    act_gain_ffn,
    act_gate,
    act_up,
    act_down,
    prefix_cotangent,
    action_cotangent,
):
    n, m = lax.axis_size("dp"), lax.axis_size("mp")
    me, col = lax.axis_index("dp"), lax.axis_index("mp")
    length, wide = prefix_input.shape
    slot_count, steps, dims_count = action_input.shape
    narrow = action_cotangent.shape[2]
    rq = round_up(-(-length // m), 16)
    aq = round_up(-(-steps // m), 16)
    rows, acts = m * rq, m * aq
    heads = pre_query.shape[1] // HD
    scale = HD ** (-0.5)
    kvw = 2 * HD // m

    d_pre, d_act = pre_query.shape[0], act_query.shape[0]
    lanes = 128

    def pad_rows(array, count):
        return jnp.pad(array, ((0, count - array.shape[0]), (0, 0)))

    def lane_rows(array):
        flat = array.reshape(-1)
        count = round_up(-(-flat.shape[0] // lanes), 16)
        return jnp.pad(flat, (0, count * lanes - flat.shape[0])).reshape(count, lanes)

    smalls = [pre_gain_attn, pre_gain_ffn, act_gain_attn, act_gain_ffn, act_embed, action_input]
    small = jnp.concatenate([lane_rows(a) for a in smalls], axis=0)
    ints = jnp.pad(jnp.stack([slot_item, valid_dims]), ((0, 6), (0, lanes - slot_count)))
    cot_rows = lax.dynamic_slice_in_dim(
        jnp.pad(action_cotangent, ((0, 0), (0, acts - steps), (0, 0))), col * aq, aq, 1
    ).reshape(slot_count * aq, narrow)

    def share_of(key, value):
        return lax.dynamic_slice_in_dim(
            jnp.concatenate([key, value], axis=1), col * kvw, kvw, 1
        )

    split = heads * HD
    small, ints, w_q_pre, w_q_act, w_kv_pre, w_kv_act, w_out_pre, w_out_act, cot_all = gather_all(
        [
            small,
            ints,
            pre_query,
            act_query,
            share_of(pre_key, pre_value),
            share_of(act_key, act_value),
            pre_output,
            act_output,
            cot_rows,
        ],
        [
            (n * small.shape[0], lanes),
            (n * 8, lanes),
            (wide, split),
            (narrow, split),
            (m, wide, kvw),
            (m, narrow, kvw),
            (split, wide),
            (n, split, d_act),
            (n * slot_count * aq, narrow),
        ],
        [
            by_rows(small.shape[0]),
            by_rows(8),
            by_rows(d_pre),
            by_rows(d_act),
            by_share(d_pre),
            by_share(d_act),
            by_columns(d_pre),
            by_lead,
            by_rows(slot_count * aq),
        ],
        (4, 5),
        1,
    )
    small = small.reshape(n, -1, lanes)
    smalls_all, begin = [], 0
    for a in smalls:
        count = round_up(-(-a.size // lanes), 16)
        flat = small[:, begin : begin + count].reshape(n, -1)[:, : a.size]
        smalls_all.append(flat.reshape((n,) + a.shape))
        begin += count
    gain_pa, gain_pf, gain_aa, gain_af = [g.reshape(-1).astype(F32) for g in smalls_all[:4]]
    embed = smalls_all[4].transpose(1, 0, 2).reshape(dims_count, narrow)
    act_all = smalls_all[5].reshape(n * slot_count, steps, dims_count)
    ints = ints.reshape(n, 8, lanes)
    slot_all = ints[:, 0, :slot_count].reshape(-1)
    valid_all = ints[:, 1, :slot_count].reshape(-1)
    cot_all = cot_all.reshape(n * slot_count, aq, narrow)
    w_out_act = w_out_act.transpose(1, 0, 2).reshape(split, narrow)
    w_in_pre = jnp.concatenate([w_q_pre] + [w_kv_pre[k] for k in range(m)], axis=1)
    w_in_act = jnp.concatenate([w_q_act] + [w_kv_act[k] for k in range(m)], axis=1)
    twice = wide // narrow

    def by_block(array):
        padded = jnp.pad(array, ((0, rows - length), (0, 0)))
        return own_order(padded.reshape(m, rq, array.shape[1]))

    x_blocks = by_block(prefix_input)
    gz_pre = by_block(prefix_cotangent)[0]
    seg = jnp.pad(segments[0], (0, rows - length), constant_values=1 << 20)
    seg = own_order(seg.reshape(m, rq)).reshape(rows)
    act_place = own_order(jnp.arange(acts, dtype=jnp.int32).reshape(m, aq)).reshape(acts)
    last = 1 << 10
    seg_q = jnp.concatenate([jnp.minimum(seg, last), jnp.full((acts,), last, jnp.int32)])
    seg_k = jnp.concatenate([seg, jnp.where(act_place < steps, last, 1 << 20)])
    allowed = seg_q[:, None] >= seg_k[None, :]

    mine = (slot_all == me).astype(F32)
    valid = jnp.sum(mine * valid_all.astype(F32))
    dims_mask = (lax.broadcasted_iota(jnp.int32, (1, dims_count), 1).astype(F32) < valid).astype(BF)
    act_in = jnp.sum(mine[:, None, None] * act_all.astype(F32), axis=0).astype(BF) * dims_mask
    act_in = own_order(
        jnp.pad(act_in, ((0, acts - steps), (0, 0))).reshape(m, aq, dims_count)
    ).reshape(acts, dims_count)

    x_pre = x_blocks.reshape(rows, wide).astype(F32)
    h1_pre = rms_gain(x_pre, gain_pa).astype(BF)
    x_act = dot_plain(act_in, embed)
    h1_act = rms_gain(x_act, gain_aa).astype(BF)

    in_pre = dot_plain(h1_pre, w_in_pre).astype(BF)
    in_act = dot_plain(h1_act, w_in_act).astype(BF)
    into_all = jnp.concatenate([in_pre, in_act], axis=0)
    query, kv_part = into_all[:, : heads * HD], into_all[:, heads * HD :]

    def reorder(array, s):
        if s == 0:
            return array
        pieces = [array[(r ^ s) * rq : (r ^ s) * rq + rq] for r in range(m)]
        pieces += [array[rows + (r ^ s) * aq : rows + (r ^ s) * aq + aq] for r in range(m)]
        return jnp.concatenate(pieces, axis=0)

    keys, values = kv_part[:, :HD], kv_part[:, HD:]

    probs, mixed = [], []
    for h in range(heads):
        scores = dot_right(query[:, h * HD : (h + 1) * HD], keys) * scale
        masked = jnp.where(allowed, scores, -1e30)
        top = jnp.max(masked, axis=-1, keepdims=True)
        raised = jnp.exp(masked - top)
        p = (raised / jnp.sum(raised, axis=-1, keepdims=True)).astype(BF)
        probs.append(p)
        mixed.append(dot_plain(p, values).astype(BF))
    mixed = jnp.concatenate(mixed, axis=1)

    def blocks_of(pre, act):
        return jnp.concatenate(
            [
                pack(pre[s * rq : (s + 1) * rq], act[s * aq : (s + 1) * aq])
                for s in range(m)
            ],
            axis=0,
        )

    def rows_of(blocks):
        pairs = [unpack(b, rq, narrow) for b in jnp.split(blocks, m, axis=0)]
        return jnp.concatenate([p[0] for p in pairs] + []), jnp.concatenate([p[1] for p in pairs])

    y_pre = dot_plain(mixed[:rows], w_out_pre).astype(BF)
    y_act = dot_plain(mixed[rows:], w_out_act).astype(BF)
    y = reduce_mp(blocks_of(y_pre, y_act), 0)
    y_pre, y_act = unpack(y, rq, narrow)
    x2_pre = x_pre[:rq] + y_pre
    x2_act = x_act[:aq] + y_act
    h2 = pack(rms_gain(x2_pre, gain_pf).astype(BF), rms_gain(x2_act, gain_af).astype(BF))


    def items_of(blocks):
        pairs = [unpack(b, rq, narrow) for b in jnp.split(blocks, n, axis=0)]
        return jnp.concatenate([p[0] for p in pairs]), jnp.concatenate([p[1] for p in pairs])

    def by_item(pre, act):
        return jnp.stack(
            [
                pack(pre[s * rq : (s + 1) * rq], act[s * aq : (s + 1) * aq])
                for s in range(n)
            ]
        )

    few = act_gate.shape[1] // n

    def columns_first(array):
        return array.reshape(array.shape[0], n, -1).transpose(1, 0, 2)

    act_weights = jnp.concatenate(
        [
            columns_first(act_gate),
            columns_first(act_up),
            act_down.reshape(n, few, d_act).transpose(0, 2, 1),
        ],
        axis=1,
    )
    wg, wu, wd, act_weights, h2_all, gz_pre_all = deal_all(
        [pre_gate, pre_up, pre_down, act_weights], (0, 0, 1, 2), [h2, gz_pre], 2
    )

    def square(array):
        return array.transpose(1, 2, 0, 3).reshape(narrow, m * few)

    ag, au = square(act_weights[:, :, :d_act]), square(act_weights[:, :, d_act : 2 * d_act])
    ad = square(act_weights[:, :, 2 * d_act :]).T
    h2_pre, h2_act = items_of(h2_all)
    match = (lax.broadcasted_iota(jnp.int32, (n, 1), 0) == slot_all[None, :]).astype(BF)
    gz_act_all = dot_plain(match, cot_all.reshape(cot_all.shape[0], -1)).astype(BF)
    gz_act_all = gz_act_all.reshape(n * aq, narrow)
    gz_act = lax.dynamic_slice_in_dim(gz_act_all, me * aq, aq, 0)

    def forward(h2_rows, gate_w, up_w, down_w):
        gate = dot_plain(h2_rows, gate_w)
        upward = dot_plain(h2_rows, up_w)
        hidden = glu_value(gate, upward).astype(BF)
        return gate.astype(BF), upward.astype(BF), hidden, dot_plain(hidden, down_w).astype(BF)

    def backward(h2_rows, gate, upward, hidden, gate_w, up_w, down_w, gz):
        grad_hidden = dot_right(gz, down_w)
        unused, pull = jax.vjp(glu_value, gate.astype(F32), upward.astype(F32))
        dgate, dup = pull(grad_hidden)
        dgate, dup = dgate.astype(BF), dup.astype(BF)
        dh2 = (dot_right(dgate, gate_w) + dot_right(dup, up_w)).astype(BF)
        return (
            dh2,
            dot_left(h2_rows, dgate).astype(BF),
            dot_left(h2_rows, dup).astype(BF),
            dot_left(hidden, gz).astype(BF),
        )

    gate_p, up_p, hid_p, z_p = forward(h2_pre, wg, wu, wd)
    gate_a, up_a, hid_a, z_a = forward(h2_act, ag, au, ad)
    dh2_p, g_gate_p, g_up_p, g_down_p = backward(
        h2_pre, gate_p, up_p, hid_p, wg, wu, wd, gz_pre_all
    )
    dh2_a, g_gate_a, g_up_a, g_down_a = backward(
        h2_act, gate_a, up_a, hid_a, ag, au, ad, gz_act_all
    )
    z_pre, z_act = unpack(reduce_dp(by_item(z_p, z_a)), rq, narrow)
    dh2_pre, dh2_act = unpack(reduce_dp(by_item(dh2_p, dh2_a)), rq, narrow)

    def natural(blocks, count):
        return jnp.concatenate([pick_mp(blocks, place) for place in range(m)], axis=0)[:count]

    out_pre = (x2_pre + z_pre).astype(BF)
    out_act = (x2_act + z_act).astype(BF)
    prefix_output = natural([out_pre] + [swap_mp(out_pre, s) for s in range(1, m)], length)
    out_act = natural([out_act] + [swap_mp(out_act, s) for s in range(1, m)], acts)

    gx2n_pre, g_gain_pf = norm_backward(x2_pre, gain_pf, dh2_pre)
    gx2n_act, g_gain_af = norm_backward(x2_act, gain_af, dh2_act)
    gx2_pre = gz_pre.astype(F32) + gx2n_pre
    gx2_act = gz_act.astype(F32) + gx2n_act
    gy = gather_mp(pack(gx2_pre.astype(BF), gx2_act.astype(BF)), 0)
    gy_pre, gy_act = rows_of(gy)

    g_out_pre = dot_left(mixed[:rows], gy_pre).astype(BF)
    g_out_act = dot_left(mixed[rows:], gy_act).astype(BF)
    gmix = jnp.concatenate(
        [dot_right(gy_pre, w_out_pre).astype(BF), dot_right(gy_act, w_out_act).astype(BF)], axis=0
    )
    gq, gk, gv = [], 0.0, 0.0
    for h in range(heads):
        cut = slice(h * HD, (h + 1) * HD)
        gm = gmix[:, cut]
        pe = probs[h].astype(F32)
        gp = dot_right(gm, values)
        ds = (pe * (gp - jnp.sum(pe * gp, axis=-1, keepdims=True))).astype(BF)
        gq.append((dot_plain(ds, keys) * scale).astype(BF))
        gk = gk + dot_left(ds, query[:, cut]) * scale
        gv = gv + dot_left(probs[h], gm)
    gkv = jnp.concatenate([gk, gv], axis=1).astype(BF)

    def share(s):
        return lax.dynamic_slice_in_dim(gkv, (col ^ s) * kvw, kvw, 1)

    gkv_sum = share(0).astype(F32)
    for s in range(1, m):
        gkv_sum = gkv_sum + reorder(swap_mp(share(s), s), s).astype(F32)
    gin = jnp.concatenate(gq + [gkv], axis=1)
    gh1_pre = dot_right(gin[:rows], w_in_pre).astype(BF)
    gh1_act = dot_right(gin[rows:], w_in_act).astype(BF)
    gh1 = reduce_mp(blocks_of(gh1_pre, gh1_act), 0)
    gh1_pre, gh1_act = unpack(gh1, rq, narrow)
    gin = jnp.concatenate(gq + [gkv_sum.astype(BF)], axis=1)
    g_in_pre = dot_left(h1_pre, gin[:rows]).astype(BF)
    g_in_act = dot_left(h1_act, gin[rows:]).astype(BF)

    gxn_pre, g_gain_pa = norm_backward(x_pre[:rq], gain_pa, gh1_pre)
    gxn_act, g_gain_aa = norm_backward(x_act[:aq], gain_aa, gh1_act)
    grad_pre = (gx2_pre + gxn_pre).astype(BF)
    prefix_grad = natural(
        [grad_pre] + [swap_mp(grad_pre, s) for s in range(1, m)], length
    ).astype(F32)
    gxa = (gx2_act + gxn_act).astype(BF)
    g_embed = dot_left(act_in[:aq], gxa)
    act_grad = dot_right(gxa, embed)
    act_grad = natural([act_grad] + [swap_mp(act_grad, s) for s in range(1, m)], acts)

    def by_index(vector):
        return vector.reshape(n, -1, narrow // n).transpose(1, 0, 2).reshape(-1, narrow)

    tiny = jnp.concatenate(
        [
            by_index(g_gain_pa),
            by_index(g_gain_pf),
            by_index(g_gain_aa),
            by_index(g_gain_af),
            g_embed,
        ],
        axis=0,
    )
    tiny_rows = tiny.shape[0]
    tiny = columns_first(pad_rows(tiny, round_up(tiny_rows, 8)))
    tiny_sum = tiny
    for s in range(1, m):
        tiny_sum = tiny_sum + swap_mp(tiny, s)
    act_grad, out_act, tiny = return_all(
        [jnp.pad(act_grad, ((0, 0), (0, lanes - dims_count))), out_act, tiny_sum], (3, 3, 4), 4
    )
    mine_items = (slot_item[:, None] == lax.broadcasted_iota(jnp.int32, (1, n), 1)).astype(BF)
    action_output = dot_plain(mine_items, out_act[:, :steps].reshape(n, steps * narrow))
    action_output = action_output.astype(BF).reshape(slot_count, steps, narrow)
    own_mask = lax.broadcasted_iota(jnp.int32, (slot_count, dims_count), 1) < valid_dims[:, None]
    action_grad = jnp.sum(
        mine_items.astype(F32)[:, :, None, None] * act_grad[None, :, :steps, :dims_count], axis=1
    ) * own_mask.astype(F32)[:, None, :]
    tiny = jnp.sum(tiny, axis=0)
    grad_gain_pa = tiny[:twice].reshape(-1)
    grad_gain_pf = tiny[twice : 2 * twice].reshape(-1)
    rest = tiny[2 * twice : tiny_rows]

    def attn_block(item):
        left = lax.slice_in_dim(g_in_pre, item * d_pre, (item + 1) * d_pre, axis=0)
        out = lax.slice_in_dim(g_out_pre, item * d_pre, (item + 1) * d_pre, axis=1)
        left_a = lax.slice_in_dim(g_in_act, item * d_act, (item + 1) * d_act, axis=0)
        out_a = lax.slice_in_dim(g_out_act, item * d_act, (item + 1) * d_act, axis=1)
        top = jnp.concatenate([left] + jnp.split(out, out.shape[0] // d_pre, axis=0), axis=1)
        low = jnp.concatenate([left_a] + jnp.split(out_a, out_a.shape[0] // d_act, axis=0), axis=1)
        return jnp.concatenate([top, low], axis=0)

    act_back = jnp.concatenate(
        [
            g_gate_a.reshape(n, d_act, m * few),
            g_up_a.reshape(n, d_act, m * few),
            g_down_a.T.reshape(n, d_act, m * few),
        ],
        axis=1,
    )
    act_back = reduce_mp(act_back, 2).astype(BF)
    parts = pair_sum(jnp.stack([attn_block(i) for i in range(n)]))
    returned = return_all(
        [
            reduce_mp(g_down_p, 0).astype(BF),
            reduce_mp(g_gate_p, 1).astype(BF),
            reduce_mp(g_up_p, 1).astype(BF),
            act_back,
            parts,
        ],
        (1, 0, 0, 4, 2),
        3,
    )
    grad_down, grad_gate, grad_up, act_back = [g.astype(F32) for g in returned[:4]]
    grad_gate_a = act_back[:, :d_act].transpose(1, 0, 2).reshape(d_act, n * few)
    grad_up_a = act_back[:, d_act : 2 * d_act].transpose(1, 0, 2).reshape(d_act, n * few)
    grad_down_a = act_back[:, 2 * d_act :].transpose(0, 2, 1).reshape(n * few, d_act)
    total = jnp.sum(returned[4].astype(F32), axis=0)
    grad_query, grad_kv = total[:d_pre, :split], total[:d_pre, split : split + kvw]
    grad_out = jnp.concatenate(
        jnp.split(total[:d_pre, split + kvw :], split // d_pre, axis=1), axis=0
    )
    grad_query_a, grad_kv_a = total[d_pre:, :split], total[d_pre:, split : split + kvw]
    grad_out_a = jnp.concatenate(
        jnp.split(total[d_pre:, split + kvw :], split // d_act, axis=1), axis=0
    )
    both = jnp.concatenate([grad_kv, grad_kv_a], axis=0).astype(BF)
    both = [both] + [swap_mp(both, s) for s in range(1, m)]
    both = jnp.concatenate([pick_mp(both, place) for place in range(m)], axis=1).astype(F32)

    return (
        prefix_output,
        action_output,
        prefix_grad,
        action_grad,
        grad_gain_pa,
        grad_query,
        both[:d_pre, :HD],
        both[:d_pre, HD:],
        grad_out,
        grad_gain_pf,
        grad_gate,
        grad_up,
        grad_down,
        rest[2:],
        rest[0],
        grad_query_a,
        both[d_pre:, :HD],
        both[d_pre:, HD:],
        grad_out_a,
        rest[1],
        grad_gate_a,
        grad_up_a,
        grad_down_a,
    )


def solution(mesh):
    return jax.shard_map(
        local,
        mesh=mesh,
        in_specs=(
            P("dp", None),
            P("dp", None, None),
            P("dp"),
            P("dp"),
            P("dp", None),
            P("dp"),
            P("dp", "mp"),
            P("dp", None),
            P("dp", None),
            P("mp", "dp"),
            P("dp"),
            P("dp", "mp"),
            P("dp", "mp"),
            P("mp", "dp"),
            P(None, "dp"),
            P("dp"),
            P("dp", "mp"),
            P("dp", None),
            P("dp", None),
            P("mp", "dp"),
            P("dp"),
            P("dp", "mp"),
            P("dp", "mp"),
            P("mp", "dp"),
            P("dp", None),
            P("dp", None, None),
        ),
        out_specs=(
            P("dp", None),
            P("dp", None, None),
            P("dp", None),
            P("dp", None, None),
            P("dp"),
            P("dp", "mp"),
            P("dp", None),
            P("dp", None),
            P("mp", "dp"),
            P("dp"),
            P("dp", "mp"),
            P("dp", "mp"),
            P("mp", "dp"),
            P(None, "dp"),
            P("dp"),
            P("dp", "mp"),
            P("dp", None),
            P("dp", None),
            P("mp", "dp"),
            P("dp"),
            P("dp", "mp"),
            P("dp", "mp"),
            P("mp", "dp"),
        ),
        check_vma=False,
    )
```

time: 2520 us -> 1620 us (0.64)
  waiting for transfers between devices: 1770 us -> 320 us
  Pallas kernels: 0 us -> 717 us
  blocking collectives: 237 us -> 0 us
  matrix products: 345 us -> 242 us
  local copies, waits for them, and re-layouts: 52.9 us -> 140 us
  starting transfers between devices: 2.19 us -> 55.2 us
    pallas_call x0 -> x4, Pallas kernels: none -> 717 us  [the longest x1 317 us: deal_all(): pl.pallas_call(functools.partial(deal_kernel, n, m, kinds, len(arrays)),...]
    reduce_scatter x13 -> x0, waiting for transfers between devices: 712 us -> none  [the longest x1 167 us: local(): lax.psum_scatter(g_gate_pre.astype(jnp.bfloat16), 'dp', scatter_dimension...]
    all_gather x13 -> x0, waiting for transfers between devices: 588 us -> none  [the longest x1 142 us: local(): lax.all_gather(pre_gate, 'dp', axis=0, tiled=True)]
    psum x4 -> x0, waiting for transfers between devices: 431 us -> none  [the longest x1 127 us: local(): gh2_pre, gh2_act = lax.psum((gh2_pre, gh2_act), 'mp')]
    ppermute x0 -> x51, waiting for transfers between devices: none -> 320 us  [the longest x42 257 us: swap_mp(): return lax.ppermute(block, 'mp', [(i, i ^ step) for i in range(size)])]
    psum x1 -> x0, blocking collectives: 121 us -> none  [local(): lax.psum((dot_right(gqb_pre, b_query), gkv_pre_part, dot_right(gqb_act, c...]
    all_gather x7 -> x0, blocking collectives: 88.6 us -> none  [the longest x1 16.9 us: local(): lax.all_gather(act_key, 'dp', axis=0, tiled=True)]
    dot_general x27 -> x17, matrix products: 138 us -> 72.3 us  [dot_plain(): return jnp.dot(left, right, preferred_element_type=F32)]
  transfers between devices with their start and end apart: 33 -> 51, of which waited for: 28 -> 17; matrix products, arithmetic and copies ran while one was open for 15% -> 14% of each run, Pallas kernels for 0% -> 5%
where the time goes in v1:
time: 1620 us; the launch traced here: 1590 us
  Pallas kernels  717 us (44%)
  waiting for transfers between devices  320 us (20%)
  matrix products  242 us (15%)
  local copies, waits for them, and re-layouts  140 us (9%)
  other arithmetic  116 us (7%)
  starting transfers between devices  55.2 us (3%)
    pallas_call x1, Pallas kernels, deal_all(): pl.pallas_call(functools.partial(deal_kernel, n, m, kinds, len(arrays)),...  317 us
    pallas_call x2, Pallas kernels, return_all(): pl.pallas_call(functools.partial(return_kernel, n, kinds), out_shape=[jax...  288 us
    ppermute x42, waiting for transfers between devices, swap_mp(): return lax.ppermute(block, 'mp', [(i, i ^ step) for i in range(size)])  257 us
    pallas_call x1, Pallas kernels, gather_all(): pl.pallas_call(functools.partial(gather_kernel, n, m, count, places, shar...  112 us
    dot_general x15, matrix products, dot_right(): lax.dot_general(left, right, (((1,), (1,)), ((), ())), preferred_element_...  95.4 us
    dot_general x15, matrix products, dot_left(): lax.dot_general(left, right, (((0,), (0,)), ((), ())), preferred_element_...  73.9 us
    dot_general x17, matrix products, dot_plain(): return jnp.dot(left, right, preferred_element_type=F32)  72.3 us
    ppermute x6, waiting for transfers between devices, send_dp(): lax.ppermute(block, 'dp', [(i, (i + step) % size) for i in range(size)])  62.8 us
  transfers between devices with their start and end apart: 51, of which 17 were waited for; matrix products, arithmetic and copies ran while one was open for 14% of the time, Pallas kernels for 5%

profile of v1, /device:TPU:0, one launch (start us, length us, event | category | flops | bytes accessed | tf_op | source)
XLA Modules:
  0.0 1594.3 jit_solution(2492428481850173181)
XLA Ops:
  10.2 112.2 %gather_all.1 = (bf16[1024,128]{1,0:T(8,128)(2,1)}, s32[64,128]{1,0:T(8,128)}, bf16[2048,512]{1,0:T(8,128)(2,1)}, bf16[1024,512]{1,0:T(8,128)(2,1)}, bf16[4,2048...) custom-call(bf16[128,128]{1,0:T(8,128)(2,1)} %copy-done.123, ...), custom_call_target="tpu_custom_call" | custom-call | tf_op jit(solution)/shard_map/gather_all/pallas_call | solution.py:263
  179.1 19.7 %collective-permute-done.1 = bf16[224,2048]{1,0:T(8,128)(2,1)} collective-permute-done((bf16[224,2048]{1,0:T(8,128)(2,1)}, bf16[224,2048]{1,0:T(8,128)(2,1)}, u32[]{:S(2)}, u32[]{:S(2)}) %collective-permute-start.1) | collective-permute-done | bytes 917536 | tf_op jit(solution)/shard_map/ppermute | solution.py:47
  207.7 316.9 %deal_all.1 = (bf16[2048,2048]{1,0:T(8,128)(2,1)}, bf16[2048,2048]{1,0:T(8,128)(2,1)}, bf16[2048,2048]{1,0:T(8,128)(2,1)}, bf16[4,8,384,128]{3,2,1,0:T(8,128)(2,...) custom-call(bf16[256,4096]{1,0:T(8,128)(2,1)} %refs_0_.1, bf16[256,4096]{1,0:T(8,128)(2,1)} %refs_1_.1, ...), custom_call_target="tpu_custom_call" | custom-call | tf_op jit(solution)/shard_map/deal_all/pallas_call | solution.py:468
  554.7 17.8 %fusion.268 = f32[1664,2048]{1,0:T(8,128)} fusion(bf16[1664,2048]{1,0:T(8,128)(2,1)S(1)} %slice_dynamic-update-slice_fusion, bf16[2048,2048]{1,0:T(8,128)(2,1)S(1)} %bitcast.476), kind=kOutput, calls=%fused_computation.593 | convolution fusion | flops 13958643712 | bytes 28835840 | tf_op jit(solution)/shard_map/dot_general | solution.py:30
  572.5 17.9 %fusion.267 = f32[1664,2048]{1,0:T(8,128)} fusion(bf16[1664,2048]{1,0:T(8,128)(2,1)S(1)} %slice_dynamic-update-slice_fusion, bf16[2048,2048]{1,0:T(8,128)(2,1)S(1)} %bitcast.478), kind=kOutput, calls=%fused_computation.592 | convolution fusion | flops 13958643712 | bytes 28835840 | tf_op jit(solution)/shard_map/dot_general | solution.py:30
  590.4 37.1 %fusion.19 = (bf16[1664,2048]{1,0:T(8,128)(2,1)}, bf16[1664,2048]{1,0:T(8,128)(2,1)}, bf16[1664,2048]{1,0:T(8,128)(2,1)}) fusion(f32[1664,2048]{1,0:T(8,128)} %fusion.267, f32[1664,2048]{1,0:T(8,128)} %fusion.268, bf16[1664,2048]{1,0:T(8,128)(2,1)} %get-tuple-element.60, bf16[2048,2048]{1,0:T(8,128)(2,1)} %get-tuple-element.57), kind=kOutput, calls=%fused_computation.27 | convolution fusion | flops 14088142848 | bytes 62914560 | tf_op jit(solution)/shard_map/dot_general | solution.py:38
  627.5 18.9 %convolution_convert_fusion.2 = bf16[1664,2048]{1,0:T(8,128)(2,1)S(1)} fusion(bf16[1664,2048]{1,0:T(8,128)(2,1)} %get-tuple-element.154, bf16[2048,2048]{1,0:T(8,128)(2,1)} %get-tuple-element.57), kind=kOutput, calls=%fused_computation.29 | convolution fusion | flops 13962051584 | bytes 22020096 | tf_op jit(solution)/shard_map/dot_general | solution.py:30
  646.3 21.2 %convolution_convert_fusion.5 = bf16[2048,2048]{1,0:T(8,128)(2,1)} fusion(bf16[1664,2048]{1,0:T(8,128)(2,1)} %get-tuple-element.154, bf16[1664,2048]{1,0:T(8,128)(2,1)} %get-tuple-element.60), kind=kOutput, calls=%fused_computation.32 | convolution fusion | flops 13962838016 | bytes 22020096 | tf_op jit(solution)/shard_map/dot_general | solution.py:34
  667.5 18.2 %fusion.269 = f32[1664,2048]{1,0:T(8,128)} fusion(bf16[1664,2048]{1,0:T(8,128)(2,1)} %get-tuple-element.153, bf16[2048,2048]{1,0:T(8,128)(2,1)S(1)} %bitcast.478), kind=kOutput, calls=%fused_computation.594 | convolution fusion | flops 13958643712 | bytes 28835840 | tf_op jit(solution)/shard_map/dot_general | solution.py:38
  685.8 19.3 %convolution_convert_fusion.4 = bf16[2048,2048]{1,0:T(8,128)(2,1)} fusion(bf16[1664,2048]{1,0:T(8,128)(2,1)S(1)} %bitcast.460, bf16[1664,2048]{1,0:T(8,128)(2,1)} %get-tuple-element.153), kind=kOutput, calls=%fused_computation.31 | convolution fusion | flops 13962838016 | bytes 22020096 | tf_op jit(solution)/shard_map/dot_general | solution.py:34
  715.2 17.6 %convolution_convert_fusion.3 = bf16[2048,2048]{1,0:T(8,128)(2,1)} fusion(bf16[1664,2048]{1,0:T(8,128)(2,1)S(1)} %bitcast.460, bf16[1664,2048]{1,0:T(8,128)(2,1)S(1)} %bitcast.480), kind=kOutput, calls=%fused_computation.30 | convolution fusion | flops 13962838016 | bytes 22020096 | tf_op jit(solution)/shard_map/dot_general | solution.py:34
  732.8 22.8 %add_convert_fusion = bf16[1664,2048]{1,0:T(8,128)(2,1)} fusion(f32[1664,2048]{1,0:T(8,128)} %fusion.269, bf16[1664,2048]{1,0:T(8,128)(2,1)} %get-tuple-element.152, bf16[2048,2048]{1,0:T(8,128)(2,1)} %get-tuple-element.56), kind=kOutput, calls=%fused_computation.28 | convolution fusion | flops 13965459456 | bytes 35651584 | tf_op jit(solution)/shard_map/dot_general | solution.py:38
  759.8 5.7 fusion.243
  777.8 5.6 fusion.242
  783.4 5.7 fusion.244
  792.1 22.8 %collective-permute-done.35 = bf16[2048,512]{1,0:T(8,128)(2,1)} collective-permute-done((bf16[2048,512]{1,0:T(8,128)(2,1)}, bf16[2048,512]{1,0:T(8,128)(2,1)}, u32[]{:S(2)}, u32[]{:S(2)}) %collective-permute-start.35) | collective-permute-done | bytes 2097184 | tf_op jit(solution)/shard_map/ppermute | solution.py:47
  816.9 44.4 %collective-permute-done.37 = bf16[2048,512]{1,0:T(8,128)(2,1)} collective-permute-done((bf16[2048,512]{1,0:T(8,128)(2,1)}, bf16[2048,512]{1,0:T(8,128)(2,1)}, u32[]{:S(2)}, u32[]{:S(2)}) %collective-permute-start.37) | collective-permute-done | bytes 2097184 | tf_op jit(solution)/shard_map/ppermute | solution.py:47
  866.7 5.9 add_convert_fusion.2.refs_1_
  882.8 21.9 %collective-permute-done.38 = bf16[2048,512]{1,0:T(8,128)(2,1)S(1)} collective-permute-done((bf16[2048,512]{1,0:T(8,128)(2,1)}, bf16[2048,512]{1,0:T(8,128)(2,1)S(1)}, u32[]{:S(2)}, u32[]{:S(2)}) %collective-permute-start.38) | collective-permute-done | bytes 2097184 | tf_op jit(solution)/shard_map/ppermute | solution.py:47
  904.9 44.8 %collective-permute-done.40 = bf16[2048,512]{1,0:T(8,128)(2,1)S(1)} collective-permute-done((bf16[2048,512]{1,0:T(8,128)(2,1)}, bf16[2048,512]{1,0:T(8,128)(2,1)S(1)}, u32[]{:S(2)}, u32[]{:S(2)}) %collective-permute-start.40) | collective-permute-done | bytes 2097184 | tf_op jit(solution)/shard_map/ppermute | solution.py:47
  949.7 7.7 collective-permute-done.39
  967.5 7.4 collective-permute-done.4
  976.0 16.2 %collective-permute-done.6 = bf16[224,2048]{1,0:T(8,128)(2,1)S(1)} collective-permute-done((bf16[224,2048]{1,0:T(8,128)(2,1)S(1)}, bf16[224,2048]{1,0:T(8,128)(2,1)S(1)}, u32[]{:S(2)}, u32[]{:S(2)}) %collective-permute-start.6) | collective-permute-done | bytes 917536 | tf_op jit(solution)/shard_map/ppermute | solution.py:57
  992.2 39.2 %collective-permute-done.5 = bf16[224,2048]{1,0:T(8,128)(2,1)S(1)} collective-permute-done((bf16[224,2048]{1,0:T(8,128)(2,1)S(1)}, bf16[224,2048]{1,0:T(8,128)(2,1)S(1)}, u32[]{:S(2)}, u32[]{:S(2)}) %collective-permute-start.5) | collective-permute-done | bytes 917536 | tf_op jit(solution)/shard_map/ppermute | solution.py:57
  1040.7 13.6 collective-permute-done.34
  1055.7 31.0 %collective-permute-done.33 = bf16[512,2048]{1,0:T(8,128)(2,1)S(1)} collective-permute-done((bf16[512,2048]{1,0:T(8,128)(2,1)S(1)}, bf16[512,2048]{1,0:T(8,128)(2,1)S(1)}, u32[]{:S(2)}, u32[]{:S(2)}) %collective-permute-start.33) | collective-permute-done | bytes 2097184 | tf_op jit(solution)/shard_map/ppermute | solution.py:47
  1094.3 9.1 collective-permute-done.15
  1168.4 10.4 copy.102
  1182.9 5.7 copy.118
  1223.0 73.8 %return_all.2 = (f32[8,64,128]{2,1,0:T(8,128)}, bf16[8,64,1024]{2,1,0:T(8,128)(2,1)}, f32[8,40,128]{2,1,0:T(8,128)}) custom-call(f32[64,128]{1,0:T(8,128)} %select_maximum_fusion.refs_0_, bf16[64,1024]{1,0:T(8,128)(2,1)} %pad_maximum_fusion.19.refs_1_, f32[8,40,128]{2,1,0:T(8,128)} %add_add_fusion.2.refs_2_), custom_call_target="tpu_custom_call" | custom-call | tf_op jit(solution)/shard_map/return_all/pallas_call | solution.py:540
  1310.0 32.5 %collective-permute-done.30 = bf16[208,2048]{1,0:T(8,128)(2,1)S(1)} collective-permute-done((bf16[208,2048]{1,0:T(8,128)(2,1)S(1)}, bf16[208,2048]{1,0:T(8,128)(2,1)S(1)}, u32[]{:S(2)}, u32[]{:S(2)}) %collective-permute-start.30) | collective-permute-done | bytes 852000 | tf_op jit(solution)/shard_map/ppermute | solution.py:47
  1352.5 214.5 %return_all.3 = (bf16[4096,256]{1,0:T(8,128)(2,1)}, bf16[256,4096]{1,0:T(8,128)(2,1)}, bf16[256,4096]{1,0:T(8,128)(2,1)}, bf16[8,384,128]{2,1,0:T(8,128)(2,1)}, bf16[4,384,1152]{2,1,0:T(8,128)(2,1)}) custom-call(bf16[512,2048]{1,0:T(8,128)(2,1)} %add_convert_fusion.3.refs_0_, bf16[2048,512]{1,0:T(8,128)(2,1)} %add_convert_fusion.2.refs_1_, ...), custom_call_target="tpu_custom_call" | custom-call | tf_op jit(solution)/shard_map/return_all/pallas_call | solution.py:540
  (741 shorter events, 332.8 us)
Async XLA Ops:
  157.1 41.7 %collective-permute-start.1 = (bf16[224,2048]{1,0:T(8,128)(2,1)}, bf16[224,2048]{1,0:T(8,128)(2,1)}, u32[]{:S(2)}, u32[]{:S(2)}) collective-permute-start(bf16[224,2048]{1,0:T(8,128)(2,1)} %fusion.94), channel_id=1, source_target_pairs={{0,2},{1,3},{2,0},{3,1},{4,6},{5,7},{6,4},{7,5},{8,10},{9,11},{10,... | collective-permute-start | bytes 2752520 | tf_op jit(solution)/shard_map/ppermute | solution.py:47
  158.6 40.2 %collective-permute-start.2 = (bf16[224,2048]{1,0:T(8,128)(2,1)}, bf16[224,2048]{1,0:T(8,128)(2,1)}, u32[]{:S(2)}, u32[]{:S(2)}) collective-permute-start(bf16[224,2048]{1,0:T(8,128)(2,1)} %fusion.95), channel_id=1, source_target_pairs={{0,3},{1,2},{2,1},{3,0},{4,7},{5,6},{6,5},{7,4},{8,11},{9,10},{10,... | collective-permute-start | bytes 2752520 | tf_op jit(solution)/shard_map/ppermute | solution.py:47
  708.8 63.6 %collective-permute-start.41 = (bf16[8,384,128]{2,1,0:T(8,128)(2,1)}, bf16[8,384,128]{2,1,0:T(8,128)(2,1)}, u32[]{:S(2)}, u32[]{:S(2)}) collective-permute-start(bf16[8,384,128]{2,1,0:T(8,128)(2,1)} %get-tuple-element.207), channel_id=1, source_target_pairs={{0,1},{1,0},{2,3},{3,2},{4,5},{5,4},{6,7},{7,6},{8,9},{9,8},{10,11... | collective-permute-start | bytes 2359304 | tf_op jit(solution)/shard_map/ppermute | solution.py:47
  709.3 64.5 %collective-permute-start.43 = (bf16[8,384,128]{2,1,0:T(8,128)(2,1)}, bf16[8,384,128]{2,1,0:T(8,128)(2,1)}, u32[]{:S(2)}, u32[]{:S(2)}) collective-permute-start(bf16[8,384,128]{2,1,0:T(8,128)(2,1)} %get-tuple-element.208), channel_id=1, source_target_pairs={{0,3},{1,2},{2,1},{3,0},{4,7},{5,6},{6,5},{7,4},{8,11},{9,10},{10,... | collective-permute-start | bytes 2359304 | tf_op jit(solution)/shard_map/ppermute | solution.py:47
  710.8 65.9 %collective-permute-start.42 = (bf16[8,384,128]{2,1,0:T(8,128)(2,1)}, bf16[8,384,128]{2,1,0:T(8,128)(2,1)}, u32[]{:S(2)}, u32[]{:S(2)}) collective-permute-start(bf16[8,384,128]{2,1,0:T(8,128)(2,1)} %get-tuple-element.209), channel_id=1, source_target_pairs={{0,2},{1,3},{2,0},{3,1},{4,6},{5,7},{6,4},{7,5},{8,10},{9,11},{10,... | collective-permute-start | bytes 2359304 | tf_op jit(solution)/shard_map/ppermute | solution.py:47
  765.5 49.3 %collective-permute-start.35 = (bf16[2048,512]{1,0:T(8,128)(2,1)}, bf16[2048,512]{1,0:T(8,128)(2,1)}, u32[]{:S(2)}, u32[]{:S(2)}) collective-permute-start(bf16[2048,512]{1,0:T(8,128)(2,1)} %get-tuple-element.158), channel_id=1, source_target_pairs={{0,1},{1,0},{2,3},{3,2},{4,5},{5,4},{6,7},{7,6},{8,9},{9,8},{10,11... | collective-permute-start | bytes 6291464 | tf_op jit(solution)/shard_map/ppermute | solution.py:47
  769.4 103.2 %collective-permute-start.10 = (bf16[4,224,2048]{2,1,0:T(8,128)(2,1)S(1)}, bf16[4,224,2048]{2,1,0:T(8,128)(2,1)S(1)}, u32[]{:S(2)}, u32[]{:S(2)}) collective-permute-start(bf16[4,224,2048]{2,1,0:T(8,128)(2,1)S(1)} %dynamic-slice_bitcast_fusion), channel_id=1, source_target_pairs={{0,4},{4,0},{8,12},{12,8},{16,20},{20,16},{24,28},{28,24},{1,5},{5... | collective-permute-start | bytes 11010056 | tf_op jit(solution)/shard_map/ppermute | solution.py:52
  772.3 88.9 %collective-permute-start.37 = (bf16[2048,512]{1,0:T(8,128)(2,1)}, bf16[2048,512]{1,0:T(8,128)(2,1)}, u32[]{:S(2)}, u32[]{:S(2)}) collective-permute-start(bf16[2048,512]{1,0:T(8,128)(2,1)} %get-tuple-element.159), channel_id=1, source_target_pairs={{0,3},{1,2},{2,1},{3,0},{4,7},{5,6},{6,5},{7,4},{8,11},{9,10},{10,... | collective-permute-start | bytes 6291464 | tf_op jit(solution)/shard_map/ppermute | solution.py:47
  773.8 92.3 %collective-permute-start.36 = (bf16[2048,512]{1,0:T(8,128)(2,1)}, bf16[2048,512]{1,0:T(8,128)(2,1)}, u32[]{:S(2)}, u32[]{:S(2)}) collective-permute-start(bf16[2048,512]{1,0:T(8,128)(2,1)} %get-tuple-element.160), channel_id=1, source_target_pairs={{0,2},{1,3},{2,0},{3,1},{4,6},{5,7},{6,4},{7,5},{8,10},{9,11},{10,... | collective-permute-start | bytes 6291464 | tf_op jit(solution)/shard_map/ppermute | solution.py:47
  776.7 98.3 %collective-permute-start.3 = (bf16[4,224,2048]{2,1,0:T(8,128)(2,1)}, bf16[4,224,2048]{2,1,0:T(8,128)(2,1)}, u32[]{:S(2)}, u32[]{:S(2)}) collective-permute-start(bf16[4,224,2048]{2,1,0:T(8,128)(2,1)} %dynamic-slice_bitcast_fusion.1), channel_id=1, source_target_pairs={{0,4},{4,0},{8,12},{12,8},{16,20},{20,16},{24,28},{28,24},{1,5},{5... | collective-permute-start | bytes 11010056 | tf_op jit(solution)/shard_map/ppermute | solution.py:52
  814.8 89.8 %collective-permute-start.38 = (bf16[2048,512]{1,0:T(8,128)(2,1)}, bf16[2048,512]{1,0:T(8,128)(2,1)S(1)}, u32[]{:S(2)}, u32[]{:S(2)}) collective-permute-start(bf16[2048,512]{1,0:T(8,128)(2,1)} %get-tuple-element.155), channel_id=1, source_target_pairs={{0,1},{1,0},{2,3},{3,2},{4,5},{5,4},{6,7},{7,6},{8,9},{9,8},{10,11... | collective-permute-start | bytes 6291464 | tf_op jit(solution)/shard_map/ppermute | solution.py:47
  861.3 88.5 %collective-permute-start.40 = (bf16[2048,512]{1,0:T(8,128)(2,1)}, bf16[2048,512]{1,0:T(8,128)(2,1)S(1)}, u32[]{:S(2)}, u32[]{:S(2)}) collective-permute-start(bf16[2048,512]{1,0:T(8,128)(2,1)} %get-tuple-element.156), channel_id=1, source_target_pairs={{0,3},{1,2},{2,1},{3,0},{4,7},{5,6},{6,5},{7,4},{8,11},{9,10},{10,... | collective-permute-start | bytes 6291464 | tf_op jit(solution)/shard_map/ppermute | solution.py:47
  866.1 91.3 %collective-permute-start.39 = (bf16[2048,512]{1,0:T(8,128)(2,1)}, bf16[2048,512]{1,0:T(8,128)(2,1)}, u32[]{:S(2)}, u32[]{:S(2)}) collective-permute-start(bf16[2048,512]{1,0:T(8,128)(2,1)} %get-tuple-element.157), channel_id=1, source_target_pairs={{0,2},{1,3},{2,0},{3,1},{4,6},{5,7},{6,4},{7,5},{8,10},{9,11},{10,... | collective-permute-start | bytes 6291464 | tf_op jit(solution)/shard_map/ppermute | solution.py:47
  874.9 82.9 %collective-permute-start.11 = (bf16[224,2048]{1,0:T(8,128)(2,1)S(1)}, bf16[224,2048]{1,0:T(8,128)(2,1)S(1)}, u32[]{:S(2)}, u32[]{:S(2)}) collective-permute-start(bf16[224,2048]{1,0:T(8,128)(2,1)S(1)} %get-tuple-element.181), channel_id=1, source_target_pairs={{0,8},{4,12},{8,16},{12,20},{16,24},{20,28},{24,0},{28,4},{1,9},{5... | collective-permute-start | bytes 2752520 | tf_op jit(solution)/shard_map/ppermute | solution.py:57
  875.0 87.8 %collective-permute-start.13 = (bf16[224,2048]{1,0:T(8,128)(2,1)S(1)}, bf16[224,2048]{1,0:T(8,128)(2,1)}, u32[]{:S(2)}, u32[]{:S(2)}) collective-permute-start(bf16[224,2048]{1,0:T(8,128)(2,1)S(1)} %get-tuple-element.182), channel_id=1, source_target_pairs={{0,24},{4,28},{8,0},{12,4},{16,8},{20,12},{24,16},{28,20},{1,25},{... | collective-permute-start | bytes 2752520 | tf_op jit(solution)/shard_map/ppermute | solution.py:57
  904.7 58.8 %collective-permute-start.12 = (bf16[224,2048]{1,0:T(8,128)(2,1)S(1)}, bf16[224,2048]{1,0:T(8,128)(2,1)S(1)}, u32[]{:S(2)}, u32[]{:S(2)}) collective-permute-start(bf16[224,2048]{1,0:T(8,128)(2,1)S(1)} %get-tuple-element.183), channel_id=1, source_target_pairs={{0,16},{4,20},{8,24},{12,28},{16,0},{20,4},{24,8},{28,12},{1,17},{... | collective-permute-start | bytes 2752520 | tf_op jit(solution)/shard_map/ppermute | solution.py:57
  957.9 73.5 %collective-permute-start.5 = (bf16[224,2048]{1,0:T(8,128)(2,1)S(1)}, bf16[224,2048]{1,0:T(8,128)(2,1)S(1)}, u32[]{:S(2)}, u32[]{:S(2)}) collective-permute-start(bf16[224,2048]{1,0:T(8,128)(2,1)S(1)} %get-tuple-element.186), channel_id=1, source_target_pairs={{0,16},{4,20},{8,24},{12,28},{16,0},{20,4},{24,8},{28,12},{1,17},{... | collective-permute-start | bytes 2752520 | tf_op jit(solution)/shard_map/ppermute | solution.py:57
  962.8 76.4 %collective-permute-start.32 = (bf16[512,2048]{1,0:T(8,128)(2,1)S(1)}, bf16[512,2048]{1,0:T(8,128)(2,1)S(1)}, u32[]{:S(2)}, u32[]{:S(2)}) collective-permute-start(bf16[512,2048]{1,0:T(8,128)(2,1)S(1)} %copy-done.51), channel_id=1, source_target_pairs={{0,1},{1,0},{2,3},{3,2},{4,5},{5,4},{6,7},{7,6},{8,9},{9,8},{10,11... | collective-permute-start | bytes 6291464 | tf_op jit(solution)/shard_map/ppermute | solution.py:47
  963.5 90.8 %collective-permute-start.34 = (bf16[512,2048]{1,0:T(8,128)(2,1)S(1)}, bf16[512,2048]{1,0:T(8,128)(2,1)S(1)}, u32[]{:S(2)}, u32[]{:S(2)}) collective-permute-start(bf16[512,2048]{1,0:T(8,128)(2,1)S(1)} %copy-done.50), channel_id=1, source_target_pairs={{0,3},{1,2},{2,1},{3,0},{4,7},{5,6},{6,5},{7,4},{8,11},{9,10},{10,... | collective-permute-start | bytes 6291464 | tf_op jit(solution)/shard_map/ppermute | solution.py:47
  974.9 111.8 %collective-permute-start.33 = (bf16[512,2048]{1,0:T(8,128)(2,1)S(1)}, bf16[512,2048]{1,0:T(8,128)(2,1)S(1)}, u32[]{:S(2)}, u32[]{:S(2)}) collective-permute-start(bf16[512,2048]{1,0:T(8,128)(2,1)S(1)} %copy-done.49), channel_id=1, source_target_pairs={{0,2},{1,3},{2,0},{3,1},{4,6},{5,7},{6,4},{7,5},{8,10},{9,11},{10,... | collective-permute-start | bytes 6291464 | tf_op jit(solution)/shard_map/ppermute | solution.py:47
  1034.1 53.7 %collective-permute-start.25 = (bf16[16,1024]{1,0:T(8,128)(2,1)S(1)}, bf16[16,1024]{1,0:T(8,128)(2,1)S(1)}, u32[]{:S(2)}, u32[]{:S(2)}) collective-permute-start(bf16[16,1024]{1,0:T(8,128)(2,1)S(1)} %get-tuple-element.360), channel_id=1, source_target_pairs={{0,1},{1,0},{2,3},{3,2},{4,5},{5,4},{6,7},{7,6},{8,9},{9,8},{10,11... | collective-permute-start | bytes 98312 | tf_op jit(solution)/shard_map/ppermute | solution.py:47
  1035.1 58.4 %collective-permute-start.24 = (bf16[16,1024]{1,0:T(8,128)(2,1)S(1)}, bf16[16,1024]{1,0:T(8,128)(2,1)S(1)}, u32[]{:S(2)}, u32[]{:S(2)}) collective-permute-start(bf16[16,1024]{1,0:T(8,128)(2,1)S(1)} %get-tuple-element.360), channel_id=1, source_target_pairs={{0,2},{1,3},{2,0},{3,1},{4,6},{5,7},{6,4},{7,5},{8,10},{9,11},{10,... | collective-permute-start | bytes 98312 | tf_op jit(solution)/shard_map/ppermute | solution.py:47
  1039.2 54.3 %collective-permute-start.23 = (bf16[16,1024]{1,0:T(8,128)(2,1)S(1)}, bf16[16,1024]{1,0:T(8,128)(2,1)S(1)}, u32[]{:S(2)}, u32[]{:S(2)}) collective-permute-start(bf16[16,1024]{1,0:T(8,128)(2,1)S(1)} %get-tuple-element.360), channel_id=1, source_target_pairs={{0,3},{1,2},{2,1},{3,0},{4,7},{5,6},{6,5},{7,4},{8,11},{9,10},{10,... | collective-permute-start | bytes 98312 | tf_op jit(solution)/shard_map/ppermute | solution.py:47
  1054.3 39.9 %collective-permute-start.16 = (bf16[224,2048]{1,0:T(8,128)(2,1)S(1)}, bf16[224,2048]{1,0:T(8,128)(2,1)S(1)}, u32[]{:S(2)}, u32[]{:S(2)}) collective-permute-start(bf16[224,2048]{1,0:T(8,128)(2,1)S(1)} %fusion.121), channel_id=1, source_target_pairs={{0,3},{1,2},{2,1},{3,0},{4,7},{5,6},{6,5},{7,4},{8,11},{9,10},{10,... | collective-permute-start | bytes 2752520 | tf_op jit(solution)/shard_map/ppermute | solution.py:47
  1136.1 56.9 %collective-permute-start.17 = (bf16[224,2048]{1,0:T(8,128)(2,1)}, bf16[224,2048]{1,0:T(8,128)(2,1)}, u32[]{:S(2)}, u32[]{:S(2)}) collective-permute-start(bf16[224,2048]{1,0:T(8,128)(2,1)} %fusion.147), channel_id=1, source_target_pairs={{0,1},{1,0},{2,3},{3,2},{4,5},{5,4},{6,7},{7,6},{8,9},{9,8},{10,11... | collective-permute-start | bytes 2752520 | tf_op jit(solution)/shard_map/ppermute | solution.py:47
  1138.2 54.9 %collective-permute-start.18 = (bf16[224,2048]{1,0:T(8,128)(2,1)}, bf16[224,2048]{1,0:T(8,128)(2,1)}, u32[]{:S(2)}, u32[]{:S(2)}) collective-permute-start(bf16[224,2048]{1,0:T(8,128)(2,1)} %fusion.148), channel_id=1, source_target_pairs={{0,2},{1,3},{2,0},{3,1},{4,6},{5,7},{6,4},{7,5},{8,10},{9,11},{10,... | collective-permute-start | bytes 2752520 | tf_op jit(solution)/shard_map/ppermute | solution.py:47
  1140.3 52.8 %collective-permute-start.19 = (bf16[224,2048]{1,0:T(8,128)(2,1)}, bf16[224,2048]{1,0:T(8,128)(2,1)}, u32[]{:S(2)}, u32[]{:S(2)}) collective-permute-start(bf16[224,2048]{1,0:T(8,128)(2,1)} %fusion.149), channel_id=1, source_target_pairs={{0,3},{1,2},{2,1},{3,0},{4,7},{5,6},{6,5},{7,4},{8,11},{9,10},{10,... | collective-permute-start | bytes 2752520 | tf_op jit(solution)/shard_map/ppermute | solution.py:47
  1193.0 154.6 %collective-permute-start.47 = (bf16[4,384,1152]{2,1,0:T(8,128)(2,1)}, bf16[4,384,1152]{2,1,0:T(8,128)(2,1)}, u32[]{:S(2)}, u32[]{:S(2)}) collective-permute-start(bf16[4,384,1152]{2,1,0:T(8,128)(2,1)} %dynamic-slice_bitcast_fusion.2), channel_id=1, source_target_pairs={{0,4},{4,0},{8,12},{12,8},{16,20},{20,16},{24,28},{28,24},{1,5},{5... | collective-permute-start | bytes 10616840 | tf_op jit(solution)/shard_map/ppermute | solution.py:52
  1212.7 90.6 %collective-permute-start.9 = (bf16[208,2048]{1,0:T(8,128)(2,1)}, bf16[208,2048]{1,0:T(8,128)(2,1)}, u32[]{:S(2)}, u32[]{:S(2)}) collective-permute-start(bf16[208,2048]{1,0:T(8,128)(2,1)} %get-tuple-element.247), channel_id=1, source_target_pairs={{0,1},{1,0},{2,3},{3,2},{4,5},{5,4},{6,7},{7,6},{8,9},{9,8},{10,11... | collective-permute-start | bytes 2555912 | tf_op jit(solution)/shard_map/ppermute | solution.py:47
  1218.3 86.3 %collective-permute-start.8 = (bf16[208,2048]{1,0:T(8,128)(2,1)}, bf16[208,2048]{1,0:T(8,128)(2,1)}, u32[]{:S(2)}, u32[]{:S(2)}) collective-permute-start(bf16[208,2048]{1,0:T(8,128)(2,1)} %get-tuple-element.247), channel_id=1, source_target_pairs={{0,2},{1,3},{2,0},{3,1},{4,6},{5,7},{6,4},{7,5},{8,10},{9,11},{10,... | collective-permute-start | bytes 2555912 | tf_op jit(solution)/shard_map/ppermute | solution.py:47
  1219.3 86.8 %collective-permute-start.7 = (bf16[208,2048]{1,0:T(8,128)(2,1)}, bf16[208,2048]{1,0:T(8,128)(2,1)}, u32[]{:S(2)}, u32[]{:S(2)}) collective-permute-start(bf16[208,2048]{1,0:T(8,128)(2,1)} %get-tuple-element.247), channel_id=1, source_target_pairs={{0,3},{1,2},{2,1},{3,0},{4,7},{5,6},{6,5},{7,4},{8,11},{9,10},{10,... | collective-permute-start | bytes 2555912 | tf_op jit(solution)/shard_map/ppermute | solution.py:47
  1221.3 88.8 %collective-permute-start.31 = (bf16[208,2048]{1,0:T(8,128)(2,1)}, bf16[208,2048]{1,0:T(8,128)(2,1)}, u32[]{:S(2)}, u32[]{:S(2)}) collective-permute-start(bf16[208,2048]{1,0:T(8,128)(2,1)} %get-tuple-element.246), channel_id=1, source_target_pairs={{0,1},{1,0},{2,3},{3,2},{4,5},{5,4},{6,7},{7,6},{8,9},{9,8},{10,11... | collective-permute-start | bytes 2555912 | tf_op jit(solution)/shard_map/ppermute | solution.py:47
  (195 other events, 2212.4 us)

commit v2 on v1

--- a/solution.py
+++ b/solution.py
@@ -58,23 +58,21 @@
 
 
 def pair_sum(parts):
-    size, me = lax.axis_size("dp"), lax.axis_index("dp")
-    parts = parts.reshape((size // 2, 2) + parts.shape[1:])
-    here = lax.rem(me, 2)
-    kept = lax.dynamic_index_in_dim(parts, here, 1, False)
-    got = swap_core(lax.dynamic_index_in_dim(parts, 1 - here, 1, False))
-    return (kept.astype(F32) + got.astype(F32)).astype(BF)
+    half = parts.shape[0] // 2
+    return add(parts[:half], swap_core(parts[half:]))
+
+
+def gather_dp(block):
+    half = lax.axis_size("dp") // 2
+    same = jnp.stack([block] + [send_dp(block, -2 * s) for s in range(1, half)])
+    return jnp.concatenate([same, swap_core(same)], axis=0)
 
 
 def reduce_dp(parts):
-    size, me = lax.axis_size("dp"), lax.axis_index("dp")
-    half = size // 2
     both = pair_sum(parts)
-    total = 0.0
-    for s in range(half):
-        chip = lax.rem(me // 2 + s, half)
-        block = lax.dynamic_index_in_dim(both, chip, 0, False)
-        total = total + (send_dp(block, 2 * s) if s else block).astype(F32)
+    total = both[0].astype(F32)
+    for s in range(1, both.shape[0]):
+        total = total + send_dp(both[s], 2 * s).astype(F32)
     return total
 
 
@@ -149,39 +147,41 @@
 
 
 class Line:
-    def __init__(self, own, place, sems, row):
+    def __init__(self, own, place, sems, row, pass_on=None):
         self.n = lax.axis_size("dp")
         self.me, self.col = lax.axis_index("dp"), lax.axis_index("mp")
         self.own, self.place, self.row = own, place, row
         self.sent, self.arrived, self.local = sems
         self.chips = self.n // 2
         self.chip = self.me // 2
+        self.pass_on = pass_on
 
     def copy(self, way, k):
         step = (2, -2)[way]
         origin = lax.rem(self.me - step * (k - 1) + 2 * self.n, self.n)
-        source = self.own if k == 1 else self.place(origin)
-        target = (lax.rem(self.me + step + self.n, self.n), self.col)
+        source = self.own if k == 1 else self.place(origin, self.me)
+        target = lax.rem(self.me + step + self.n, self.n)
         slot = way * self.chips + k
         return remote(
             source,
-            self.place(origin),
+            self.place(origin, target),
             self.sent.at[self.row, slot],
             self.arrived.at[self.row, slot],
-            target,
+            (target, self.col),
         )
 
     def across(self, way, k):
         step = (2, -2)[way]
         origin = lax.rem(self.me - step * k + 2 * self.n, self.n)
-        source = self.own if k == 0 else self.place(origin)
+        source = self.own if k == 0 else self.place(origin, self.me)
         slot = (2 + way) * self.chips + k
+        target = self.me ^ 1
         return remote(
             source,
-            self.place(origin),
+            self.place(origin, target),
             self.sent.at[self.row, slot],
             self.arrived.at[self.row, slot],
-            (self.me ^ 1, self.col),
+            (target, self.col),
         )
 
     def sends(self, way, k):
@@ -194,7 +194,9 @@
         return self.chip >= k if way == 0 else self.chip < self.chips - k
 
     def start(self):
-        self.keep = pltpu.make_async_copy(self.own, self.place(self.me), self.local.at[self.row])
+        self.keep = pltpu.make_async_copy(
+            self.own, self.place(self.me, self.me), self.local.at[self.row]
+        )
         self.keep.start()
         for way in (0, 1):
             pl.when(self.sends(way, 1))(self.copy(way, 1).start)
@@ -210,14 +212,43 @@
 
             if k < self.chips - 1:
                 pl.when(self.sends(way, k + 1))(self.copy(way, k + 1).start)
+        if self.pass_on is not None:
+            self.hand_on(k)
+
+    def crossed(self, way, k):
+        self.across(way, k).wait_recv()
+        if self.pass_on is not None:
+            self.pass_on(lax.rem((self.me ^ 1) - (2, -2)[way] * k + 2 * self.n, self.n))
+
+    def hand_on(self, k):
+        if k == 1:
+            self.keep.wait()
+            self.pass_on(self.me)
+            self.crossed(0, 0)
+        for way in (0, 1):
+
+            @pl.when(self.receives(way, k))
+            def _(way=way):
+                self.pass_on(lax.rem(self.me - (2, -2)[way] * k + 2 * self.n, self.n))
+
+            if k > 1:
+                pl.when(self.receives(way, k - 1))(functools.partial(self.crossed, way, k - 1))
 
     def finish(self):
-        self.keep.wait()
-        self.across(0, 0).wait()
+        passing = self.pass_on is not None
+        if passing:
+            for way in (0, 1):
+                k = self.chips - 1
+                pl.when(self.receives(way, k))(functools.partial(self.crossed, way, k))
+        else:
+            self.keep.wait()
+        last = self.across(0, 0)
+        (last.wait_send if passing else last.wait)()
         for way in (0, 1):
             for k in range(1, self.chips):
                 pl.when(self.sends(way, k))(self.copy(way, k).wait_send)
-                pl.when(self.receives(way, k))(self.across(way, k).wait)
+                last = self.across(way, k)
+                pl.when(self.receives(way, k))(last.wait_send if passing else last.wait)
 
 
 def line_sems(count, n):
@@ -233,28 +264,38 @@
     sent, arrived, local, share_sent, share_arrived = refs[2 * count :]
     me, col = lax.axis_index("dp"), lax.axis_index("mp")
     greet(peers(n, m))
+
+    def passed(a, i, k):
+        block = places[a](results[a], i, me)
+        slot = i * m + k
+        x = shares.index(a)
+        return remote(
+            block, block, share_sent.at[x, slot], share_arrived.at[x, slot], (me, col ^ k)
+        )
+
+    def pass_on(a, i):
+        for k in range(1, m):
+            passed(a, i, k).start()
+
     lines = []
     for a in range(count):
         place = functools.partial(places[a], results[a])
-        lines.append(Line(sources[a], place, (sent, arrived, local), a))
+        hook = functools.partial(pass_on, a) if a in shares else None
+        lines.append(Line(sources[a], place, (sent, arrived, local), a, hook))
         lines[-1].start()
     for k in range(1, n // 2):
         for line in lines:
             line.step(k)
     for line in lines:
         line.finish()
-
-    def passed(x, a, s):
-        whole = results[a].at[col]
-        return remote(
-            whole, whole, share_sent.at[x, s], share_arrived.at[x, s], (me, col ^ s)
-        )
-
-    copies = [passed(x, a, s) for x, a in enumerate(shares) for s in range(1, m)]
-    for c in copies:
-        c.start()
-    for c in copies:
-        c.wait()
+    for a in shares:
+
+        def body(i, carry, a=a):
+            for k in range(1, m):
+                passed(a, i, k).wait()
+            return carry
+
+        lax.fori_loop(0, n, body, 0)
 
 
 def gather_all(arrays, shapes, places, shares, collective_id):
@@ -266,26 +307,32 @@
         in_specs=[HBM] * count,
         out_specs=[HBM] * count,
         scratch_shapes=line_sems(count, n)
-        + [pltpu.SemaphoreType.DMA((max(len(shares), 1), m))] * 2,
+        + [pltpu.SemaphoreType.DMA((max(len(shares), 1), n * m))] * 2,
         compiler_params=pltpu.CompilerParams(collective_id=collective_id, has_side_effects=True),
         name="gather_all",
     )(*arrays)
 
 
 def by_rows(size):
-    return lambda ref, i: ref.at[at(i, size)]
+    return lambda ref, i, j: ref.at[at(i, size)]
 
 
 def by_columns(size):
-    return lambda ref, i: ref.at[:, at(i, size)]
-
-
-def by_lead(ref, i):
+    return lambda ref, i, j: ref.at[:, at(i, size)]
+
+
+def by_lead(ref, i, j):
     return ref.at[i]
 
 
+def in_turn(ref, i, j):
+    chips = lax.axis_size("dp") // 2
+    chip = lax.rem(i // 2 - j // 2 + chips, chips)
+    return ref.at[chip + chips * lax.rem(i + j, 2)]
+
+
 def by_share(size):
-    return lambda ref, i: ref.at[lax.axis_index("mp"), at(i, size)]
+    return lambda ref, i, j: ref.at[lax.axis_index("mp"), at(i, size)]
 
 
 def deal_kernel(n, m, kinds, lines_count, *refs):
@@ -430,7 +477,7 @@
     lines = []
     for a in range(lines_count):
         ref = results[count + a]
-        place = functools.partial(by_rows(ref.shape[0] // n), ref)
+        place = functools.partial(in_turn, ref)
         lines.append(Line(sources[count + a], place, (line_sent, line_arrived, line_local), a))
     begin(0)
     begin(1)
@@ -463,7 +510,7 @@
             shapes.append((m,) + w.shape)
         else:
             shapes.append((n * r, m * (c // n)) if kind == 0 else (m * (r // n), n * c))
-    shapes += [(n * a.shape[0], a.shape[1]) for a in arrays]
+    shapes += [(n,) + a.shape for a in arrays]
     pair = [pltpu.SemaphoreType.DMA((count, n))] * 2
     return pl.pallas_call(
         functools.partial(deal_kernel, n, m, kinds, len(arrays)),
@@ -480,76 +527,324 @@
     )(*weights, *arrays)
 
 
-def return_kernel(n, kinds, *refs):
+ROWS = 0
+COLUMNS = 1
+CHIPS = 2
+PARTS = 3
+WHOLE = 4
+SWAP_X = 5
+SWAP_Y = 6
+HALVES_0 = 10
+HALVES_1 = 11
+WORLD = 7
+SPREAD = 8
+EACH = 9
+
+KEPT = (ROWS, COLUMNS, EACH, WORLD, SPREAD)
+
+
+def exchange_kernel(n, m, kinds, jobs, *refs):
     count = len(kinds)
-    sources, results = refs[:count], refs[count : 2 * count]
-    sent, arrived, local = refs[2 * count :]
+    takes, gives = sum(j.takes for j in jobs), sum(j.gives for j in jobs)
+    sources, given = refs[:count], refs[count : count + takes]
+    results, made = refs[count + takes : 2 * count + takes], refs[2 * count + takes :][:gives]
+    sent, arrived, local = refs[2 * count + takes + gives :]
     me, col = lax.axis_index("dp"), lax.axis_index("mp")
-    greet(peers(n, 1))
-
-    def source(t, i):
-        ref = sources[t]
-        if kinds[t] == 0:
-            return ref.at[at(i, ref.shape[0] // n)]
-        if kinds[t] == 1:
-            return ref.at[:, at(i, ref.shape[1] // n)]
-        return ref if kinds[t] == 3 else ref.at[i // 2 if kinds[t] == 2 else i]
-
-    def place(t):
-        ref = results[t]
-        if kinds[t] == 0:
-            return ref.at[:, at(me, ref.shape[1] // n)]
-        if kinds[t] == 1:
-            return ref.at[at(me, ref.shape[0] // n)]
-        return ref.at[me // 2] if kinds[t] == 2 else ref.at[me]
-
-    def move(t, s):
-        target = lax.rem(me + s, n)
-        return remote(
-            source(t, target), place(t), sent.at[t, s], arrived.at[t, s], (target, col)
-        )
+    world = any(kind in (WORLD, SPREAD) for kind in kinds)
+    over_dp = any(kind in (ROWS, COLUMNS, CHIPS, EACH) for kind in kinds)
+    over_mp = any(kind in (PARTS, WHOLE, SWAP_X, SWAP_Y, HALVES_0, HALVES_1) for kind in kinds)
+    if world:
+        greet([(lax.rem(me + s, n), col ^ k) for s in range(n) for k in range(m) if s or k])
+    else:
+        greet(peers(n if over_dp else 1, m if over_mp else 1))
+
+    def move(t, s, k=0):
+        kind, src, dst = kinds[t], sources[t], results[t]
+        target, slot = (lax.rem(me + s, n), col), s
+        if kind == ROWS:
+            src = src.at[at(target[0], src.shape[0] // n)]
+            dst = dst.at[:, at(me, dst.shape[1] // n)]
+        elif kind == COLUMNS:
+            src = src.at[:, at(target[0], src.shape[1] // n)]
+            dst = dst.at[at(me, dst.shape[0] // n)]
+        elif kind == EACH:
+            src, dst = src.at[target[0]], dst.at[me]
+        elif kind == CHIPS:
+            target = (lax.rem(me + 2 * s, n), col)
+            src, dst = src.at[s], dst.at[s]
+        elif kind == PARTS:
+            target, slot, src, dst = (me, col ^ k), k, src.at[k], dst.at[k]
+        elif kind == WHOLE:
+            target, slot, dst = (me, col ^ k), k, dst.at[k]
+        elif kind in (SWAP_X, SWAP_Y):
+            target, slot = (me, col ^ k), 0
+        elif kind in (HALVES_0, HALVES_1):
+            target, slot, dst = (me, col ^ (1 + k // 2)), k, dst.at[k]
+            axis = kind - HALVES_0
+            width, deep = src.shape[axis] // m, src.shape[1 - axis] // 2
+            block = pl.ds((1, 3, 2, 3)[k] * width, width)
+            half = pl.ds(k // 2 * deep, deep)
+            src = src.at[half, block] if axis else src.at[block, half]
+        else:
+            target, slot = (target[0], col ^ k), s * m + k
+            src = src if kind == WORLD else src.at[target[0]]
+            dst = dst.at[me, col]
+        return remote(src, dst, sent.at[t, slot], arrived.at[t, slot], target)
 
     def keep(t):
-        return pltpu.make_async_copy(source(t, me), place(t), local.at[t])
+        kind, src, dst = kinds[t], sources[t], results[t]
+        if kind == ROWS:
+            src, dst = src.at[at(me, src.shape[0] // n)], dst.at[:, at(me, dst.shape[1] // n)]
+        elif kind == COLUMNS:
+            src, dst = src.at[:, at(me, src.shape[1] // n)], dst.at[at(me, dst.shape[0] // n)]
+        elif kind == EACH:
+            src, dst = src.at[me], dst.at[me]
+        elif kind in (WORLD, SPREAD):
+            src, dst = src if kind == WORLD else src.at[me], dst.at[me, col]
+        return pltpu.make_async_copy(src, dst, local.at[t])
 
     def each(t, do):
-        if kinds[t] == 2:
-            lax.fori_loop(1, n // 2, lambda s, c: (do(t, 2 * s), c)[1], 0)
+        kind = kinds[t]
+        if kind in (ROWS, COLUMNS, EACH):
+            lax.fori_loop(1, n, lambda s, c: (do(move(t, s)), c)[1], 0)
+        elif kind == CHIPS:
+            lax.fori_loop(1, n // 2, lambda s, c: (do(move(t, s)), c)[1], 0)
+        elif kind in (PARTS, WHOLE):
+            for k in range(1, m):
+                do(move(t, 0, k))
+        elif kind in (SWAP_X, SWAP_Y):
+            do(move(t, 0, 1 if kind == SWAP_X else 2))
+        elif kind in (HALVES_0, HALVES_1):
+            for k in range(4):
+                do(move(t, 0, k))
         else:
-            lax.fori_loop(1, n, lambda s, c: (do(t, s), c)[1], 0)
+            for k in range(m):
+                lax.fori_loop(0 if k else 1, n, lambda s, c, k=k: (do(move(t, s, k)), c)[1], 0)
 
     for t in range(count):
-        keep(t).start()
-        each(t, lambda t, s: move(t, s).start())
+        if kinds[t] in KEPT:
+            keep(t).start()
+        each(t, lambda c: c.start())
+    for job in jobs:
+        job.run(given[: job.takes], made[: job.gives])
+        given, made = given[job.takes :], made[job.gives :]
     for t in range(count):
-        keep(t).wait()
-        each(t, lambda t, s: move(t, s).wait())
-
-
-def return_all(arrays, kinds, collective_id):
-    n = lax.axis_size("dp")
-    count = len(arrays)
+        if kinds[t] in KEPT:
+            keep(t).wait()
+        each(t, lambda c: c.wait())
+
+
+def exchange_all(flows, collective_id, jobs=()):
+    n, m = lax.axis_size("dp"), lax.axis_size("mp")
+    arrays, kinds = [f[0] for f in flows], tuple(f[1] for f in flows)
+    count = len(flows)
     shapes = []
-    for a, kind in zip(arrays, kinds):
-        if kind == 0:
+    for a, kind in flows:
+        if kind == ROWS:
             shapes.append((a.shape[0] // n, a.shape[1] * n))
-        elif kind == 1:
+        elif kind == COLUMNS:
             shapes.append((a.shape[0] * n, a.shape[1] // n))
+        elif kind == WHOLE:
+            shapes.append((m,) + a.shape)
+        elif kind == WORLD:
+            shapes.append((n, m) + a.shape)
+        elif kind == SPREAD:
+            shapes.append((n, m) + a.shape[1:])
+        elif kind == HALVES_0:
+            shapes.append((4, a.shape[0] // m, a.shape[1] // 2))
+        elif kind == HALVES_1:
+            shapes.append((4, a.shape[0] // 2, a.shape[1] // m))
         else:
-            shapes.append((n,) + a.shape if kind == 3 else a.shape)
+            shapes.append(a.shape)
+    inputs = [a for job in jobs for a in job.arrays]
+    outputs = [jax.ShapeDtypeStruct(s, BF) for job in jobs for s in job.shapes]
     return pl.pallas_call(
-        functools.partial(return_kernel, n, kinds),
-        out_shape=[jax.ShapeDtypeStruct(s, a.dtype) for s, a in zip(shapes, arrays)],
-        in_specs=[HBM] * count,
-        out_specs=[HBM] * count,
+        functools.partial(exchange_kernel, n, m, kinds, [job.bare() for job in jobs]),
+        out_shape=[jax.ShapeDtypeStruct(s, a.dtype) for s, a in zip(shapes, arrays)] + outputs,
+        in_specs=[HBM] * (count + len(inputs)),
+        out_specs=[HBM] * (count + len(outputs)),
         scratch_shapes=[
-            pltpu.SemaphoreType.DMA((count, n)),
-            pltpu.SemaphoreType.DMA((count, n)),
-            pltpu.SemaphoreType.DMA((count,)),
+            pltpu.SemaphoreType.DMA((max(count, 1), n * m)),
+            pltpu.SemaphoreType.DMA((max(count, 1), n * m)),
+            pltpu.SemaphoreType.DMA((max(count, 1),)),
         ],
-        compiler_params=pltpu.CompilerParams(collective_id=collective_id, has_side_effects=True),
-        name="return_all",
-    )(*arrays)
+        compiler_params=pltpu.CompilerParams(
+            collective_id=collective_id, has_side_effects=True, vmem_limit_bytes=56 << 20
+        ),
+        name="exchange",
+    )(*arrays, *inputs)
+
+
+class Job:
+    def __init__(self, body, arrays, shapes):
+        self.body, self.arrays, self.shapes = body, arrays, shapes
+        self.takes, self.gives = len(arrays), len(shapes)
+
+    def bare(self):
+        job = Job(self.body, (), self.shapes)
+        job.takes = self.takes
+        return job
+
+    def run(self, inputs, outputs):
+        self.body(inputs, outputs)
+
+
+def tile(size, most):
+    return max(t for t in range(16, most + 1, 16) if size % t == 0)
+
+
+def products_plain(inputs, outputs):
+    a, b = inputs
+    (rows, depth), width = a.shape, b.shape[1]
+    bm, bn = tile(rows, 416), tile(width, 512)
+
+    def body(a_ref, b_ref, o_ref):
+        o_ref[...] = dot_plain(a_ref[...], b_ref[...]).astype(BF)
+
+    pltpu.emit_pipeline(
+        body,
+        grid=(width // bn, rows // bm),
+        in_specs=[
+            pl.BlockSpec((bm, depth), lambda j, i: (i, 0)),
+            pl.BlockSpec((depth, bn), lambda j, i: (0, j)),
+        ],
+        out_specs=[pl.BlockSpec((bm, bn), lambda j, i: (i, j))],
+    )(a, b, outputs[0])
+
+
+def products_right(inputs, outputs):
+    pairs = len(inputs) // 2
+    (rows, depth), width = inputs[0].shape, inputs[1].shape[0]
+    bm, bn = tile(rows, 416), tile(width, 512)
+
+    def body(*refs):
+        total = dot_right(refs[0][...], refs[1][...])
+        for p in range(1, pairs):
+            total = total + dot_right(refs[2 * p][...], refs[2 * p + 1][...])
+        refs[-1][...] = total.astype(BF)
+
+    pltpu.emit_pipeline(
+        body,
+        grid=(width // bn, rows // bm),
+        in_specs=[
+            pl.BlockSpec((bm, depth), lambda j, i: (i, 0)),
+            pl.BlockSpec((bn, depth), lambda j, i: (j, 0)),
+        ]
+        * pairs,
+        out_specs=[pl.BlockSpec((bm, bn), lambda j, i: (i, j))],
+    )(*inputs, outputs[0])
+
+
+def products_left(inputs, outputs):
+    a, rest = inputs[0], inputs[1:]
+    (depth, rows), width = a.shape, rest[0].shape[1]
+    bm, bn = tile(rows, 1024), tile(width, 512)
+    count = len(rest)
+
+    def body(a_ref, *refs):
+        for p in range(count):
+            refs[count + p][...] = dot_left(a_ref[...], refs[p][...]).astype(BF)
+
+    pltpu.emit_pipeline(
+        body,
+        grid=(rows // bm, width // bn),
+        in_specs=[pl.BlockSpec((depth, bm), lambda i, j: (0, i))]
+        + [pl.BlockSpec((depth, bn), lambda i, j: (0, j))] * count,
+        out_specs=[pl.BlockSpec((bm, bn), lambda i, j: (i, j))] * count,
+    )(a, *rest, *outputs)
+
+
+def hidden_forward(inputs, outputs):
+    h, w_gate, w_up = inputs
+    (rows, depth), width = h.shape, w_gate.shape[1]
+    bm, bn = tile(rows, 416), tile(width, 512)
+
+    def body(h_ref, gate_w, up_w, gate_ref, up_ref, hidden_ref):
+        gate = dot_plain(h_ref[...], gate_w[...])
+        upward = dot_plain(h_ref[...], up_w[...])
+        gate_ref[...] = gate.astype(BF)
+        up_ref[...] = upward.astype(BF)
+        hidden_ref[...] = glu_value(gate, upward).astype(BF)
+
+    block = pl.BlockSpec((bm, bn), lambda j, i: (i, j))
+    pltpu.emit_pipeline(
+        body,
+        grid=(width // bn, rows // bm),
+        in_specs=[pl.BlockSpec((bm, depth), lambda j, i: (i, 0))]
+        + [pl.BlockSpec((depth, bn), lambda j, i: (0, j))] * 2,
+        out_specs=[block] * 3,
+    )(h, w_gate, w_up, *outputs)
+
+
+def hidden_backward(inputs, outputs):
+    gz, w_down, gate, upward = inputs
+    (rows, depth), width = gz.shape, w_down.shape[0]
+    bm, bn = tile(rows, 416), tile(width, 512)
+
+    def body(gz_ref, down_w, gate_ref, up_ref, dgate_ref, dup_ref):
+        grad = dot_right(gz_ref[...], down_w[...])
+        unused, pull = jax.vjp(
+            glu_value, gate_ref[...].astype(F32), up_ref[...].astype(F32)
+        )
+        dgate, dup = pull(grad)
+        dgate_ref[...] = dgate.astype(BF)
+        dup_ref[...] = dup.astype(BF)
+
+    block = pl.BlockSpec((bm, bn), lambda j, i: (i, j))
+    pltpu.emit_pipeline(
+        body,
+        grid=(width // bn, rows // bm),
+        in_specs=[
+            pl.BlockSpec((bm, depth), lambda j, i: (i, 0)),
+            pl.BlockSpec((bn, depth), lambda j, i: (j, 0)),
+            block,
+            block,
+        ],
+        out_specs=[block] * 2,
+    )(gz, w_down, gate, upward, *outputs)
+
+
+class Halves:
+    def __init__(self, whole, axis):
+        self.whole, self.axis = whole, axis
+
+    def first(self):
+        return [(self.whole, HALVES_1 if self.axis else HALVES_0)]
+
+    def take(self, got):
+        top, low = jnp.split(self.whole, 2, axis=1 - self.axis)
+        t, b = jnp.split(top, 4, axis=self.axis), jnp.split(low, 4, axis=self.axis)
+        self.top, self.next_y = add(t[0], got[0]), add(t[2], got[1])
+        self.low, self.next_x = add(b[0], got[2]), add(b[1], got[3])
+
+    def second(self):
+        return [(self.next_y, SWAP_Y), (self.next_x, SWAP_X)]
+
+    def total(self, from_y, from_x):
+        return jnp.concatenate(
+            [add(self.top, from_y), add(self.low, from_x)], axis=1 - self.axis
+        )
+
+
+class Direct:
+    def __init__(self, whole, axis):
+        self.whole, self.axis = whole, axis
+
+    def first(self):
+        return []
+
+    def take(self):
+        self.sum = reduce_mp(self.whole, self.axis).astype(BF)
+
+    def second(self):
+        return []
+
+    def total(self):
+        return self.sum
+
+
+def add(left, right):
+    return (left.astype(F32) + right.astype(F32)).astype(BF)
 
 
 def local(
@@ -694,6 +989,9 @@
         jnp.pad(act_in, ((0, acts - steps), (0, 0))).reshape(m, aq, dims_count)
     ).reshape(acts, dims_count)
 
+    gz_pre, embed = lax.optimization_barrier((gz_pre, embed))
+    gz_pre_all = gather_dp(gz_pre).reshape(n * rq, wide)
+
     x_pre = x_blocks.reshape(rows, wide).astype(F32)
     h1_pre = rms_gain(x_pre, gain_pa).astype(BF)
     x_act = dot_plain(act_in, embed)
@@ -725,21 +1023,17 @@
     mixed = jnp.concatenate(mixed, axis=1)
 
     def blocks_of(pre, act):
-        return jnp.concatenate(
-            [
-                pack(pre[s * rq : (s + 1) * rq], act[s * aq : (s + 1) * aq])
-                for s in range(m)
-            ],
-            axis=0,
+        return jnp.stack(
+            [pack(pre[s * rq : (s + 1) * rq], act[s * aq : (s + 1) * aq]) for s in range(m)]
         )
 
     def rows_of(blocks):
-        pairs = [unpack(b, rq, narrow) for b in jnp.split(blocks, m, axis=0)]
-        return jnp.concatenate([p[0] for p in pairs] + []), jnp.concatenate([p[1] for p in pairs])
+        pairs = [unpack(b, rq, narrow) for b in blocks]
+        return jnp.concatenate([p[0] for p in pairs]), jnp.concatenate([p[1] for p in pairs])
 
     y_pre = dot_plain(mixed[:rows], w_out_pre).astype(BF)
     y_act = dot_plain(mixed[rows:], w_out_act).astype(BF)
-    y = reduce_mp(blocks_of(y_pre, y_act), 0)
+    y = reduce_mp(blocks_of(y_pre, y_act), 0)[0]
     y_pre, y_act = unpack(y, rq, narrow)
     x2_pre = x_pre[:rq] + y_pre
     x2_act = x_act[:aq] + y_act
@@ -747,7 +1041,7 @@
 
 
     def items_of(blocks):
-        pairs = [unpack(b, rq, narrow) for b in jnp.split(blocks, n, axis=0)]
+        pairs = [unpack(blocks[i], rq, narrow) for i in range(n)]
         return jnp.concatenate([p[0] for p in pairs]), jnp.concatenate([p[1] for p in pairs])
 
     def by_item(pre, act):
@@ -771,8 +1065,8 @@
         ],
         axis=1,
     )
-    wg, wu, wd, act_weights, h2_all, gz_pre_all = deal_all(
-        [pre_gate, pre_up, pre_down, act_weights], (0, 0, 1, 2), [h2, gz_pre], 2
+    wg, wu, wd, act_weights, h2_all = deal_all(
+        [pre_gate, pre_up, pre_down, act_weights], (0, 0, 1, 2), [h2], 2
     )
 
     def square(array):
@@ -781,55 +1075,105 @@
     ag, au = square(act_weights[:, :, :d_act]), square(act_weights[:, :, d_act : 2 * d_act])
     ad = square(act_weights[:, :, 2 * d_act :]).T
     h2_pre, h2_act = items_of(h2_all)
-    match = (lax.broadcasted_iota(jnp.int32, (n, 1), 0) == slot_all[None, :]).astype(BF)
+    half = n // 2
+    turns = [lax.rem(me + 2 * k, n) for k in range(half)]
+    turns = turns + [t ^ 1 for t in turns]
+    match = (jnp.stack(turns)[:, None] == slot_all[None, :]).astype(BF)
     gz_act_all = dot_plain(match, cot_all.reshape(cot_all.shape[0], -1)).astype(BF)
     gz_act_all = gz_act_all.reshape(n * aq, narrow)
-    gz_act = lax.dynamic_slice_in_dim(gz_act_all, me * aq, aq, 0)
-
-    def forward(h2_rows, gate_w, up_w, down_w):
+    gz_act = gz_act_all[:aq]
+
+    summed = Halves if m == 4 else Direct
+
+    def feed_forward(h2_rows, gate_w, up_w, down_w, gz):
         gate = dot_plain(h2_rows, gate_w)
         upward = dot_plain(h2_rows, up_w)
         hidden = glu_value(gate, upward).astype(BF)
-        return gate.astype(BF), upward.astype(BF), hidden, dot_plain(hidden, down_w).astype(BF)
-
-    def backward(h2_rows, gate, upward, hidden, gate_w, up_w, down_w, gz):
+        z = dot_plain(hidden, down_w).astype(BF)
+        g_down = dot_left(hidden, gz).astype(BF)
         grad_hidden = dot_right(gz, down_w)
-        unused, pull = jax.vjp(glu_value, gate.astype(F32), upward.astype(F32))
+        unused, pull = jax.vjp(glu_value, gate, upward)
         dgate, dup = pull(grad_hidden)
         dgate, dup = dgate.astype(BF), dup.astype(BF)
+        g_gate, g_up = dot_left(h2_rows, dgate).astype(BF), dot_left(h2_rows, dup).astype(BF)
         dh2 = (dot_right(dgate, gate_w) + dot_right(dup, up_w)).astype(BF)
-        return (
-            dh2,
-            dot_left(h2_rows, dgate).astype(BF),
-            dot_left(h2_rows, dup).astype(BF),
-            dot_left(hidden, gz).astype(BF),
-        )
-
-    gate_p, up_p, hid_p, z_p = forward(h2_pre, wg, wu, wd)
-    gate_a, up_a, hid_a, z_a = forward(h2_act, ag, au, ad)
-    dh2_p, g_gate_p, g_up_p, g_down_p = backward(
-        h2_pre, gate_p, up_p, hid_p, wg, wu, wd, gz_pre_all
-    )
-    dh2_a, g_gate_a, g_up_a, g_down_a = backward(
-        h2_act, gate_a, up_a, hid_a, ag, au, ad, gz_act_all
-    )
-    z_pre, z_act = unpack(reduce_dp(by_item(z_p, z_a)), rq, narrow)
-    dh2_pre, dh2_act = unpack(reduce_dp(by_item(dh2_p, dh2_a)), rq, narrow)
+        return z, dh2, g_gate, g_up, g_down
+
+    z_a, dh2_a, g_gate_a, g_up_a, g_down_a = feed_forward(h2_act, ag, au, ad, gz_act_all)
+    items, units = n * rq, wg.shape[1]
+    gate = dot_plain(h2_pre, wg)
+    upward = dot_plain(h2_pre, wu)
+    hidden = glu_value(gate, upward).astype(BF)
+    gate, upward = gate.astype(BF), upward.astype(BF)
+    g_down = summed(dot_left(hidden, gz_pre_all).astype(BF), 0)
+    z_parts = pair_sum(by_item(dot_plain(hidden, wd).astype(BF), z_a))
+    *got, dgate, dup = exchange_all(
+        [(z_parts, CHIPS)] + g_down.first(),
+        7,
+        [Job(hidden_backward, [gz_pre_all, wd, gate, upward], [(items, units)] * 2)],
+    )
+    z_sum = z_parts[0].astype(F32)
+    for k in range(1, half):
+        z_sum = z_sum + got[0][k].astype(F32)
+    z_pre, z_act = unpack(z_sum, rq, narrow)
+    g_down.take(*got[1:])
+    *got, g_gate, g_up = exchange_all(
+        g_down.second(),
+        8,
+        [Job(products_left, [h2_pre, dgate, dup], [(wide, units)] * 2)],
+    )
+    g_down = g_down.total(*got)
+    g_gate, g_up = summed(g_gate, 1), summed(g_up, 1)
+    grad_down, *got, dh2_p = exchange_all(
+        [(g_down, COLUMNS)] + g_gate.first() + g_up.first(),
+        9,
+        [Job(products_right, [dgate, wg, dup, wu], [(items, wide)])],
+    )
+    g_gate.take(*got[: len(got) // 2])
+    g_up.take(*got[len(got) // 2 :])
+    dh2_parts = pair_sum(by_item(dh2_p, dh2_a))
+    act_back = jnp.stack(
+        [
+            jnp.concatenate(
+                [
+                    g_gate_a[:, k * few : (k + 1) * few],
+                    g_up_a[:, k * few : (k + 1) * few],
+                    g_down_a[k * few : (k + 1) * few].T,
+                ],
+                axis=0,
+            )
+            for k in range(m)
+        ]
+    )
+    got = exchange_all(
+        [(dh2_parts, CHIPS), (act_back, PARTS)] + g_gate.second() + g_up.second(), 3
+    )
+    dh2 = dh2_parts[0].astype(F32)
+    for k in range(1, half):
+        dh2 = dh2 + got[0][k].astype(F32)
+    dh2_pre, dh2_act = unpack(dh2, rq, narrow)
+    act_sum = act_back[0].astype(F32)
+    for k in range(1, m):
+        act_sum = act_sum + got[1][k].astype(F32)
+    act_sum = act_sum.astype(BF).reshape(3, n, d_act, few).transpose(1, 0, 2, 3)
+    act_sum = act_sum.reshape(n, 3 * d_act, few)
+    pairs = len(g_gate.second())
+    g_gate = g_gate.total(*got[2 : 2 + pairs])
+    g_up = g_up.total(*got[2 + pairs :])
 
     def natural(blocks, count):
         return jnp.concatenate([pick_mp(blocks, place) for place in range(m)], axis=0)[:count]
 
     out_pre = (x2_pre + z_pre).astype(BF)
     out_act = (x2_act + z_act).astype(BF)
-    prefix_output = natural([out_pre] + [swap_mp(out_pre, s) for s in range(1, m)], length)
-    out_act = natural([out_act] + [swap_mp(out_act, s) for s in range(1, m)], acts)
-
     gx2n_pre, g_gain_pf = norm_backward(x2_pre, gain_pf, dh2_pre)
     gx2n_act, g_gain_af = norm_backward(x2_act, gain_af, dh2_act)
     gx2_pre = gz_pre.astype(F32) + gx2n_pre
     gx2_act = gz_act.astype(F32) + gx2n_act
-    gy = gather_mp(pack(gx2_pre.astype(BF), gx2_act.astype(BF)), 0)
-    gy_pre, gy_act = rows_of(gy)
+    gy = pack(gx2_pre.astype(BF), gx2_act.astype(BF))
+    got = exchange_all([(gy, WHOLE), (g_gate, ROWS)], 4)
+    gy_pre, gy_act = rows_of([gy] + [got[0][k] for k in range(1, m)])
+    grad_gate = got[1].astype(F32)
 
     g_out_pre = dot_left(mixed[:rows], gy_pre).astype(BF)
     g_out_act = dot_left(mixed[rows:], gy_act).astype(BF)
@@ -848,16 +1192,20 @@
         gv = gv + dot_left(probs[h], gm)
     gkv = jnp.concatenate([gk, gv], axis=1).astype(BF)
 
-    def share(s):
-        return lax.dynamic_slice_in_dim(gkv, (col ^ s) * kvw, kvw, 1)
-
-    gkv_sum = share(0).astype(F32)
-    for s in range(1, m):
-        gkv_sum = gkv_sum + reorder(swap_mp(share(s), s), s).astype(F32)
+    shares = [lax.dynamic_slice_in_dim(gkv, (col ^ k) * kvw, kvw, 1) for k in range(m)]
     gin = jnp.concatenate(gq + [gkv], axis=1)
     gh1_pre = dot_right(gin[:rows], w_in_pre).astype(BF)
     gh1_act = dot_right(gin[rows:], w_in_act).astype(BF)
-    gh1 = reduce_mp(blocks_of(gh1_pre, gh1_act), 0)
+    gh1_parts = blocks_of(gh1_pre, gh1_act)
+    got = exchange_all(
+        [(jnp.stack(shares), PARTS), (gh1_parts, PARTS), (g_up, ROWS)], 5
+    )
+    gkv_sum = shares[0].astype(F32)
+    gh1 = gh1_parts[0].astype(F32)
+    for k in range(1, m):
+        gkv_sum = gkv_sum + reorder(got[0][k], k).astype(F32)
+        gh1 = gh1 + got[1][k].astype(F32)
+    grad_up = got[2].astype(F32)
     gh1_pre, gh1_act = unpack(gh1, rq, narrow)
     gin = jnp.concatenate(gq + [gkv_sum.astype(BF)], axis=1)
     g_in_pre = dot_left(h1_pre, gin[:rows]).astype(BF)
@@ -866,14 +1214,9 @@
     gxn_pre, g_gain_pa = norm_backward(x_pre[:rq], gain_pa, gh1_pre)
     gxn_act, g_gain_aa = norm_backward(x_act[:aq], gain_aa, gh1_act)
     grad_pre = (gx2_pre + gxn_pre).astype(BF)
-    prefix_grad = natural(
-        [grad_pre] + [swap_mp(grad_pre, s) for s in range(1, m)], length
-    ).astype(F32)
     gxa = (gx2_act + gxn_act).astype(BF)
     g_embed = dot_left(act_in[:aq], gxa)
     act_grad = dot_right(gxa, embed)
-    act_grad = natural([act_grad] + [swap_mp(act_grad, s) for s in range(1, m)], acts)
-
     def by_index(vector):
         return vector.reshape(n, -1, narrow // n).transpose(1, 0, 2).reshape(-1, narrow)
 
@@ -889,59 +1232,52 @@
     )
     tiny_rows = tiny.shape[0]
     tiny = columns_first(pad_rows(tiny, round_up(tiny_rows, 8)))
-    tiny_sum = tiny
-    for s in range(1, m):
-        tiny_sum = tiny_sum + swap_mp(tiny, s)
-    act_grad, out_act, tiny = return_all(
-        [jnp.pad(act_grad, ((0, 0), (0, lanes - dims_count))), out_act, tiny_sum], (3, 3, 4), 4
-    )
+
+    def attn_block(item):
+        left = lax.dynamic_slice_in_dim(g_in_pre, item * d_pre, d_pre, 0)
+        out = lax.dynamic_slice_in_dim(g_out_pre, item * d_pre, d_pre, 1)
+        left_a = lax.dynamic_slice_in_dim(g_in_act, item * d_act, d_act, 0)
+        out_a = lax.dynamic_slice_in_dim(g_out_act, item * d_act, d_act, 1)
+        top = jnp.concatenate([left] + jnp.split(out, out.shape[0] // d_pre, axis=0), axis=1)
+        low = jnp.concatenate([left_a] + jnp.split(out_a, out_a.shape[0] // d_act, axis=0), axis=1)
+        return jnp.concatenate([top, low], axis=0)
+
+    parts = pair_sum(jnp.stack([attn_block(i) for i in turns]))
+    got = exchange_all(
+        [
+            (act_sum, EACH),
+            (parts, CHIPS),
+            (grad_pre, WHOLE),
+            (out_pre, WHOLE),
+            (jnp.pad(act_grad, ((0, 0), (0, lanes - dims_count))), WORLD),
+            (out_act, WORLD),
+            (tiny, SPREAD),
+        ],
+        6,
+    )
+    grad_down = grad_down.astype(F32)
+    act_back = got[0].astype(F32)
+    grad_gate_a = act_back[:, :d_act].transpose(1, 0, 2).reshape(d_act, n * few)
+    grad_up_a = act_back[:, d_act : 2 * d_act].transpose(1, 0, 2).reshape(d_act, n * few)
+    grad_down_a = act_back[:, 2 * d_act :].transpose(0, 2, 1).reshape(n * few, d_act)
+    total = parts[0].astype(F32)
+    for k in range(1, half):
+        total = total + got[1][k].astype(F32)
+    prefix_grad = natural([grad_pre] + [got[2][k] for k in range(1, m)], length).astype(F32)
+    prefix_output = natural([out_pre] + [got[3][k] for k in range(1, m)], length)
+    act_grad = got[4].reshape(n, acts, lanes)[:, :steps, :dims_count]
+    out_act = got[5].reshape(n, acts, narrow)[:, :steps]
     mine_items = (slot_item[:, None] == lax.broadcasted_iota(jnp.int32, (1, n), 1)).astype(BF)
-    action_output = dot_plain(mine_items, out_act[:, :steps].reshape(n, steps * narrow))
+    action_output = dot_plain(mine_items, out_act.reshape(n, steps * narrow))
     action_output = action_output.astype(BF).reshape(slot_count, steps, narrow)
     own_mask = lax.broadcasted_iota(jnp.int32, (slot_count, dims_count), 1) < valid_dims[:, None]
     action_grad = jnp.sum(
-        mine_items.astype(F32)[:, :, None, None] * act_grad[None, :, :steps, :dims_count], axis=1
+        mine_items.astype(F32)[:, :, None, None] * act_grad[None], axis=1
     ) * own_mask.astype(F32)[:, None, :]
-    tiny = jnp.sum(tiny, axis=0)
+    tiny = jnp.sum(got[6], axis=(0, 1))
     grad_gain_pa = tiny[:twice].reshape(-1)
     grad_gain_pf = tiny[twice : 2 * twice].reshape(-1)
     rest = tiny[2 * twice : tiny_rows]
-
-    def attn_block(item):
-        left = lax.slice_in_dim(g_in_pre, item * d_pre, (item + 1) * d_pre, axis=0)
-        out = lax.slice_in_dim(g_out_pre, item * d_pre, (item + 1) * d_pre, axis=1)
-        left_a = lax.slice_in_dim(g_in_act, item * d_act, (item + 1) * d_act, axis=0)
-        out_a = lax.slice_in_dim(g_out_act, item * d_act, (item + 1) * d_act, axis=1)
-        top = jnp.concatenate([left] + jnp.split(out, out.shape[0] // d_pre, axis=0), axis=1)
-        low = jnp.concatenate([left_a] + jnp.split(out_a, out_a.shape[0] // d_act, axis=0), axis=1)
-        return jnp.concatenate([top, low], axis=0)
-
-    act_back = jnp.concatenate(
-        [
-            g_gate_a.reshape(n, d_act, m * few),
-            g_up_a.reshape(n, d_act, m * few),
-            g_down_a.T.reshape(n, d_act, m * few),
-        ],
-        axis=1,
-    )
-    act_back = reduce_mp(act_back, 2).astype(BF)
-    parts = pair_sum(jnp.stack([attn_block(i) for i in range(n)]))
-    returned = return_all(
-        [
-            reduce_mp(g_down_p, 0).astype(BF),
-            reduce_mp(g_gate_p, 1).astype(BF),
-            reduce_mp(g_up_p, 1).astype(BF),
-            act_back,
-            parts,
-        ],
-        (1, 0, 0, 4, 2),
-        3,
-    )
-    grad_down, grad_gate, grad_up, act_back = [g.astype(F32) for g in returned[:4]]
-    grad_gate_a = act_back[:, :d_act].transpose(1, 0, 2).reshape(d_act, n * few)
-    grad_up_a = act_back[:, d_act : 2 * d_act].transpose(1, 0, 2).reshape(d_act, n * few)
-    grad_down_a = act_back[:, 2 * d_act :].transpose(0, 2, 1).reshape(n * few, d_act)
-    total = jnp.sum(returned[4].astype(F32), axis=0)
     grad_query, grad_kv = total[:d_pre, :split], total[:d_pre, split : split + kvw]
     grad_out = jnp.concatenate(
         jnp.split(total[:d_pre, split + kvw :], split // d_pre, axis=1), axis=0

time: 1620 us -> 1380 us (0.85); the launches traced: 1590 us -> 1370 us
  waiting for transfers between devices: 320 us -> 19.6 us
  Pallas kernels: 717 us -> 924 us
  matrix products: 242 us -> 137 us
  starting transfers between devices: 55.2 us -> 9.42 us
    pallas_call x2 -> x7, Pallas kernels: 288 us -> 562 us  [exchange_all(): pl.pallas_call(functools.partial(exchange_kernel, n, m, kinds, [job.bare(...]
    ppermute x42 -> x6, waiting for transfers between devices: 257 us -> 18.6 us  [swap_mp(): return lax.ppermute(block, 'mp', [(i, i ^ step) for i in range(size)])]
    dot_general x15 -> x12, matrix products: 95.4 us -> 17.3 us  [dot_right(): lax.dot_general(left, right, (((1,), (1,)), ((), ())), preferred_element_...]
    ppermute x6 -> x3, waiting for transfers between devices: 62.8 us -> 0.99 us  [send_dp(): lax.ppermute(block, 'dp', [(i, (i + step) % size) for i in range(size)])]
    ppermute x42 -> x6, starting transfers between devices: 50.7 us -> 6.98 us  [swap_mp(): return lax.ppermute(block, 'mp', [(i, i ^ step) for i in range(size)])]
    dot_general x15 -> x13, matrix products: 73.9 us -> 33.6 us  [dot_left(): lax.dot_general(left, right, (((0,), (0,)), ((), ())), preferred_element_...]
    pallas_call x1, Pallas kernels: 317 us -> 280 us  [deal_all(): pl.pallas_call(functools.partial(deal_kernel, n, m, kinds, len(arrays)),...]
    unnamed x398 -> x384, local copies, waits for them, and re-layouts: 38.7 us -> 70.4 us
  transfers between devices with their start and end apart: 51 -> 13, of which waited for: 17 -> 3; matrix products, arithmetic and copies ran while one was open for 14% -> 20% of each run, Pallas kernels for 5% -> 20%
where the time goes in v2:
time: 1380 us; the launch traced here: 1370 us
  Pallas kernels  924 us (67%)
  local copies, waits for them, and re-layouts  146 us (11%)
  matrix products  137 us (10%)
  other arithmetic  131 us (9%)
  waiting for transfers between devices  19.6 us (1%)
    pallas_call x7, Pallas kernels, exchange_all(): pl.pallas_call(functools.partial(exchange_kernel, n, m, kinds, [job.bare(...  562 us
    pallas_call x1, Pallas kernels, deal_all(): pl.pallas_call(functools.partial(deal_kernel, n, m, kinds, len(arrays)),...  280 us
    dot_general x17, matrix products, dot_plain(): return jnp.dot(left, right, preferred_element_type=F32)  86.4 us
    pallas_call x1, Pallas kernels, gather_all(): pl.pallas_call(functools.partial(gather_kernel, n, m, count, places, shar...  81.7 us
    unnamed x384, local copies, waits for them, and re-layouts  70.4 us
    dot_general x13, matrix products, dot_left(): lax.dot_general(left, right, (((0,), (0,)), ((), ())), preferred_element_...  33.6 us
    convert_element_type x9, other arithmetic, add(): return (left.astype(F32) + right.astype(F32)).astype(BF)  29.4 us
  transfers between devices with their start and end apart: 13, of which 3 were waited for; matrix products, arithmetic and copies ran while one was open for 20% of the time, Pallas kernels for 20%

profile of v2, /device:TPU:0, one launch (start us, length us, event | category | flops | bytes accessed | tf_op | source)
XLA Modules:
  0.0 1371.2 jit_solution(8641487259893777915)
XLA Ops:
  10.7 81.7 %gather_all.1 = (bf16[1024,128]{1,0:T(8,128)(2,1)}, s32[64,128]{1,0:T(8,128)}, bf16[2048,512]{1,0:T(8,128)(2,1)}, bf16[1024,512]{1,0:T(8,128)(2,1)}, bf16[4,2048...) custom-call(bf16[128,128]{1,0:T(8,128)(2,1)} %copy-done.131, ...), custom_call_target="tpu_custom_call" | custom-call | tf_op jit(solution)/shard_map/gather_all/pallas_call | solution.py:304
  97.9 4.1 pad.129
  123.7 3.7 fusion.10
  127.9 3.7 convolution_convert_fusion.8
  143.8 3.6 convolution_convert_fusion.5
  174.3 17.1 %collective-permute-done.1 = bf16[1,224,2048]{2,1,0:T(8,128)(2,1)} collective-permute-done((bf16[1,224,2048]{2,1,0:T(8,128)(2,1)}, bf16[1,224,2048]{2,1,0:T(8,128)(2,1)}, u32[]{:S(2)}, u32[]{:S(2)}) %collective-permute-start.1) | collective-permute-done | bytes 917536 | tf_op jit(solution)/shard_map/ppermute | solution.py:47
  197.8 280.5 %deal_all.1 = (bf16[2048,2048]{1,0:T(8,128)(2,1)}, bf16[2048,2048]{1,0:T(8,128)(2,1)}, bf16[2048,2048]{1,0:T(8,128)(2,1)}, bf16[4,8,384,128]{3,2,1,0:T(8,128)(2,1)}, bf16[8,224,2048]{2,1,0:T(8,128)(2,1)}) custom-call(bf16[256,4096]{1,0:T(8,128)(2,1)} %refs_0_.1, bf16[256,4096]{1,0:T(8,128)(2,1)} %refs_1_.1, bf16[4096,256]{1,0:T(8,128)(2,1)} %refs_2_.3, ...), custom_call_target="tpu_custom_call" | custom-call | tf_op jit(solution)/shard_map/deal_all/pallas_call | solution.py:515
  478.3 6.0 slice_bitcast_fusion.10
  516.3 20.3 %fusion.244 = f32[1664,2048]{1,0:T(8,128)} fusion(bf16[1664,2048]{1,0:T(8,128)(2,1)} %bitcast_dynamic-update-slice_fusion.refs_2_, bf16[2048,2048]{1,0:T(8,128)(2,1)} %get-tuple-element.81.refs_4_), kind=kOutput, calls=%fused_computation.631 | convolution fusion | flops 13958643712 | bytes 28835840 | tf_op jit(solution)/shard_map/dot_general | solution.py:30
  536.6 27.8 %fusion.228 = (bf16[1664,2048]{1,0:T(8,128)(2,1)}, bf16[1664,2048]{1,0:T(8,128)(2,1)}, bf16[1664,2048]{1,0:T(8,128)(2,1)}) fusion(f32[1664,2048]{1,0:T(8,128)} %fusion.244, bf16[1664,2048]{1,0:T(8,128)(2,1)} %bitcast_dynamic-update-slice_fusion.refs_2_, bf16[2048,2048]{1,0:T(8,128)(2,1)} %get-tuple-element.82.refs_6_), kind=kOutput, calls=%fused_computation.615 | convolution fusion | flops 13999538176 | bytes 49283072 | tf_op jit(solution)/shard_map/dot_general | solution.py:30
  564.4 18.5 %convolution_convert_fusion.2 = bf16[1664,2048]{1,0:T(8,128)(2,1)S(1)} fusion(bf16[1664,2048]{1,0:T(8,128)(2,1)} %get-tuple-element.201, bf16[2048,2048]{1,0:T(8,128)(2,1)} %get-tuple-element.84.refs_3_), kind=kOutput, calls=%fused_computation.12 | convolution fusion | flops 13962051584 | bytes 22020096 | tf_op jit(solution)/shard_map/dot_general | solution.py:30
  591.1 4.8 constant_dynamic-update-slice_fusion.16
  595.9 19.7 %convolution_convert_fusion.3.refs_1_ = bf16[2048,2048]{1,0:T(8,128)(2,1)} fusion(bf16[1664,2048]{1,0:T(8,128)(2,1)S(1)} %bitcast.655, bf16[1664,2048]{1,0:T(8,128)(2,1)} %bitcast.76.refs_2_), kind=kOutput, calls=%fused_computation.13 | convolution fusion | flops 13962838016 | bytes 22020096 | tf_op jit(solution)/shard_map/dot_general | solution.py:34
  618.4 70.0 %exchange.7 = (bf16[4,224,2048]{2,1,0:T(8,128)(2,1)}, bf16[4,512,1024]{2,1,0:T(8,128)(2,1)}, bf16[1664,2048]{1,0:T(8,128)(2,1)}, bf16[1664,2048]{1,0:T(8,128)(2,1)}) custom-call(bf16[4,224,2048]{2,1,0:T(8,128)(2,1)} %add_convert_fusion.1.refs_0_, bf16[2048,2048]{1,0:T(8,128)(2,1)} %convolution_convert_fusion.3.refs_1_, bf16[1664,2048]{1,0:T(8,128)(2,1)} %bitcast.76.refs_2_, ...), custom_call_target="tpu_custom_call" | custom-call | tf_op jit(solution)/shard_map/exchange/pallas_call | solution.py:661
  688.4 4.5 fusion.27
  692.9 39.3 %exchange.8 = (bf16[512,1024]{1,0:T(8,128)(2,1)}, bf16[512,1024]{1,0:T(8,128)(2,1)}, bf16[2048,2048]{1,0:T(8,128)(2,1)}, bf16[2048,2048]{1,0:T(8,128)(2,1)}) custom-call(bf16[512,1024]{1,0:T(8,128)(2,1)} %get-tuple-element.214.refs_0_, bf16[512,1024]{1,0:T(8,128)(2,1)} %get-tuple-element.213.refs_1_, ...), custom_call_target="tpu_custom_call" | custom-call | tf_op jit(solution)/shard_map/exchange/pallas_call | solution.py:661
  732.2 3.6 add_convert_fusion.8
  737.4 115.8 %exchange.9 = (bf16[4096,256]{1,0:T(8,128)(2,1)}, bf16[4,1024,512]{2,1,0:T(8,128)(2,1)}, bf16[4,1024,512]{2,1,0:T(8,128)(2,1)}, bf16[1664,2048]{1,0:T(8,128)(2,1)}) custom-call(bf16[512,2048]{1,0:T(8,128)(2,1)} %pad_maximum_fusion.13.refs_0_, bf16[2048,2048]{1,0:T(8,128)(2,1)} %get-tuple-element.90.refs_1_, bf16[2048,2048]{1,0:T(8,128)(2,1)} %get-tuple-element.91.refs_2_, ...), custom_call_target="tpu_custom_call" | custom-call | tf_op jit(solution)/shard_map/exchange/pallas_call | solution.py:661
  853.3 3.8 fusion.229
  867.0 3.6 fusion.24
  870.7 3.6 fusion.22
  878.7 85.7 %exchange.10 = (bf16[4,224,2048]{2,1,0:T(8,128)(2,1)}, bf16[4,3072,128]{2,1,0:T(8,128)(2,1)}, bf16[1024,512]{1,0:T(8,128)(2,1)}, bf16[1024,512]{1,0:T(8,128)(2,1...) custom-call(bf16[4,224,2048]{2,1,0:T(8,128)(2,1)} %add_convert_fusion.refs_0_, ...), custom_call_target="tpu_custom_call" | custom-call | tf_op jit(solution)/shard_map/exchange/pallas_call | solution.py:661
  976.6 45.7 %exchange.11 = (bf16[4,224,2048]{2,1,0:T(8,128)(2,1)}, bf16[256,4096]{1,0:T(8,128)(2,1)}) custom-call(bf16[224,2048]{1,0:T(8,128)(2,1)} %fusion.128.refs_0_, bf16[2048,512]{1,0:T(8,128)(2,1)} %pad_maximum_fusion.14.refs_1_), custom_call_target="tpu_custom_call" | custom-call | tf_op jit(solution)/shard_map/exchange/pallas_call | solution.py:661
  1026.7 4.6 convolution_convert_fusion.14
  1044.4 3.5 convolution_convert_fusion.7
  1048.0 4.0 convolution_convert_fusion.4
  1062.6 60.5 %exchange.12 = (bf16[4,896,128]{2,1,0:T(8,128)(2,1)}, bf16[4,224,2048]{2,1,0:T(8,128)(2,1)}, bf16[256,4096]{1,0:T(8,128)(2,1)}) custom-call(bf16[4,896,128]{2,1,0:T(8,128)(2,1)} %pad_maximum_fusion.18.refs_0_, bf16[4,224,2048]{2,1,0:T(8,128)(2,1)} %pad_maximum_fusion.2.refs_1_, bf16[2048,512]{1,0:T(8,128)(2,1)} %pad_maximum_fusion.15.refs_2_), custom_call_target="tpu_custom_call" | custom-call | tf_op jit(solution)/shard_map/exchange/pallas_call | solution.py:661
  1133.8 3.6 convolution_convert_fusion.6
  1167.0 3.5 fusion.59
  1170.5 3.7 add_convert_fusion.2.refs_1_
  1174.3 144.7 %exchange.13 = (bf16[8,384,128]{2,1,0:T(8,128)(2,1)}, bf16[4,384,1152]{2,1,0:T(8,128)(2,1)}, bf16[4,208,2048]{2,1,0:T(8,128)(2,1)}, bf16[4,208,2048]{2,1,0:T(8,1...) custom-call(bf16[8,384,128]{2,1,0:T(8,128)(2,1)} %bitcast.608, ...), custom_call_target="tpu_custom_call" | custom-call | tf_op jit(solution)/shard_map/exchange/pallas_call | solution.py:661
  1319.0 3.5 fusion.145
  (655 shorter events, 268.6 us)
Async XLA Ops:
  93.3 29.3 %copy-start.87 = (bf16[4,8,8,128]{3,1,2,0:T(8,128)(2,1)}, bf16[4,8,8,128]{3,1,2,0:T(8,128)(2,1)S(1)}, u32[]{:S(2)}) copy-start(bf16[4,8,8,128]{3,1,2,0:T(8,128)(2,1)S(1)} %copy.209) | copy-start | bytes 196612
  95.7 67.2 %copy-start.4 = (bf16[208,2048]{1,0:T(8,128)(2,1)}, bf16[208,2048]{1,0:T(8,128)(2,1)S(1)}, u32[]{:S(2)}) copy-start(bf16[208,2048]{1,0:T(8,128)(2,1)S(1)} %dynamic-slice_bitcast_fusion) | copy-start | bytes 2555908
  95.7 64.9 %collective-permute-start.3 = (bf16[208,2048]{1,0:T(8,128)(2,1)S(1)}, bf16[208,2048]{1,0:T(8,128)(2,1)}, u32[]{:S(2)}, u32[]{:S(2)}) collective-permute-start(bf16[208,2048]{1,0:T(8,128)(2,1)S(1)} %dynamic-slice_bitcast_fusion), channel_id=1, source_target_pairs={{0,24},{4,28},{8,0},{12,4},{16,8},{20,12},{24,16},{28,20},{1,25},{... | collective-permute-start | bytes 2555912 | tf_op jit(solution)/shard_map/ppermute | solution.py:57
  97.2 65.7 %collective-permute-start.4 = (bf16[208,2048]{1,0:T(8,128)(2,1)S(1)}, bf16[208,2048]{1,0:T(8,128)(2,1)}, u32[]{:S(2)}, u32[]{:S(2)}) collective-permute-start(bf16[208,2048]{1,0:T(8,128)(2,1)S(1)} %dynamic-slice_bitcast_fusion), channel_id=1, source_target_pairs={{0,16},{4,20},{8,24},{12,28},{16,0},{20,4},{24,8},{28,12},{1,17},{... | collective-permute-start | bytes 2555912 | tf_op jit(solution)/shard_map/ppermute | solution.py:57
  97.2 65.7 %collective-permute-start.5 = (bf16[208,2048]{1,0:T(8,128)(2,1)S(1)}, bf16[208,2048]{1,0:T(8,128)(2,1)}, u32[]{:S(2)}, u32[]{:S(2)}) collective-permute-start(bf16[208,2048]{1,0:T(8,128)(2,1)S(1)} %dynamic-slice_bitcast_fusion), channel_id=1, source_target_pairs={{0,8},{4,12},{8,16},{12,20},{16,24},{20,28},{24,0},{28,4},{1,9},{5... | collective-permute-start | bytes 2555912 | tf_op jit(solution)/shard_map/ppermute | solution.py:57
  110.2 13.5 copy-start.125
  115.3 16.3 %copy-start.13 = (bf16[1024,1024]{1,0:T(8,128)(2,1)}, bf16[1024,1024]{1,0:T(8,128)(2,1)S(1)}, u32[]{:S(2)}) copy-start(bf16[1024,1024]{1,0:T(8,128)(2,1)S(1)} %bitcast_dynamic-update-slice_fusion.12) | copy-start | bytes 6291460
  122.9 72.4 %copy-start.34 = (f32[64,1024]{1,0:T(8,128)}, f32[64,1024]{1,0:T(8,128)S(1)}, u32[]{:S(2)}) copy-start(f32[64,1024]{1,0:T(8,128)S(1)} %get-tuple-element.453) | copy-start | bytes 786436
  149.7 24.5 %collective-permute-start.2 = (bf16[1,224,2048]{2,1,0:T(8,128)(2,1)}, bf16[1,224,2048]{2,1,0:T(8,128)(2,1)}, u32[]{:S(2)}, u32[]{:S(2)}) collective-permute-start(bf16[1,224,2048]{2,1,0:T(8,128)(2,1)} %fusion.94), channel_id=1, source_target_pairs={{0,3},{1,2},{2,1},{3,0},{4,7},{5,6},{6,5},{7,4},{8,11},{9,10},{10,... | collective-permute-start | bytes 2752520 | tf_op jit(solution)/shard_map/ppermute | solution.py:47
  151.4 39.9 %collective-permute-start.1 = (bf16[1,224,2048]{2,1,0:T(8,128)(2,1)}, bf16[1,224,2048]{2,1,0:T(8,128)(2,1)}, u32[]{:S(2)}, u32[]{:S(2)}) collective-permute-start(bf16[1,224,2048]{2,1,0:T(8,128)(2,1)} %fusion.92), channel_id=1, source_target_pairs={{0,2},{1,3},{2,0},{3,1},{4,6},{5,7},{6,4},{7,5},{8,10},{9,11},{10,... | collective-permute-start | bytes 2752520 | tf_op jit(solution)/shard_map/ppermute | solution.py:47
  158.5 37.7 %copy-start.129 = (f32[1024]{0:T(1024)}, f32[1024]{0:T(1024)S(1)}, u32[]{:S(2)}) copy-start(f32[1024]{0:T(1024)S(1)} %fusion.194) | copy-start | bytes 12292
  158.5 37.7 %copy-start.113 = (f32[1,2,8,128]{3,1,2,0:T(2,128)}, f32[1,2,8,128]{3,1,2,0:T(2,128)S(1)}, u32[]{:S(2)}) copy-start(f32[1,2,8,128]{3,1,2,0:T(2,128)S(1)} %copy.162) | copy-start | bytes 24580
  160.6 30.8 %collective-permute-start = (bf16[1,224,2048]{2,1,0:T(8,128)(2,1)S(1)}, bf16[1,224,2048]{2,1,0:T(8,128)(2,1)S(1)}, u32[]{:S(2)}, u32[]{:S(2)}) collective-permute-start(bf16[1,224,2048]{2,1,0:T(8,128)(2,1)S(1)} %fusion.90), channel_id=1, source_target_pairs={{0,1},{1,0},{2,3},{3,2},{4,5},{5,4},{6,7},{7,6},{8,9},{9,8},{10,11... | collective-permute-start | bytes 2752520 | tf_op jit(solution)/shard_map/ppermute | solution.py:47
  166.1 425.0 %collective-permute-start.6 = (bf16[4,208,2048]{2,1,0:T(8,128)(2,1)}, bf16[4,208,2048]{2,1,0:T(8,128)(2,1)}, u32[]{:S(2)}, u32[]{:S(2)}) collective-permute-start(bf16[4,208,2048]{2,1,0:T(8,128)(2,1)} %pad_maximum_fusion.4), channel_id=1, source_target_pairs={{0,4},{4,0},{8,12},{12,8},{16,20},{20,16},{24,28},{28,24},{1,5},{5... | collective-permute-start | bytes 10223624 | tf_op jit(solution)/shard_map/ppermute | solution.py:52
  168.3 23.1 %copy-start.43 = (bf16[1,208,2048]{2,1,0:T(8,128)(2,1)S(1)}, bf16[1,208,2048]{2,1,0:T(8,128)(2,1)}, u32[]{:S(2)}) copy-start(bf16[1,208,2048]{2,1,0:T(8,128)(2,1)} %get-tuple-element.256) | copy-start | bytes 2555908
  195.3 390.8 %copy-start.141 = (f32[208]{0:T(256)}, f32[208]{0:T(256)S(1)}, u32[]{:S(2)}) copy-start(f32[208]{0:T(256)S(1)} %get-tuple-element.223) | copy-start | bytes 2500
  195.5 395.1 %copy-start.155 = (f32[16]{0:T(128)}, f32[16]{0:T(128)S(1)}, u32[]{:S(2)}) copy-start(f32[16]{0:T(128)S(1)} %get-tuple-element.400) | copy-start | bytes 196
  495.3 15.8 %slice-start = ((s8[7340032]{0:T(1024)(128)(4,1)}), s8[3145728]{0:T(1024)(128)(4,1)S(1)}, s32[]{:S(2)}) async-start(s8[7340032]{0:T(1024)(128)(4,1)} %bitcast.594), calls=%async_computation | async-start | bytes 6291456
  505.7 10.3 copy-start.123
  585.2 30.4 %collective-permute-start.7 = (bf16[4,224,2048]{2,1,0:T(8,128)(2,1)S(1)}, bf16[4,224,2048]{2,1,0:T(8,128)(2,1)S(1)}, u32[]{:S(2)}, u32[]{:S(2)}) collective-permute-start(bf16[4,224,2048]{2,1,0:T(8,128)(2,1)S(1)} %pad_maximum_fusion), channel_id=1, source_target_pairs={{0,4},{4,0},{8,12},{12,8},{16,20},{20,16},{24,28},{28,24},{1,5},{5... | collective-permute-start | bytes 11010056 | tf_op jit(solution)/shard_map/ppermute | solution.py:52
  692.9 39.3 %copy-start.29 = (bf16[4,512,1024]{2,1,0:T(8,128)(2,1)S(1)}, bf16[4,512,1024]{2,1,0:T(8,128)(2,1)}, u32[]{:S(2)}) copy-start(bf16[4,512,1024]{2,1,0:T(8,128)(2,1)} %get-tuple-element.85) | copy-start | bytes 12582916
  858.6 17.5 %collective-permute-start.8 = (bf16[4,224,2048]{2,1,0:T(8,128)(2,1)S(1)}, bf16[4,224,2048]{2,1,0:T(8,128)(2,1)S(1)}, u32[]{:S(2)}, u32[]{:S(2)}) collective-permute-start(bf16[4,224,2048]{2,1,0:T(8,128)(2,1)S(1)} %pad_maximum_fusion.1), channel_id=1, source_target_pairs={{0,4},{4,0},{8,12},{12,8},{16,20},{20,16},{24,28},{28,24},{1,5},{5... | collective-permute-start | bytes 11010056 | tf_op jit(solution)/shard_map/ppermute | solution.py:52
  876.1 93.7 %copy-start.20 = (f32[1,224,2048]{2,1,0:T(8,128)}, f32[1,224,2048]{2,1,0:T(8,128)S(1)}, u32[]{:S(2)}) copy-start(f32[1,224,2048]{2,1,0:T(8,128)S(1)} %convert_add_fusion.15) | copy-start | bytes 5505028
  969.7 55.7 %copy-start.36 = (bf16[208,2048]{1,0:T(8,128)(2,1)}, bf16[208,2048]{1,0:T(8,128)(2,1)S(1)}, u32[]{:S(2)}) copy-start(bf16[208,2048]{1,0:T(8,128)(2,1)S(1)} %fusion.224) | copy-start | bytes 2555908
  970.7 60.6 %copy-start.89 = (bf16[16,1024]{1,0:T(8,128)(2,1)}, bf16[16,1024]{1,0:T(8,128)(2,1)S(1)}, u32[]{:S(2)}) copy-start(bf16[16,1024]{1,0:T(8,128)(2,1)S(1)} %get-tuple-element.194) | copy-start | bytes 98308
  1133.8 19.1 %copy-start.7 = (f32[224,2048]{1,0:T(8,128)}, f32[224,2048]{1,0:T(8,128)S(1)}, u32[]{:S(2)}) copy-start(f32[224,2048]{1,0:T(8,128)S(1)} %convert_add_fusion.12) | copy-start | bytes 5505028
  1145.5 25.1 %collective-permute-start.9 = (bf16[4,384,1152]{2,1,0:T(8,128)(2,1)}, bf16[4,384,1152]{2,1,0:T(8,128)(2,1)}, u32[]{:S(2)}, u32[]{:S(2)}) collective-permute-start(bf16[4,384,1152]{2,1,0:T(8,128)(2,1)} %pad_maximum_fusion.3), channel_id=1, source_target_pairs={{0,4},{4,0},{8,12},{12,8},{16,20},{20,16},{24,28},{28,24},{1,5},{5... | collective-permute-start | bytes 10616840 | tf_op jit(solution)/shard_map/ppermute | solution.py:52
  1174.3 144.7 %copy-start.12 = (bf16[208,2048]{1,0:T(8,128)(2,1)S(1)}, bf16[208,2048]{1,0:T(8,128)(2,1)}, u32[]{:S(2)}) copy-start(bf16[208,2048]{1,0:T(8,128)(2,1)} %get-tuple-element.304.refs_3_) | copy-start | bytes 2555908
  1330.7 37.3 %collective-permute-start.10 = (bf16[384,128]{1,0:T(8,128)(2,1)}, bf16[384,128]{1,0:T(8,128)(2,1)}, u32[]{:S(2)}, u32[]{:S(2)}) collective-permute-start(bf16[384,128]{1,0:T(8,128)(2,1)} %concatenate.368), channel_id=1, source_target_pairs={{0,3},{1,2},{2,1},{3,0},{4,7},{5,6},{6,5},{7,4},{8,11},{9,10},{10,... | collective-permute-start | bytes 294920 | tf_op jit(solution)/shard_map/ppermute | solution.py:47
  1332.2 35.9 %collective-permute-start.11 = (bf16[384,128]{1,0:T(8,128)(2,1)}, bf16[384,128]{1,0:T(8,128)(2,1)}, u32[]{:S(2)}, u32[]{:S(2)}) collective-permute-start(bf16[384,128]{1,0:T(8,128)(2,1)} %concatenate.368), channel_id=1, source_target_pairs={{0,2},{1,3},{2,0},{3,1},{4,6},{5,7},{6,4},{7,5},{8,10},{9,11},{10,... | collective-permute-start | bytes 294920 | tf_op jit(solution)/shard_map/ppermute | solution.py:47
  1333.5 34.5 %collective-permute-start.12 = (bf16[384,128]{1,0:T(8,128)(2,1)}, bf16[384,128]{1,0:T(8,128)(2,1)}, u32[]{:S(2)}, u32[]{:S(2)}) collective-permute-start(bf16[384,128]{1,0:T(8,128)(2,1)} %concatenate.368), channel_id=1, source_target_pairs={{0,1},{1,0},{2,3},{3,2},{4,5},{5,4},{6,7},{7,6},{8,9},{9,8},{10,11... | collective-permute-start | bytes 294920 | tf_op jit(solution)/shard_map/ppermute | solution.py:47
  1349.0 9.2 copy-start.153
  (146 other events, 403.3 us)

commit v3 on v0

v3 whole, which is shorter than its diff:
```python
import functools

import jax
import jax.numpy as jnp
from jax import lax
from jax.experimental import pallas as pl
from jax.experimental.pallas import tpu as pltpu
from jax.sharding import PartitionSpec as P

HD = 256
EPS = 1e-06
BF = jnp.bfloat16
F32 = jnp.float32
MESH = pl.DeviceIdType.MESH
HBM = pl.BlockSpec(memory_space=pl.ANY)


def rms_gain(values, gain):
    return values * lax.rsqrt(jnp.mean(values * values, axis=-1, keepdims=True) + EPS) * gain


def norm_backward(values, gain, grad_out):
    unused, pull = jax.vjp(rms_gain, values, gain)
    return pull(grad_out)


def glu_value(gate, upward):
    return jax.nn.gelu(gate, approximate=True) * upward


def glu_backward(gate, upward, grad):
    unused, pull = jax.vjp(glu_value, gate, upward)
    return pull(grad)


def dot_plain(left, right):
    return jnp.dot(left, right, preferred_element_type=F32)


def dot_left(left, right):
    return lax.dot_general(left, right, (((0,), (0,)), ((), ())), preferred_element_type=F32)


def dot_right(left, right):
    return lax.dot_general(left, right, (((1,), (1,)), ((), ())), preferred_element_type=F32)


def round_up(value, step):
    return -(-value // step) * step


def add(left, right):
    return (left.astype(F32) + right.astype(F32)).astype(BF)


def greet(devices):
    barrier = pltpu.get_barrier_semaphore()
    for device in devices:
        pl.semaphore_signal(barrier, inc=1, device_id=device, device_id_type=MESH)
    pl.semaphore_wait(barrier, len(devices))


def at(start, size):
    return pl.ds(pl.multiple_of(start * size, size), size)


class Place:
    def __init__(self, n, m, sent, arrived, row):
        self.n, self.m = n, m
        self.me, self.col = lax.axis_index("dp"), lax.axis_index("mp")
        self.sent, self.arrived, self.row = sent, arrived, row

    def remote(self, src, dst, slot, device):
        return pltpu.make_async_remote_copy(
            src_ref=src,
            dst_ref=dst,
            send_sem=self.sent.at[self.row, slot],
            recv_sem=self.arrived.at[self.row, slot],
            device_id=device,
            device_id_type=MESH,
        )

    def keep(self, src, dst):
        def scoped(buffer):
            pltpu.sync_copy(src, buffer)
            pltpu.sync_copy(buffer, dst)

        pl.run_scoped(scoped, pltpu.VMEM(src.shape, src.dtype))

    def over_dp(self, s):
        return (lax.rem(self.me + s, self.n), self.col)

    def over_mp(self, k):
        return (self.me, self.col ^ k)


def loop(first, last, body):
    lax.fori_loop(first, last, lambda s, carry: (body(s), carry)[1], 0)


class Flow:
    reach = "dp"
    kept = False

    def result(self, shape, n, m):
        return shape

    def each(self, p, src, dst, do):
        pass

    def own(self, p, src, dst):
        return None

    def start(self, p, src, dst):
        self.each(p, src, dst, lambda c: c.start())
        if self.kept:
            p.keep(*self.own(p, src, dst))

    def relay(self, p, src, dst, k):
        return None

    def wait(self, p, src, dst):
        self.each(p, src, dst, lambda c: c.wait())


class Rows(Flow):
    kept = True

    def result(self, shape, n, m):
        return (shape[0] // n, shape[1] * n)

    def own(self, p, src, dst):
        return src.at[at(p.me, src.shape[0] // p.n)], dst.at[:, at(p.me, dst.shape[1] // p.n)]

    def each(self, p, src, dst, do):
        def body(s):
            target = p.over_dp(s)
            block = src.at[at(target[0], src.shape[0] // p.n)]
            do(p.remote(block, dst.at[:, at(p.me, dst.shape[1] // p.n)], s, target))

        loop(1, p.n, body)


class Columns(Flow):
    kept = True

    def result(self, shape, n, m):
        return (shape[0] * n, shape[1] // n)

    def own(self, p, src, dst):
        return src.at[:, at(p.me, src.shape[1] // p.n)], dst.at[at(p.me, dst.shape[0] // p.n)]

    def each(self, p, src, dst, do):
        def body(s):
            target = p.over_dp(s)
            block = src.at[:, at(target[0], src.shape[1] // p.n)]
            do(p.remote(block, dst.at[at(p.me, dst.shape[0] // p.n)], s, target))

        loop(1, p.n, body)


class Each(Flow):
    kept = True

    def own(self, p, src, dst):
        return src.at[p.me], dst.at[p.me]

    def each(self, p, src, dst, do):
        def body(s):
            target = p.over_dp(s)
            do(p.remote(src.at[target[0]], dst.at[p.me], s, target))

        loop(1, p.n, body)


class Chips(Flow):
    def each(self, p, src, dst, do):
        loop(1, p.n // 2, lambda s: do(p.remote(src.at[s], dst.at[s], s, p.over_dp(2 * s))))


class Core(Flow):
    def result(self, shape, n, m):
        return (shape[0] // 2, shape[1])

    def each(self, p, src, dst, do):
        half = src.shape[0] // 2
        do(p.remote(src.at[pl.ds(half, half)], dst, 0, (p.me ^ 1, p.col)))


class CoreRows(Flow):
    axis = 0

    def result(self, shape, n, m):
        return (shape[0] // 2, shape[1]) if self.axis == 0 else (shape[0], shape[1] // 2)

    def cut(self, ref, i, count):
        size = ref.shape[self.axis] // count
        return ref.at[at(i, size)] if self.axis == 0 else ref.at[:, at(i, size)]

    def each(self, p, src, dst, do):
        def body(c):
            block = self.cut(src, 2 * c + lax.rem(p.me + 1, 2), p.n)
            do(p.remote(block, self.cut(dst, c, p.n // 2), c, (p.me ^ 1, p.col)))

        loop(0, p.n // 2, body)


class CoreColumns(CoreRows):
    axis = 1


class ChipRows(CoreRows):
    def result(self, shape, n, m):
        if self.axis == 0:
            return (n // 2, shape[0] // (n // 2), shape[1])
        return (n // 2, shape[0], shape[1] // (n // 2))

    def each(self, p, src, dst, do):
        def body(s):
            target = p.over_dp(2 * s)
            do(p.remote(self.cut(src, target[0] // 2, p.n // 2), dst.at[s], s, target))

        loop(1, p.n // 2, body)


class ChipColumns(ChipRows):
    axis = 1


class Line(Flow):
    def __init__(self, place=None, result=None, share=False):
        self.place = place or Line.in_turn
        self.shape = result
        self.share = share
        self.reach = "both" if share else "dp"

    def in_turn(ref, i, j):
        chips = lax.axis_size("dp") // 2
        chip = lax.rem(i // 2 - j // 2 + chips, chips)
        return ref.at[chip + chips * lax.rem(i + j, 2)]

    def result(self, shape, n, m):
        return self.shape or (n,) + shape

    def origin(self, p, first, way, k):
        return lax.rem(first - (2, -2)[way] * k + 2 * p.n, p.n)

    def along(self, p, src, dst, way, k):
        i = self.origin(p, p.me, way, k - 1)
        target = lax.rem(p.me + (2, -2)[way] + p.n, p.n)
        source = src if k == 1 else self.place(dst, i, p.me)
        slot = way * p.n // 2 + k
        return p.remote(source, self.place(dst, i, target), slot, (target, p.col))

    def across(self, p, src, dst, way, k):
        i = self.origin(p, p.me, way, k)
        source = src if k == 0 else self.place(dst, i, p.me)
        slot = (2 + way) * p.n // 2 + k
        return p.remote(source, self.place(dst, i, p.me ^ 1), slot, (p.me ^ 1, p.col))

    def passed(self, p, dst, i, k, source=None):
        block = self.place(dst, i, p.me)
        source = block if source is None else source
        return p.remote(source, block, 2 * p.n + i * p.m + k, p.over_mp(k))

    def receives(self, p, way, k):
        chip = p.me // 2
        if k == 0:
            return chip >= 0
        return chip >= k if way == 0 else chip < p.n // 2 - k

    def sends(self, p, way, k):
        chip = p.me // 2
        beyond = chip < p.n // 2 - 1 if way == 0 else chip > 0
        return beyond & self.receives(p, way, k - 1)

    def start(self, p, src, dst):
        for way in (0, 1):
            pl.when(self.sends(p, way, 1))(self.along(p, src, dst, way, 1).start)
        self.across(p, src, dst, 0, 0).start()
        self.hand(p, dst, p.me, src)
        p.keep(src, self.place(dst, p.me, p.me))

    def hand(self, p, dst, i, source=None):
        if self.share:
            for k in range(1, p.m):
                self.passed(p, dst, i, k, source).start()

    def crossed(self, p, src, dst, way, k):
        self.across(p, src, dst, way, k).wait_recv()
        self.hand(p, dst, self.origin(p, p.me ^ 1, way, k))

    def relay(self, p, src, dst, k):
        if k == 1:
            self.crossed(p, src, dst, 0, 0)
        for way in (0, 1):

            @pl.when(self.receives(p, way, k))
            def _(way=way):
                self.along(p, src, dst, way, k).wait_recv()
                self.across(p, src, dst, way, k).start()
                self.hand(p, dst, self.origin(p, p.me, way, k))

            if k < p.n // 2 - 1:
                pl.when(self.sends(p, way, k + 1))(self.along(p, src, dst, way, k + 1).start)
            if k > 1:
                before = functools.partial(self.crossed, p, src, dst, way, k - 1)
                pl.when(self.receives(p, way, k - 1))(before)

    def wait(self, p, src, dst):
        last = p.n // 2 - 1
        for way in (0, 1):
            end = functools.partial(self.crossed, p, src, dst, way, last)
            pl.when(self.receives(p, way, last))(end)
        self.across(p, src, dst, 0, 0).wait_send()
        for way in (0, 1):
            for k in range(1, last + 1):
                pl.when(self.sends(p, way, k))(self.along(p, src, dst, way, k).wait_send)
                pl.when(self.receives(p, way, k))(self.across(p, src, dst, way, k).wait_send)
        if self.share:
            for k in range(1, p.m):
                loop(0, p.n, lambda i, k=k: self.passed(p, dst, i, k).wait())


class Pass(Flow):
    reach = "mp"
    kept = True
    parts = 8

    def __init__(self, axis):
        self.axis = axis

    def result(self, shape, n, m):
        return (shape[0], m * shape[1]) if self.axis else (m * shape[0], shape[1])

    def spot(self, p, src, dst, k, c=None):
        rows, width = src.shape
        first, count = (0, rows) if c is None else (c * (rows // self.parts), rows // self.parts)
        if self.axis:
            return dst.at[pl.ds(first, count), pl.ds(k * width, width)]
        return dst.at[pl.ds(k * rows + first, count)]

    def own(self, p, src, dst):
        return src, self.spot(p, src, dst, 0)

    def direct(self, p, src, dst, k, c):
        few = src.shape[0] // self.parts
        block = src.at[pl.ds(c * few, few)]
        slot = k * self.parts + c
        return p.remote(block, self.spot(p, src, dst, k, c), slot, p.over_mp(k))

    def turned(self, p, src, dst, c):
        via = 1 + c % 2
        source = self.spot(p, src, dst, via, c)
        slot = 3 * self.parts + c
        return p.remote(source, self.spot(p, src, dst, 3, c), slot, p.over_mp(3 - via))

    def each(self, p, src, dst, do):
        for c in range(self.parts):
            for k in range(1, 3 if p.m == 4 else p.m):
                do(self.direct(p, src, dst, k, c))

    def start(self, p, src, dst):
        self.each(p, src, dst, lambda c: c.start())

    def relay(self, p, src, dst, k):
        if p.m == 4:
            for c in range((k - 1) * self.parts // 2, k * self.parts // 2):
                self.direct(p, src, dst, 1 + c % 2, c).wait_recv()
                self.turned(p, src, dst, c).start()

    def wait(self, p, src, dst):
        p.keep(*self.own(p, src, dst))
        for c in range(self.parts):
            for k in range(1, 3 if p.m == 4 else p.m):
                copy = self.direct(p, src, dst, k, c)
                (copy.wait_send if p.m == 4 and k == 1 + c % 2 else copy.wait)()
            if p.m == 4:
                self.turned(p, src, dst, c).wait()


class Parts(Flow):
    reach = "mp"

    def result(self, shape, n, m):
        return shape if len(shape) == 3 else (m, shape[0] // m, shape[1])

    def each(self, p, src, dst, do):
        for k in range(1, p.m):
            target = p.over_mp(k)
            if len(src.shape) == 3:
                block = src.at[target[1]]
            else:
                block = src.at[at(target[1], src.shape[0] // p.m)]
            do(p.remote(block, dst.at[k], k, target))


class Swaps(Parts):
    def each(self, p, src, dst, do):
        for k in range(1, p.m):
            do(p.remote(src.at[k], dst.at[k], k, p.over_mp(k)))


class Whole(Flow):
    reach = "mp"
    kept = True

    def result(self, shape, n, m):
        return (m * shape[0], shape[1])

    def own(self, p, src, dst):
        return src, dst.at[at(p.col, src.shape[0])]

    def each(self, p, src, dst, do):
        for k in range(1, p.m):
            do(p.remote(src, dst.at[at(p.col, src.shape[0])], k, p.over_mp(k)))


class Swap(Flow):
    reach = "mp"

    def __init__(self, k):
        self.k = k

    def each(self, p, src, dst, do):
        do(p.remote(src, dst, 0, p.over_mp(self.k)))


class First(Flow):
    reach = "mp"

    def __init__(self, axis):
        self.axis = axis

    def result(self, shape, n, m):
        if self.axis:
            return (4, shape[0] // 2, shape[1] // m)
        return (4, shape[0] // m, shape[1] // 2)

    def each(self, p, src, dst, do):
        width, deep = src.shape[self.axis] // p.m, src.shape[1 - self.axis] // 2
        for k, part in enumerate((1, 3, 2, 3)):
            block, half = pl.ds(part * width, width), pl.ds(k // 2 * deep, deep)
            source = src.at[half, block] if self.axis else src.at[block, half]
            do(p.remote(source, dst.at[k], k, p.over_mp(1 + k // 2)))


class World(Flow):
    reach = "world"
    kept = True

    def result(self, shape, n, m):
        return (n, m) + shape

    def block(self, src, i):
        return src

    def own(self, p, src, dst):
        return self.block(src, p.me), dst.at[p.me, p.col]

    def each(self, p, src, dst, do):
        for k in range(p.m):

            def body(s, k=k):
                target = (lax.rem(p.me + s, p.n), p.col ^ k)
                copy = p.remote(
                    self.block(src, target[0]), dst.at[p.me, p.col], s * p.m + k, target
                )
                do(copy)

            loop(0 if k else 1, p.n, body)


class Spread(World):
    def result(self, shape, n, m):
        return (n, m) + shape[1:]

    def block(self, src, i):
        return src.at[i]


class Kernel:
    def __init__(self, collective_id):
        self.collective_id = collective_id
        self.inputs, self.outputs, self.flows, self.steps = [], [], [], []

    def operand(self, source):
        if isinstance(source, int):
            return ("out", source)
        self.inputs.append(source)
        return ("in", len(self.inputs) - 1)

    def shape_of(self, source):
        return self.outputs[source] if isinstance(source, int) else source

    def new_output(self, shape, dtype):
        self.outputs.append(jax.ShapeDtypeStruct(shape, dtype))
        return len(self.outputs) - 1

    def flow(self, kind, source, now=True, into=None):
        n, m = lax.axis_size("dp"), lax.axis_size("mp")
        like = self.shape_of(source)
        out = into
        if into is None:
            out = self.new_output(kind.result(like.shape, n, m), like.dtype)
        name = out if into is None else -1 - len(self.flows)
        self.flows.append((kind, self.operand(source), out, name))
        if now:
            self.go(name)
        return name

    def go(self, name):
        self.steps.append(("start", name))

    def relay(self, name, k):
        self.steps.append(("relay", name, k))

    def ready(self, name):
        self.steps.append(("wait", name))

    def job(self, body, sources, shapes, dtype=BF, into=None):
        outs = into or [self.new_output(s, dtype) for s in shapes]
        self.steps.append(("job", body, [self.operand(s) for s in sources], outs))
        return outs if len(outs) > 1 else outs[0]

    def call(self, name):
        n, m = lax.axis_size("dp"), lax.axis_size("mp")
        takes, gives = len(self.inputs), len(self.outputs)
        flows, steps = self.flows, self.steps
        count = max(len(flows), 1)
        rows = {flow[3]: row for row, flow in enumerate(flows)}
        reach = {flow[0].reach for flow in flows}
        slots = max(2 * n + n * m, 4 * Pass.parts, Pass.parts * m)

        def kernel(*refs):
            ins, outs = refs[:takes], refs[takes : takes + gives]
            sent, arrived = refs[takes + gives :]
            me, col = lax.axis_index("dp"), lax.axis_index("mp")
            if "world" in reach:
                greet([(lax.rem(me + s, n), col ^ k) for s in range(n) for k in range(m) if s or k])
            else:
                column = [(lax.rem(me + s, n), col) for s in range(1, n)]
                row = [(me, col ^ k) for k in range(1, m)]
                greet(
                    (column if reach & {"dp", "both"} else [])
                    + (row if reach & {"mp", "both"} else [])
                )

            def ref(operand):
                return (ins if operand[0] == "in" else outs)[operand[1]]

            def act(what, name, *rest):
                kind, source, out, unused = flows[rows[name]]
                place = Place(n, m, sent, arrived, rows[name])
                getattr(kind, what)(place, ref(source), outs[out], *rest)

            ended = set()
            for step in steps:
                if step[0] == "job":
                    step[1]([ref(s) for s in step[2]], [outs[o] for o in step[3]])
                else:
                    act(*step)
                    if step[0] == "wait":
                        ended.add(step[1])
            for flow in flows:
                if flow[3] not in ended:
                    act("wait", flow[3])

        return pl.pallas_call(
            kernel,
            out_shape=self.outputs,
            in_specs=[HBM] * takes,
            out_specs=[HBM] * gives,
            scratch_shapes=[
                pltpu.SemaphoreType.DMA((count, slots)),
                pltpu.SemaphoreType.DMA((count, slots)),
            ],
            compiler_params=pltpu.CompilerParams(
                collective_id=self.collective_id,
                has_side_effects=True,
                vmem_limit_bytes=56 << 20,
            ),
            name=name,
        )(*self.inputs)


def tile(size, most):
    return max(t for t in range(16, most + 1, 16) if size % t == 0)


def products_plain(inputs, outputs):
    a, b = inputs
    (rows, depth), width = a.shape, b.shape[1]
    bm, bn = tile(rows, 416), tile(width, 512)

    def body(a_ref, b_ref, o_ref):
        o_ref[...] = dot_plain(a_ref[...], b_ref[...]).astype(BF)

    pltpu.emit_pipeline(
        body,
        grid=(width // bn, rows // bm),
        in_specs=[
            pl.BlockSpec((bm, depth), lambda j, i: (i, 0)),
            pl.BlockSpec((depth, bn), lambda j, i: (0, j)),
        ],
        out_specs=[pl.BlockSpec((bm, bn), lambda j, i: (i, j))],
    )(a, b, outputs[0])


def products_right(inputs, outputs):
    pairs = len(inputs) // 2
    rows, width = inputs[0].shape[0], inputs[1].shape[0]
    bm, bn = tile(rows, 416), tile(width, 512)

    def body(*refs):
        total = dot_right(refs[0][...], refs[1][...])
        for p in range(1, pairs):
            total = total + dot_right(refs[2 * p][...], refs[2 * p + 1][...])
        refs[-1][...] = total.astype(BF)

    specs = []
    for p in range(pairs):
        depth = inputs[2 * p].shape[1]
        specs.append(pl.BlockSpec((bm, depth), lambda j, i: (i, 0)))
        specs.append(pl.BlockSpec((bn, depth), lambda j, i: (j, 0)))
    pltpu.emit_pipeline(
        body,
        grid=(width // bn, rows // bm),
        in_specs=specs,
        out_specs=[pl.BlockSpec((bm, bn), lambda j, i: (i, j))],
    )(*inputs, outputs[0])


def products_left(inputs, outputs):
    a, rest = inputs[0], inputs[1:]
    (depth, rows), width = a.shape, rest[0].shape[1]
    bm, bn = tile(rows, 1024), tile(width, 512)
    count = len(rest)

    def body(a_ref, *refs):
        for p in range(count):
            refs[count + p][...] = dot_left(a_ref[...], refs[p][...]).astype(BF)

    pltpu.emit_pipeline(
        body,
        grid=(rows // bm, width // bn),
        in_specs=[pl.BlockSpec((depth, bm), lambda i, j: (0, i))]
        + [pl.BlockSpec((depth, bn), lambda i, j: (0, j))] * count,
        out_specs=[pl.BlockSpec((bm, bn), lambda i, j: (i, j))] * count,
    )(a, *rest, *outputs)


def hidden_forward(part, parts, inputs, outputs):
    h, w_gate, w_up = inputs
    (rows, depth), width = h.shape, w_gate.shape[1] // parts
    cut = pl.ds(part * width, width)
    w_gate, w_up = w_gate.at[:, cut], w_up.at[:, cut]
    outputs = [o.at[:, cut] for o in outputs]
    bm, bn = tile(rows, 416), tile(width, 512)

    def body(h_ref, gate_w, up_w, gate_ref, up_ref, hidden_ref):
        gate = dot_plain(h_ref[...], gate_w[...])
        upward = dot_plain(h_ref[...], up_w[...])
        gate_ref[...] = gate.astype(BF)
        up_ref[...] = upward.astype(BF)
        hidden_ref[...] = glu_value(gate, upward).astype(BF)

    block = pl.BlockSpec((bm, bn), lambda j, i: (i, j))
    pltpu.emit_pipeline(
        body,
        grid=(width // bn, rows // bm),
        in_specs=[pl.BlockSpec((bm, depth), lambda j, i: (i, 0))]
        + [pl.BlockSpec((depth, bn), lambda j, i: (0, j))] * 2,
        out_specs=[block] * 3,
    )(h, w_gate, w_up, *outputs)


def hidden_backward(inputs, outputs):
    gz, w_down, gate, upward = inputs
    (rows, depth), width = gz.shape, w_down.shape[0]
    bm, bn = tile(rows, 416), tile(width, 512)

    def body(gz_ref, down_w, gate_ref, up_ref, dgate_ref, dup_ref):
        grad = dot_right(gz_ref[...], down_w[...])
        dgate, dup = glu_backward(gate_ref[...].astype(F32), up_ref[...].astype(F32), grad)
        dgate_ref[...] = dgate.astype(BF)
        dup_ref[...] = dup.astype(BF)

    block = pl.BlockSpec((bm, bn), lambda j, i: (i, j))
    pltpu.emit_pipeline(
        body,
        grid=(width // bn, rows // bm),
        in_specs=[
            pl.BlockSpec((bm, depth), lambda j, i: (i, 0)),
            pl.BlockSpec((bn, depth), lambda j, i: (j, 0)),
            block,
            block,
        ],
        out_specs=[block] * 2,
    )(gz, w_down, gate, upward, *outputs)


def attend_forward(inputs, outputs):
    query, keys, values, seg_q, seg_k = inputs
    probs, mixed = outputs
    total = query.shape[0]
    rows = tile(total, 448)

    def body(q_ref, k_ref, v_ref, sq_ref, sk_ref, p_ref, o_ref):
        allowed = sq_ref[:, :1] >= sk_ref[:1]
        scores = dot_right(q_ref[...], k_ref[...]) * HD ** (-0.5)
        scores = jnp.where(allowed, scores, -1e30)
        raised = jnp.exp(scores - jnp.max(scores, axis=-1, keepdims=True))
        p = (raised / jnp.sum(raised, axis=-1, keepdims=True)).astype(BF)
        p_ref[...] = p
        o_ref[...] = dot_plain(p, v_ref[...]).astype(BF)

    def rest(shape):
        return pl.BlockSpec(shape, lambda i: (0, 0))

    pltpu.emit_pipeline(
        body,
        grid=(total // rows,),
        in_specs=[
            pl.BlockSpec((rows, HD), lambda i: (i, 0)),
            rest(keys.shape),
            rest(values.shape),
            pl.BlockSpec((rows, seg_q.shape[1]), lambda i: (i, 0)),
            rest(seg_k.shape),
        ],
        out_specs=[
            pl.BlockSpec((rows, total), lambda i: (i, 0)),
            pl.BlockSpec((rows, HD), lambda i: (i, 0)),
        ],
    )(query, keys, values, seg_q, seg_k, probs, mixed)


def attend_backward(heads, inputs, outputs):
    probs, query = inputs[:heads], inputs[heads : 2 * heads]
    keys, values, grad = inputs[2 * heads :]
    grad_query, (both, shares) = outputs[:heads], outputs[heads:]
    total, scale = keys.shape[0], HD ** (-0.5)
    rows = tile(total, 448)
    width = shares.shape[2]

    def scoped(sums, rounded, parted):
        sums[...] = jnp.zeros_like(sums)

        def body(*refs):
            k_ref, v_ref, g_ref = refs[2 * heads : 2 * heads + 3]
            for h in range(heads):
                g = g_ref[:, h * HD : (h + 1) * HD]
                p, q = refs[h][...], refs[heads + h][...]
                wide_p = p.astype(F32)
                dp = dot_right(g, v_ref[...])
                ds = wide_p * (dp - jnp.sum(wide_p * dp, axis=-1, keepdims=True))
                ds = ds.astype(BF)
                refs[2 * heads + 3 + h][...] = (dot_plain(ds, k_ref[...]) * scale).astype(BF)
                sums[:, :HD] += dot_left(ds, q) * scale
                sums[:, HD:] += dot_left(p, g)

        def rest(ref):
            return pl.BlockSpec(ref.shape, lambda i: (0, 0))

        block = pl.BlockSpec((rows, HD), lambda i: (i, 0))
        pltpu.emit_pipeline(
            body,
            grid=(total // rows,),
            in_specs=[pl.BlockSpec((rows, total), lambda i: (i, 0))] * heads
            + [block] * heads
            + [rest(keys), rest(values), pl.BlockSpec((rows, heads * HD), lambda i: (i, 0))],
            out_specs=[block] * heads,
        )(*probs, *query, keys, values, grad, *grad_query)
        rounded[...] = sums[...].astype(BF)
        for k in range(shares.shape[0]):
            parted[k] = sums[:, k * width : (k + 1) * width].astype(BF)
        pltpu.sync_copy(rounded, both)
        pltpu.sync_copy(parted, shares)

    pl.run_scoped(
        scoped,
        pltpu.VMEM((total, 2 * HD), F32),
        pltpu.VMEM((total, 2 * HD), BF),
        pltpu.VMEM(shares.shape, BF),
    )


def rows_from(first, count, body):
    return lambda inputs, outputs: body([inputs[0].at[pl.ds(first, count)]] + inputs[1:], outputs)


class Halves:
    def __init__(self, whole, axis):
        self.whole, self.axis = whole, axis

    def take(self, got):
        top, low = jnp.split(self.whole, 2, axis=1 - self.axis)
        t, b = jnp.split(top, 4, axis=self.axis), jnp.split(low, 4, axis=self.axis)
        self.top, self.next_y = add(t[0], got[0]), add(t[2], got[1])
        self.low, self.next_x = add(b[0], got[2]), add(b[1], got[3])

    def second(self, kernel):
        self.from_y = kernel.flow(Swap(2), self.next_y)
        self.from_x = kernel.flow(Swap(1), self.next_x)

    def total(self, got):
        return jnp.concatenate(
            [add(self.top, got[self.from_y]), add(self.low, got[self.from_x])], axis=1 - self.axis
        )


class Direct:
    def __init__(self, whole, axis):
        parts = jnp.split(whole, lax.axis_size("mp"), axis=axis)
        total = parts[0].astype(F32)
        for k in range(1, len(parts)):
            pairs = [(i, i ^ k) for i in range(len(parts))]
            total = total + lax.ppermute(parts[k], "mp", pairs).astype(F32)
        self.sum = total.astype(BF)

    def take(self, got):
        return None

    def second(self, kernel):
        return None

    def total(self, got):
        return self.sum


def local(
    prefix_input,
    action_input,
    valid_dims,
    slot_item,
    segments,
    pre_gain_attn,
    pre_query,
    pre_key,
    pre_value,
    pre_output,
    pre_gain_ffn,
    pre_gate,
    pre_up,
    pre_down,
    act_embed,
    act_gain_attn,
    act_query,
    act_key,
    act_value,
    act_output,
    act_gain_ffn,
    act_gate,
    act_up,
    act_down,
    prefix_cotangent,
    action_cotangent,
):
    n, m = lax.axis_size("dp"), lax.axis_size("mp")
    me, col = lax.axis_index("dp"), lax.axis_index("mp")
    length, wide = prefix_input.shape
    slot_count, steps, dims_count = action_input.shape
    narrow = action_cotangent.shape[2]
    rq = round_up(-(-length // m), 16)
    aq = round_up(-(-steps // m), 16)
    rows, acts = m * rq, m * aq
    total_rows = rows + acts
    half = n // 2
    heads = pre_query.shape[1] // HD
    split = heads * HD
    scale = HD ** (-0.5)
    kvw = 2 * HD // m
    d_pre, d_act = pre_query.shape[0], act_query.shape[0]
    few = act_gate.shape[1] // n
    lanes = 128
    twice = wide // narrow
    turns = [lax.rem(me + 2 * k, n) for k in range(half)]
    turns = turns + [t ^ 1 for t in turns]

    def own(array, count):
        return lax.dynamic_slice_in_dim(array, col * count, count, 0)

    def pad_rows(array, count):
        return jnp.pad(array, ((0, count - array.shape[0]), (0, 0)))

    def lane_rows(array):
        flat = array.reshape(-1)
        count = round_up(-(-flat.shape[0] // lanes), 16)
        return jnp.pad(flat, (0, count * lanes - flat.shape[0])).reshape(count, lanes)

    def columns_first(array):
        return array.reshape(array.shape[0], n, -1).transpose(1, 0, 2)

    smalls = [pre_gain_attn, pre_gain_ffn, act_gain_attn, act_gain_ffn, act_embed, action_input]
    small = jnp.concatenate([lane_rows(a) for a in smalls], axis=0)
    ints = jnp.pad(jnp.stack([slot_item, valid_dims]), ((0, 6), (0, lanes - slot_count)))
    cot_rows = lax.dynamic_slice_in_dim(
        jnp.pad(action_cotangent, ((0, 0), (0, acts - steps), (0, 0))), col * aq, aq, 1
    ).reshape(slot_count * aq, narrow)

    def share_of(key, value):
        return own(jnp.concatenate([key, value], axis=1).T, kvw).T

    def by_rows(size):
        return lambda ref, i, j: ref.at[at(i, size)]

    def by_columns(size):
        return lambda ref, i, j: ref.at[:, at(i, size)]

    def by_share(size):
        return lambda ref, i, j: ref.at[lax.axis_index("mp"), at(i, size)]

    def by_lead(ref, i, j):
        return ref.at[i]

    kernel = Kernel(1)
    aligned = kvw % lanes == 0
    in_pre, in_act = (wide, split + 2 * HD), (narrow, split + 2 * HD)
    kv_pre, kv_act = share_of(pre_key, pre_value), share_of(act_key, act_value)

    def in_columns(size, share):
        def place(ref, i, j):
            start = split + lax.axis_index("mp") * kvw if share else 0
            columns = pl.ds(pl.multiple_of(start, lanes), kvw if share else split)
            return ref.at[at(i, size), columns]

        return place

    if aligned:
        w_in_pre = kernel.flow(Line(in_columns(d_pre, True), in_pre, True), kv_pre)
        w_in_act = kernel.flow(Line(in_columns(d_act, True), in_act, True), kv_act)
        lines = [w_in_pre, w_in_act]
    else:
        w_kv_pre = kernel.flow(Line(by_share(d_pre), (m, wide, kvw), True), kv_pre)
        w_kv_act = kernel.flow(Line(by_share(d_act), (m, narrow, kvw), True), kv_act)
        lines = [w_kv_pre, w_kv_act]
    small = kernel.flow(Line(by_lead, (n,) + small.shape), small)
    ints = kernel.flow(Line(by_lead, (n, 8, lanes)), ints)
    if aligned:
        w_q_pre = kernel.flow(Line(in_columns(d_pre, False)), pre_query, into=w_in_pre)
        w_q_act = kernel.flow(Line(in_columns(d_act, False)), act_query, into=w_in_act)
    else:
        w_q_pre = kernel.flow(Line(by_rows(d_pre), (wide, split)), pre_query)
        w_q_act = kernel.flow(Line(by_rows(d_act), (narrow, split)), act_query)
    w_out_pre = kernel.flow(Line(by_columns(d_pre), (split, wide)), pre_output)
    w_out_act = kernel.flow(Line(by_lead, (n, split, d_act)), act_output)
    cot_all = kernel.flow(Line(by_lead, (n, slot_count * aq, narrow)), cot_rows)
    lines += [small, ints, w_q_pre, w_q_act, w_out_pre, w_out_act, cot_all]
    for k in range(1, half):
        for out in lines:
            kernel.relay(out, k)
    got = kernel.call("gather")
    small, ints, cot_all = got[small], got[ints], got[cot_all]
    w_out_pre, w_out_act = got[w_out_pre], got[w_out_act]
    if aligned:
        w_in_pre, w_in_act = got[w_in_pre], got[w_in_act]
    else:
        w_in_pre = jnp.concatenate([got[w_q_pre]] + [got[w_kv_pre][k] for k in range(m)], axis=1)
        w_in_act = jnp.concatenate([got[w_q_act]] + [got[w_kv_act][k] for k in range(m)], axis=1)
    smalls_all, begin = [], 0
    for a in smalls:
        count = round_up(-(-a.size // lanes), 16)
        flat = small[:, begin : begin + count].reshape(n, -1)[:, : a.size]
        smalls_all.append(flat.reshape((n,) + a.shape))
        begin += count
    gain_pa, gain_pf, gain_aa, gain_af = [g.reshape(-1).astype(F32) for g in smalls_all[:4]]
    embed = smalls_all[4].transpose(1, 0, 2).reshape(dims_count, narrow)
    act_all = smalls_all[5].reshape(n * slot_count, steps, dims_count)
    slot_all = ints[:, 0, :slot_count].reshape(-1)
    valid_all = ints[:, 1, :slot_count].reshape(-1)
    w_out_act = w_out_act.transpose(1, 0, 2).reshape(split, narrow)

    mine = (slot_all == me).astype(F32)
    valid = jnp.sum(mine * valid_all.astype(F32))
    dims_mask = (lax.broadcasted_iota(jnp.int32, (1, dims_count), 1).astype(F32) < valid).astype(BF)
    act_in = jnp.sum(mine[:, None, None] * act_all.astype(F32), axis=0).astype(BF) * dims_mask
    act_in = pad_rows(act_in, acts)

    x_pre = pad_rows(prefix_input, rows).astype(F32)
    h1_pre = rms_gain(x_pre, gain_pa).astype(BF)
    x_act = dot_plain(act_in, embed)
    h1_act = rms_gain(x_act, gain_aa).astype(BF)
    into = jnp.concatenate(
        [dot_plain(h1_pre, w_in_pre).astype(BF), dot_plain(h1_act, w_in_act).astype(BF)], axis=0
    )
    query = [into[:, h * HD : (h + 1) * HD] for h in range(heads)]
    keys, values = into[:, split : split + HD], into[:, split + HD :]
    last, never = 1 << 10, 1 << 20
    seg = jnp.pad(segments[0], (0, rows - length), constant_values=never)
    seg_q = jnp.concatenate([jnp.minimum(seg, last), jnp.full((acts,), last, jnp.int32)])
    own_keys = jnp.where(jnp.arange(acts, dtype=jnp.int32) < steps, last, never)
    seg_k = jnp.concatenate([seg, own_keys])
    seg_q = jnp.broadcast_to(seg_q[:, None], (total_rows, lanes))
    seg_k = jnp.broadcast_to(seg_k[None, :], (8, total_rows))

    gz_pre = own(pad_rows(prefix_cotangent, rows), rq)
    even = few % lanes == 0 and d_act % lanes == 0
    if not even:
        act_weights = jnp.concatenate(
            [
                columns_first(act_gate),
                columns_first(act_up),
                act_down.reshape(n, few, d_act).transpose(0, 2, 1),
            ],
            axis=1,
        )

    def project(first, count):
        def body(inputs, outputs):
            pairs = len(inputs) - 1
            w_out = inputs[-1]
            width = w_out.shape[1]
            bm, bn = tile(count, 416), tile(width, 1024)

            def step(*refs):
                value = dot_plain(refs[0][...], refs[1][...])
                for h in range(1, pairs):
                    value = value + dot_plain(refs[2 * h][...], refs[2 * h + 1][...])
                refs[-1][...] = value.astype(BF)

            operands, specs = [], []
            for h in range(pairs):
                operands += [inputs[h].at[pl.ds(first, count)], w_out.at[pl.ds(h * HD, HD)]]
                specs += [
                    pl.BlockSpec((bm, HD), lambda j, i: (i, 0)),
                    pl.BlockSpec((HD, bn), lambda j, i: (0, j)),
                ]
            pltpu.emit_pipeline(
                step,
                grid=(width // bn, count // bm),
                in_specs=specs,
                out_specs=[pl.BlockSpec((bm, bn), lambda j, i: (i, j))],
            )(*operands, outputs[0])

        return body

    kernel = Kernel(2)
    gate_own = kernel.flow(Columns(), pre_gate)
    if even:
        act_own = [kernel.flow(Columns(), act_gate), kernel.flow(Columns(), act_up)]
        act_own.append(kernel.flow(Rows(), act_down))
    else:
        act_own = [kernel.flow(Each(), act_weights)]
    up_own = kernel.flow(Columns(), pre_up, now=False)
    probs, mixed = [], []
    for h in range(heads):
        p, o = kernel.job(
            attend_forward,
            [query[h], keys, values, seg_q, seg_k],
            [(total_rows, total_rows), (total_rows, HD)],
        )
        probs.append(p)
        mixed.append(o)
        if h == 0:
            kernel.go(up_own)
    y_pre = kernel.job(project(0, rows), mixed + [w_out_pre], [(rows, wide)])
    y_act = kernel.job(project(rows, acts), mixed + [w_out_act], [(acts, narrow)])
    y_pre_parts = kernel.flow(Parts(), y_pre)
    y_act_parts = kernel.flow(Parts(), y_act)
    kernel.ready(gate_own)
    w_gate = kernel.flow(Pass(1), gate_own)
    down_own = kernel.flow(Rows(), pre_down)
    kernel.relay(w_gate, 1)
    kernel.relay(w_gate, 2)
    got = kernel.call("attend")
    probs, mixed = [got[p] for p in probs], [got[o] for o in mixed]
    up_own, down_own, w_gate = got[up_own], got[down_own], got[w_gate]
    act_own = [got[a] for a in act_own]

    def summed(first, parts):
        value = first.astype(F32)
        for k in range(1, parts.shape[0]):
            value = value + parts[k].astype(F32)
        return value

    x2_pre = own(x_pre, rq) + summed(own(got[y_pre], rq), got[y_pre_parts])
    x2_act = own(x_act, aq) + summed(own(got[y_act], aq), got[y_act_parts])
    h2_pre = rms_gain(x2_pre, gain_pf).astype(BF)
    h2_act = rms_gain(x2_act, gain_af).astype(BF)

    kernel = Kernel(3)
    h2_pre = kernel.flow(Line(), h2_pre)
    h2_act = kernel.flow(Line(), h2_act)
    w_up = kernel.flow(Pass(1), up_own)
    if even:
        act_all_w = [kernel.flow(Pass(axis), a) for axis, a in zip((1, 1, 0), act_own)]
    else:
        act_all_w = [kernel.flow(Pass(0), act_own[0].reshape(n * 3 * d_act, few))]
    for k in range(1, half):
        kernel.relay(h2_pre, k)
        kernel.relay(h2_act, k)
        if k < 3:
            kernel.relay(w_up, k)
    for k in (1, 2):
        for a in act_all_w:
            kernel.relay(a, k)
    got = kernel.call("spread")
    h2_pre, h2_act = got[h2_pre].reshape(n * rq, wide), got[h2_act].reshape(n * aq, narrow)
    w_up = got[w_up]
    if even:
        act_gate_w, act_up_w, act_down_w = [got[a] for a in act_all_w]
    else:
        act_all_w = got[act_all_w[0]].reshape(m, n, 3, d_act, few).transpose(2, 1, 3, 0, 4)
        act_gate_w, act_up_w, act_down_w = act_all_w.reshape(3, narrow, m * few)
        act_down_w = act_down_w.T

    match = (jnp.stack(turns)[:, None] == slot_all[None, :]).astype(BF)
    cot_all = cot_all.reshape(n * slot_count, aq * narrow)
    gz_act_all = dot_plain(match, cot_all).astype(BF).reshape(n * aq, narrow)
    gz_act = gz_act_all[:aq]
    gate_a = dot_plain(h2_act, act_gate_w)
    up_a = dot_plain(h2_act, act_up_w)
    hid_a = glu_value(gate_a, up_a).astype(BF)
    z_a = dot_plain(hid_a, act_down_w).astype(BF)
    dgate_a, dup_a = glu_backward(gate_a, up_a, dot_right(gz_act_all, act_down_w))
    dgate_a, dup_a = dgate_a.astype(BF), dup_a.astype(BF)
    dh2_a = (dot_right(dgate_a, act_gate_w) + dot_right(dup_a, act_up_w)).astype(BF)
    act_back = [dot_left(h2_act, dgate_a), dot_left(h2_act, dup_a)]
    if even:
        g_down_a = dot_left(hid_a, gz_act_all).astype(BF).reshape(m, few, narrow)
    else:
        act_back.append(dot_left(gz_act_all, hid_a))
    act_back = [jnp.concatenate(act_back, axis=0).astype(BF)]
    act_back = [jnp.stack(jnp.split(a, m, axis=1)) for a in act_back]
    if even:
        act_back.append(g_down_a)

    items, units = h2_pre.shape[0], w_gate.shape[1]
    summing = Halves if m == 4 else Direct

    kernel = Kernel(4)
    gz_all = kernel.flow(Line(), gz_pre)
    w_down = kernel.flow(Pass(0), down_own)
    pieces = max(half - 1, m)
    relays = [(gz_all, k) for k in range(1, half)]
    turn = {pieces // 2: (w_down, 1), pieces - 1: (w_down, 2)}
    into = None
    for piece in range(pieces):
        into = kernel.job(
            functools.partial(hidden_forward, piece, pieces),
            [h2_pre, w_gate, w_up],
            [(items, units)] * 3,
            into=into,
        )
        if piece in turn:
            kernel.relay(*turn[piece])
        if piece < len(relays):
            kernel.relay(*relays[piece])
    got = kernel.call("hidden")
    gate, upward, hidden = [got[o] for o in into]
    w_down, gz_pre_all = got[w_down], got[gz_all].reshape(n * rq, wide)

    kernel = Kernel(5)
    g_down = kernel.job(products_left, [hidden, gz_pre_all], [(units, wide)])
    first = kernel.flow(First(0), g_down) if m == 4 else None
    z_p = kernel.job(products_plain, [hidden, w_down], [(items, wide)])
    z_p_core, z_a_core = kernel.flow(Core(), z_p), kernel.flow(Core(), z_a)
    dgate, dup = kernel.job(
        hidden_backward, [gz_pre_all, w_down, gate, upward], [(items, units)] * 2
    )
    got = kernel.call("hidden_grads")
    dgate, dup = got[dgate], got[dup]
    g_down = summing(got[g_down], 0)
    g_down.take(got[first] if m == 4 else None)

    def pair_sum(parts, other):
        return add(parts[: other.shape[0]], other).reshape(half, -1, other.shape[1])

    z_p = pair_sum(got[z_p], got[z_p_core])
    z_a = pair_sum(z_a, got[z_a_core])

    kernel = Kernel(6)
    z_p_parts, z_a_parts = kernel.flow(Chips(), z_p), kernel.flow(Chips(), z_a)
    g_down.second(kernel)
    g_gate = kernel.job(products_left, [h2_pre, dgate], [(wide, units)])
    first = kernel.flow(First(1), g_gate) if m == 4 else None
    g_up = kernel.job(products_left, [h2_pre, dup], [(wide, units)])
    got = kernel.call("in_grads")
    g_gate, g_up = summing(got[g_gate], 1), got[g_up]
    g_gate.take(got[first] if m == 4 else None)
    g_down = g_down.total(got)
    out_pre = (x2_pre + summed(z_p[0], got[z_p_parts])).astype(BF)
    out_act = (x2_act + summed(z_a[0], got[z_a_parts])).astype(BF)

    kernel = Kernel(7)
    first = kernel.flow(First(1), g_up) if m == 4 else None
    grad_down = kernel.flow(Columns(), g_down)
    out_act = kernel.flow(Line(), out_act)
    dh2_p = kernel.job(products_right, [dgate, w_gate, dup, w_up], [(items, wide)])
    dh2_p_core, dh2_a_core = kernel.flow(Core(), dh2_p), kernel.flow(Core(), dh2_a)
    for k in range(1, half):
        kernel.relay(out_act, k)
    got = kernel.call("row_grads")
    out_act = got[out_act].reshape(n * aq, narrow)
    g_up = summing(g_up, 1)
    g_up.take(got[first] if m == 4 else None)
    grad_down = got[grad_down].astype(F32)
    dh2_p = pair_sum(got[dh2_p], got[dh2_p_core])
    dh2_a = pair_sum(dh2_a, got[dh2_a_core])

    kernel = Kernel(8)
    dh2_p_parts, dh2_a_parts = kernel.flow(Chips(), dh2_p), kernel.flow(Chips(), dh2_a)
    g_gate.second(kernel)
    g_up.second(kernel)
    act_parts = [kernel.flow(Swaps(), a) for a in act_back]
    got = kernel.call("sum_rows")
    g_gate, g_up = g_gate.total(got), g_up.total(got)
    act_sum = [summed(a[0], got[b]).astype(BF) for a, b in zip(act_back, act_parts)]
    if not even:
        act_sum = jnp.concatenate(act_sum, axis=0).reshape(3, n, d_act, few)
        act_sum = [act_sum.transpose(1, 0, 2, 3).reshape(n, 3 * d_act, few)]
    gx2n_pre, g_gain_pf = norm_backward(x2_pre, gain_pf, summed(dh2_p[0], got[dh2_p_parts]))
    gx2n_act, g_gain_af = norm_backward(x2_act, gain_af, summed(dh2_a[0], got[dh2_a_parts]))
    gx2_pre = gz_pre.astype(F32) + gx2n_pre
    gx2_act = gz_act.astype(F32) + gx2n_act

    def both_rows(inputs, outputs):
        products_right(inputs[:2], [outputs[0].at[pl.ds(0, rows)]])
        products_right(inputs[2:], [outputs[0].at[pl.ds(rows, acts)]])

    def input_grads(first, count, inputs, outputs):
        w_in, operands = inputs[-1], []
        for h in range(heads):
            operands += [inputs[h].at[pl.ds(first, count)], w_in.at[:, pl.ds(h * HD, HD)]]
        operands += [inputs[heads].at[pl.ds(first, count)], w_in.at[:, pl.ds(split, 2 * HD)]]
        products_right(operands, outputs)

    def weight_grads(first, count, inputs, outputs):
        products_left([a if a.shape[0] == count else a.at[pl.ds(first, count)] for a in inputs], outputs)

    kernel = Kernel(9)
    gy_pre = kernel.flow(Whole(), gx2_pre.astype(BF))
    gy_act = kernel.flow(Whole(), gx2_act.astype(BF))
    grad_gate = kernel.flow(Rows(), g_gate)
    kernel.ready(gy_pre)
    kernel.ready(gy_act)
    grad_up = kernel.flow(Rows(), g_up)
    gmix = kernel.job(both_rows, [gy_pre, w_out_pre, gy_act, w_out_act], [(total_rows, split)])
    *gq, gkv, shares = kernel.job(
        functools.partial(attend_backward, heads),
        probs + query + [keys, values, gmix],
        [(total_rows, HD)] * heads + [(total_rows, 2 * HD), (m, total_rows, kvw)],
    )
    share_parts = kernel.flow(Parts(), shares)
    gh1_pre = kernel.job(
        functools.partial(input_grads, 0, rows), gq + [gkv, w_in_pre], [(rows, wide)]
    )
    gh1_pre_parts = kernel.flow(Parts(), gh1_pre)
    gh1_act = kernel.job(
        functools.partial(input_grads, rows, acts), gq + [gkv, w_in_act], [(acts, narrow)]
    )
    gh1_act_parts = kernel.flow(Parts(), gh1_act)
    if even:
        both = [kernel.flow(Rows(), act_sum[0][k * narrow : (k + 1) * narrow]) for k in (0, 1)]
        act_sum = both + [kernel.flow(Columns(), act_sum[1])]
    else:
        act_sum = [kernel.flow(Each(), act_sum[0])]
    out_act = kernel.flow(Whole(), out_act)
    g_out_pre, g_out_act, g_q_pre, g_q_act = [], [], [], []
    for h in range(heads):
        of_pre = functools.partial(weight_grads, 0, rows)
        of_act = functools.partial(weight_grads, rows, acts)
        g_out_pre.append(kernel.job(of_pre, [mixed[h], gy_pre], [(HD, wide)]))
        g_q_pre.append(kernel.job(of_pre, [h1_pre, gq[h]], [(wide, HD)]))
        g_out_act.append(kernel.job(of_act, [mixed[h], gy_act], [(HD, narrow)]))
        g_q_act.append(kernel.job(of_act, [h1_act, gq[h]], [(narrow, HD)]))
    got = kernel.call("heads")
    grad_gate, grad_up = got[grad_gate].astype(F32), got[grad_up].astype(F32)
    g_out_pre, g_out_act, g_q_pre, g_q_act = [
        [got[o] for o in group] for group in (g_out_pre, g_out_act, g_q_pre, g_q_act)
    ]
    shares, gh1_pre, gh1_act, out_act = got[shares], got[gh1_pre], got[gh1_act], got[out_act]
    gkv_sum = summed(lax.dynamic_index_in_dim(shares, col, 0, False), got[share_parts])
    gh1_pre = summed(own(gh1_pre, rq), got[gh1_pre_parts])
    gh1_act = summed(own(gh1_act, aq), got[gh1_act_parts])
    act_sum = [got[a].astype(F32) for a in act_sum]
    gkv_sum = gkv_sum.astype(BF)
    g_in_pre = g_q_pre + [dot_left(h1_pre, gkv_sum[:rows]).astype(BF)]
    g_in_act = g_q_act + [dot_left(h1_act, gkv_sum[rows:]).astype(BF)]
    gxn_pre, g_gain_pa = norm_backward(own(x_pre, rq), gain_pa, gh1_pre)
    gxn_act, g_gain_aa = norm_backward(own(x_act, aq), gain_aa, gh1_act)
    grad_pre = (gx2_pre + gxn_pre).astype(BF)
    gxa = (gx2_act + gxn_act).astype(BF)
    g_embed = dot_left(own(act_in, aq), gxa)
    act_grad = dot_right(gxa, embed).reshape(aq * dims_count // lanes, lanes)

    def attn_block(item):
        left = [lax.dynamic_slice_in_dim(g, item * d_pre, d_pre, 0) for g in g_in_pre]
        out = [lax.dynamic_slice_in_dim(g, item * d_pre, d_pre, 1) for g in g_out_pre]
        left_a = [lax.dynamic_slice_in_dim(g, item * d_act, d_act, 0) for g in g_in_act]
        out_a = [lax.dynamic_slice_in_dim(g, item * d_act, d_act, 1) for g in g_out_act]

        def aside(blocks, height):
            return [p for b in blocks for p in jnp.split(b, b.shape[0] // height, axis=0)]

        top = jnp.concatenate(left + aside(out, d_pre), axis=1)
        low = jnp.concatenate(left_a + aside(out_a, d_act), axis=1)
        return jnp.concatenate([top, low], axis=0)

    parts = jnp.stack([attn_block(i) for i in turns])
    swapped = lax.ppermute(parts[half:], "dp", [(i, i ^ 1) for i in range(n)])
    parts = add(parts[:half], swapped)

    def by_index(vector):
        return vector.reshape(n, -1, narrow // n).transpose(1, 0, 2).reshape(-1, narrow)

    tiny = [by_index(g) for g in (g_gain_pa, g_gain_pf, g_gain_aa, g_gain_af)] + [g_embed]
    tiny = jnp.concatenate(tiny, axis=0)
    tiny_rows = tiny.shape[0]
    tiny = columns_first(pad_rows(tiny, round_up(tiny_rows, 16)).astype(BF))

    kernel = Kernel(11)
    attn_parts = kernel.flow(Chips(), parts)
    prefix_grad = kernel.flow(Whole(), grad_pre)
    prefix_output = kernel.flow(Whole(), out_pre)
    act_grad = kernel.flow(World(), act_grad)
    tiny = kernel.flow(Spread(), tiny)
    got = kernel.call("finish")
    total = summed(parts[0], got[attn_parts])
    prefix_grad = got[prefix_grad][:length].astype(F32)
    prefix_output = got[prefix_output][:length]
    act_grad = got[act_grad].reshape(n, acts, dims_count)[:, :steps]
    tiny = jnp.sum(got[tiny].astype(F32), axis=(0, 1))
    mine_items = (slot_item[:, None] == lax.broadcasted_iota(jnp.int32, (1, n), 1)).astype(F32)
    mine_turns = (slot_item[:, None] == jnp.stack(turns)[None, :]).astype(F32)
    out_act = out_act.reshape(1, m, n, aq, narrow).astype(F32)
    action_output = jnp.sum(mine_turns[:, None, :, None, None] * out_act, axis=2)
    action_output = action_output.reshape(slot_count, acts, narrow)[:, :steps].astype(BF)
    own_mask = lax.broadcasted_iota(jnp.int32, (slot_count, dims_count), 1) < valid_dims[:, None]
    action_grad = jnp.sum(
        mine_items[:, :, None, None] * act_grad[None], axis=1
    ) * own_mask.astype(F32)[:, None, :]
    grad_gain_pa = tiny[:twice].reshape(-1)
    grad_gain_pf = tiny[twice : 2 * twice].reshape(-1)
    rest = tiny[2 * twice : tiny_rows]

    if even:
        grad_gate_a, grad_up_a, grad_down_a = act_sum
    else:
        act_sum = act_sum[0]
        grad_gate_a = act_sum[:, :d_act].transpose(1, 0, 2).reshape(d_act, n * few)
        grad_up_a = act_sum[:, d_act : 2 * d_act].transpose(1, 0, 2).reshape(d_act, n * few)
        grad_down_a = act_sum[:, 2 * d_act :].transpose(0, 2, 1).reshape(n * few, d_act)
    grad_query, grad_kv = total[:d_pre, :split], total[:d_pre, split : split + kvw]
    grad_out = jnp.concatenate(
        jnp.split(total[:d_pre, split + kvw :], split // d_pre, axis=1), axis=0
    )
    grad_query_a, grad_kv_a = total[d_pre:, :split], total[d_pre:, split : split + kvw]
    grad_out_a = jnp.concatenate(
        jnp.split(total[d_pre:, split + kvw :], split // d_act, axis=1), axis=0
    )
    both = jnp.concatenate([grad_kv, grad_kv_a], axis=0).astype(BF)
    both = lax.all_gather(both, "mp", axis=1, tiled=True).astype(F32)

    return (
        prefix_output,
        action_output,
        prefix_grad,
        action_grad,
        grad_gain_pa,
        grad_query,
        both[:d_pre, :HD],
        both[:d_pre, HD:],
        grad_out,
        grad_gain_pf,
        grad_gate,
        grad_up,
        grad_down,
        rest[2:],
        rest[0],
        grad_query_a,
        both[d_pre:, :HD],
        both[d_pre:, HD:],
        grad_out_a,
        rest[1],
        grad_gate_a,
        grad_up_a,
        grad_down_a,
    )


def solution(mesh):
    return jax.shard_map(
        local,
        mesh=mesh,
        in_specs=(
            P("dp", None),
            P("dp", None, None),
            P("dp"),
            P("dp"),
            P("dp", None),
            P("dp"),
            P("dp", "mp"),
            P("dp", None),
            P("dp", None),
            P("mp", "dp"),
            P("dp"),
            P("dp", "mp"),
            P("dp", "mp"),
            P("mp", "dp"),
            P(None, "dp"),
            P("dp"),
            P("dp", "mp"),
            P("dp", None),
            P("dp", None),
            P("mp", "dp"),
            P("dp"),
            P("dp", "mp"),
            P("dp", "mp"),
            P("mp", "dp"),
            P("dp", None),
            P("dp", None, None),
        ),
        out_specs=(
            P("dp", None),
            P("dp", None, None),
            P("dp", None),
            P("dp", None, None),
            P("dp"),
            P("dp", "mp"),
            P("dp", None),
            P("dp", None),
            P("mp", "dp"),
            P("dp"),
            P("dp", "mp"),
            P("dp", "mp"),
            P("mp", "dp"),
            P(None, "dp"),
            P("dp"),
            P("dp", "mp"),
            P("dp", None),
            P("dp", None),
            P("mp", "dp"),
            P("dp"),
            P("dp", "mp"),
            P("dp", "mp"),
            P("mp", "dp"),
        ),
        check_vma=False,
    )
```

time: 2520 us -> 1240 us (0.49)
  waiting for transfers between devices: 1770 us -> 0.01 us
  Pallas kernels: 0 us -> 1010 us
  matrix products: 345 us -> 23.4 us
  blocking collectives: 237 us -> 8.68 us
  other arithmetic: 92.5 us -> 128 us
    pallas_call x0 -> x10, Pallas kernels: none -> 1010 us  [call(): pl.pallas_call(kernel, out_shape=self.outputs, in_specs=[HBM] * takes, ou...]
    reduce_scatter x13 -> x0, waiting for transfers between devices: 712 us -> none  [the longest x1 167 us: local(): lax.psum_scatter(g_gate_pre.astype(jnp.bfloat16), 'dp', scatter_dimension...]
    all_gather x13 -> x0, waiting for transfers between devices: 588 us -> none  [the longest x1 142 us: local(): lax.all_gather(pre_gate, 'dp', axis=0, tiled=True)]
    psum x4 -> x0, waiting for transfers between devices: 431 us -> none  [the longest x1 127 us: local(): gh2_pre, gh2_act = lax.psum((gh2_pre, gh2_act), 'mp')]
    dot_general x27 -> x7, matrix products: 138 us -> 13.5 us  [dot_plain(): return jnp.dot(left, right, preferred_element_type=F32)]
    psum x1 -> x0, blocking collectives: 121 us -> none  [local(): lax.psum((dot_right(gqb_pre, b_query), gkv_pre_part, dot_right(gqb_act, c...]
    dot_general x13 -> x4, matrix products: 104 us -> 4.5 us  [dot_right(): lax.dot_general(left, right, (((1,), (1,)), ((), ())), preferred_element_...]
    dot_general x13 -> x6, matrix products: 103 us -> 5.48 us  [dot_left(): lax.dot_general(left, right, (((0,), (0,)), ((), ())), preferred_element_...]
  transfers between devices with their start and end apart: 33 -> 1, of which waited for: 28 -> 0; matrix products, arithmetic and copies ran while one was open for 15% -> 3% of each run, Pallas kernels for 0% -> 0%
where the time goes in v3:
time: 1240 us; the launch traced here: 1230 us
  Pallas kernels  1010 us (81%)
  other arithmetic  128 us (10%)
  local copies, waits for them, and re-layouts  57.1 us (5%)
  matrix products  23.4 us (2%)
    pallas_call x10, Pallas kernels, call(): pl.pallas_call(kernel, out_shape=self.outputs, in_specs=[HBM] * takes, ou...  1010 us
    convert_element_type x11, other arithmetic, add(): return (left.astype(F32) + right.astype(F32)).astype(BF)  39.5 us
    unnamed x239, local copies, waits for them, and re-layouts  29.7 us
  transfers between devices with their start and end apart: 1, of which 0 were waited for; matrix products, arithmetic and copies ran while one was open for 3% of the time, Pallas kernels for 0%

profile of v3, /device:TPU:0, one launch (start us, length us, event | category | flops | bytes accessed | tf_op | source)
XLA Modules:
  0.0 1226.9 jit_solution(6274783795038367080)
XLA Ops:
  11.3 90.6 %gather.1 = (bf16[2048,1024]{1,0:T(8,128)(2,1)}, bf16[1024,1024]{1,0:T(8,128)(2,1)}, bf16[8,128,128]{2,1,0:T(8,128)(2,1)}, s32[8,8,128]{2,1,0:T(8,128)}, bf16[51...) custom-call(bf16[256,128]{1,0:T(8,128)(2,1)} %fusion.40.refs_0_, ...), custom_call_target="tpu_custom_call" | custom-call | tf_op jit(solution)/shard_map/gather/pallas_call | solution.py:569
  104.9 2.7 multiply_reduce_fusion
  107.6 3.7 pad_convert_fusion
  127.1 3.7 convolution_convert_fusion.2
  133.8 151.5 %attend.1 = (bf16[2048,512]{1,0:T(8,128)(2,1)}, bf16[1024,128]{1,0:T(8,128)(2,1)}, bf16[1024,128]{1,0:T(8,128)(2,1)}, bf16[128,1024]{1,0:T(8,128)(2,1)}, bf16[20...) custom-call(bf16[256,4096]{1,0:T(8,128)(2,1)} %refs_0_.1, ...), custom_call_target="tpu_custom_call" | custom-call | tf_op jit(solution)/shard_map/attend/pallas_call | solution.py:569
  285.3 3.8 multiply_reduce_fusion.7
  292.5 118.3 %spread.1 = (bf16[8,208,2048]{2,1,0:T(8,128)(2,1)}, bf16[8,16,1024]{2,1,0:T(8,128)(2,1)}, bf16[2048,2048]{1,0:T(8,128)(2,1)}, bf16[1024,512]{1,0:T(8,128)(2,1)},...) custom-call(bf16[208,2048]{1,0:T(8,128)(2,1)} %multiply_convert_fusion.1.refs_0_, ...), custom_call_target="tpu_custom_call" | custom-call | tf_op jit(solution)/shard_map/spread/pallas_call | solution.py:569
  417.6 2.7 multiply_convert_fusion.2
  427.9 89.7 %hidden.1 = (bf16[8,208,2048]{2,1,0:T(8,128)(2,1)}, bf16[2048,2048]{1,0:T(8,128)(2,1)}, bf16[1664,2048]{1,0:T(8,128)(2,1)}, bf16[1664,2048]{1,0:T(8,128)(2,1)}, bf16[1664,2048]{1,0:T(8,128)(2,1)}) custom-call(bf16[208,2048]{1,0:T(8,128)(2,1)} %pad_dynamic-slice_fusion.refs_0_, bf16[512,2048]{1,0:T(8,128)(2,1)} %get-tuple-element.114.refs_1_, ...), custom_call_target="tpu_custom_call" | custom-call | tf_op jit(solution)/shard_map/hidden/pallas_call | solution.py:569
  517.6 86.1 %hidden_grads.1 = (bf16[2048,2048]{1,0:T(8,128)(2,1)}, bf16[4,512,1024]{2,1,0:T(8,128)(2,1)}, bf16[1664,2048]{1,0:T(8,128)(2,1)}, bf16[832,2048]{1,0:T(8,128)(2,...) custom-call(bf16[1664,2048]{1,0:T(8,128)(2,1)} %get-tuple-element.126.refs_0_.refs_2_, ...), custom_call_target="tpu_custom_call" | custom-call | tf_op jit(solution)/shard_map/hidden_grads/pallas_call | solution.py:569
  605.3 6.6 add_convert_fusion.2
  612.0 3.8 fusion.10
  615.8 84.1 %in_grads.1 = (bf16[4,208,2048]{2,1,0:T(8,128)(2,1)}, bf16[4,16,1024]{2,1,0:T(8,128)(2,1)}, bf16[512,1024]{1,0:T(8,128)(2,1)}, bf16[512,1024]{1,0:T(8,128)(2,1)}...) custom-call(bf16[4,208,2048]{2,1,0:T(8,128)(2,1)} %bitcast.372, ...), custom_call_target="tpu_custom_call" | custom-call | tf_op jit(solution)/shard_map/in_grads/pallas_call | solution.py:569
  703.3 3.6 add_convert_fusion.8
  708.4 62.4 %row_grads.1 = (bf16[4,1024,512]{2,1,0:T(8,128)(2,1)}, bf16[4096,256]{1,0:T(8,128)(2,1)}, bf16[8,16,1024]{2,1,0:T(8,128)(2,1)}, bf16[1664,2048]{1,0:T(8,128)(2,1...) custom-call(bf16[2048,2048]{1,0:T(8,128)(2,1)} %get-tuple-element.142.refs_0_, ...), custom_call_target="tpu_custom_call" | custom-call | tf_op jit(solution)/shard_map/row_grads/pallas_call | solution.py:569
  772.4 4.3 fusion.4
  776.7 5.6 add_convert_fusion.1
  782.4 3.6 fusion.6
  787.9 89.7 %sum_rows.1 = (bf16[4,208,2048]{2,1,0:T(8,128)(2,1)}, bf16[4,16,1024]{2,1,0:T(8,128)(2,1)}, bf16[1024,512]{1,0:T(8,128)(2,1)}, bf16[1024,512]{1,0:T(8,128)(2,1)}...) custom-call(bf16[4,208,2048]{2,1,0:T(8,128)(2,1)} %bitcast.371, ...), custom_call_target="tpu_custom_call" | custom-call | tf_op jit(solution)/shard_map/sum_rows/pallas_call | solution.py:569
  877.7 3.4 multiply_reduce_fusion.2
  890.9 2.6 add_convert_fusion.6
  900.3 4.7 fusion.16
  905.0 138.8 %heads.1 = (bf16[832,2048]{1,0:T(8,128)(2,1)}, bf16[64,1024]{1,0:T(8,128)(2,1)}, bf16[256,4096]{1,0:T(8,128)(2,1)}, bf16[256,4096]{1,0:T(8,128)(2,1)}, bf16[896,...) custom-call(bf16[208,2048]{1,0:T(8,128)(2,1)} %get-tuple-element.236, ...), custom_call_target="tpu_custom_call" | custom-call | tf_op jit(solution)/shard_map/heads/pallas_call | solution.py:569
  1075.8 2.5 convert_element_type.933
  1078.4 2.5 convert_element_type.934
  1080.9 2.5 convert_element_type.935
  1086.1 3.1 multiply_reduce_fusion.3
  1097.6 3.9 fusion.14.refs_1_
  1101.5 3.7 add_convert_fusion.refs_0_
  1105.2 95.8 %finish.1 = (bf16[4,384,1152]{2,1,0:T(8,128)(2,1)}, bf16[832,2048]{1,0:T(8,128)(2,1)}, bf16[832,2048]{1,0:T(8,128)(2,1)}, f32[8,4,4,128]{3,2,1,0:T(4,128)}, bf16[8,4,48,128]{3,2,1,0:T(8,128)(2,1)}) custom-call(bf16[4,384,1152]{2,1,0:T(8,128)(2,1)} %add_convert_fusion.refs_0_, bf16[208,2048]{1,0:T(8,128)(2,1)} %fusion.14.refs_1_, ...), custom_call_target="tpu_custom_call" | custom-call | tf_op jit(solution)/shard_map/finish/pallas_call | solution.py:569
  1206.9 8.7 all_gather.3
  1220.4 3.7 slice_convert_fusion
  (371 shorter events, 132.1 us)
Async XLA Ops:
  101.9 5.7 copy-start.2
  102.9 14.3 %copy-start.48 = (bf16[8,4,8,128]{3,2,1,0:T(8,128)(2,1)}, bf16[8,4,8,128]{3,2,1,0:T(8,128)(2,1)S(1)}, u32[]{:S(2)}) copy-start(bf16[8,4,8,128]{3,2,1,0:T(8,128)(2,1)S(1)} %get-tuple-element.346) | copy-start | bytes 196612
  107.6 10.7 copy-start.102
  114.5 6.2 copy-start.79
  118.3 5.7 copy-start.76
  120.8 779.5 %copy-start.74 = (f32[1,2,8,128]{3,1,2,0:T(2,128)}, f32[1,2,8,128]{3,1,2,0:T(2,128)S(1)}, u32[]{:S(2)}) copy-start(f32[1,2,8,128]{3,1,2,0:T(2,128)S(1)} %copy.80) | copy-start | bytes 24580
  124.8 6.0 copy-start
  289.1 121.7 %copy-start.93 = (f32[208]{0:T(256)}, f32[208]{0:T(256)S(1)}, u32[]{:S(2)}) copy-start(f32[208]{0:T(256)S(1)} %get-tuple-element.206) | copy-start | bytes 2500
  289.1 121.7 %copy-start.86 = (f32[208]{0:T(256)}, f32[208]{0:T(256)S(1)}, u32[]{:S(2)}) copy-start(f32[208]{0:T(256)S(1)} %fusion.59) | copy-start | bytes 2500
  290.6 120.2 %copy-start.106 = (f32[16]{0:T(128)}, f32[16]{0:T(128)S(1)}, u32[]{:S(2)}) copy-start(f32[16]{0:T(128)S(1)} %get-tuple-element.204) | copy-start | bytes 196
  290.7 120.2 %copy-start.98 = (f32[16]{0:T(128)}, f32[16]{0:T(128)S(1)}, u32[]{:S(2)}) copy-start(f32[16]{0:T(128)S(1)} %fusion.61) | copy-start | bytes 196
  410.8 4.7 copy-start.52
  415.8 4.5 copy-start.13
  421.3 364.6 %copy-start.4 = (bf16[1024,512]{1,0:T(8,128)(2,1)}, bf16[1024,512]{1,0:T(8,128)(2,1)S(1)}, u32[]{:S(2)}) copy-start(bf16[1024,512]{1,0:T(8,128)(2,1)S(1)} %convolution_convert_fusion.5) | copy-start | bytes 3145732
  517.6 86.1 %copy-start.26 = (bf16[128,1024]{1,0:T(8,128)(2,1)S(1)}, bf16[128,1024]{1,0:T(8,128)(2,1)}, u32[]{:S(2)}) copy-start(bf16[128,1024]{1,0:T(8,128)(2,1)} %convolution_convert_fusion.7.refs_4_) | copy-start | bytes 786436
  605.3 6.7 copy-start.11
  615.8 84.2 %copy-start.28 = (f32[16,1024]{1,0:T(8,128)S(1)}, f32[16,1024]{1,0:T(8,128)}, u32[]{:S(2)}) copy-start(f32[16,1024]{1,0:T(8,128)} %copy-done.27) | copy-start | bytes 196612
  615.8 85.8 %copy-start.53 = (bf16[128,512]{1,0:T(8,128)(2,1)S(1)}, bf16[128,512]{1,0:T(8,128)(2,1)}, u32[]{:S(2)}) copy-start(bf16[128,512]{1,0:T(8,128)(2,1)} %get-tuple-element.325) | copy-start | bytes 393220
  702.1 83.9 %copy-start.5 = (bf16[1024,512]{1,0:T(8,128)(2,1)}, bf16[1024,512]{1,0:T(8,128)(2,1)S(1)}, u32[]{:S(2)}) copy-start(bf16[1024,512]{1,0:T(8,128)(2,1)S(1)} %convolution_convert_fusion.4) | copy-start | bytes 3145732
  708.4 62.4 %copy-start.25 = (bf16[128,1024]{1,0:T(8,128)(2,1)S(1)}, bf16[128,1024]{1,0:T(8,128)(2,1)}, u32[]{:S(2)}) copy-start(bf16[128,1024]{1,0:T(8,128)(2,1)} %fusion.18.refs_7_) | copy-start | bytes 786436
  776.7 5.6 copy-start.8
  787.9 89.7 %copy-start.87 = (f32[208]{0:T(256)S(1)}, f32[208]{0:T(256)}, u32[]{:S(2)}) copy-start(f32[208]{0:T(256)} %copy-done.86) | copy-start | bytes 2500
  877.7 4.7 copy-start.29
  884.5 6.4 copy-start.9
  905.0 140.3 %copy-start.20 = (bf16[64,1024]{1,0:T(8,128)(2,1)S(1)}, bf16[64,1024]{1,0:T(8,128)(2,1)}, u32[]{:S(2)}) copy-start(bf16[64,1024]{1,0:T(8,128)(2,1)} %copy-done.19) | copy-start | bytes 393220
  905.0 141.2 %copy-start.1 = (bf16[832,2048]{1,0:T(8,128)(2,1)S(1)}, bf16[832,2048]{1,0:T(8,128)(2,1)}, u32[]{:S(2)}) copy-start(bf16[832,2048]{1,0:T(8,128)(2,1)} %copy-done) | copy-start | bytes 10223620
  1057.0 6.2 copy-start.33
  1067.5 4.7 copy-start.97
  1069.7 31.8 %collective-permute-start = (bf16[4,384,1152]{2,1,0:T(8,128)(2,1)}, bf16[4,384,1152]{2,1,0:T(8,128)(2,1)}, u32[]{:S(2)}, u32[]{:S(2)}) collective-permute-start(bf16[4,384,1152]{2,1,0:T(8,128)(2,1)} %pad_maximum_fusion), channel_id=1, source_target_pairs={{0,4},{4,0},{8,12},{12,8},{16,20},{20,16},{24,28},{28,24},{1,5},{5... | collective-permute-start | bytes 10616840 | tf_op jit(solution)/shard_map/ppermute | solution.py:1301
  1080.9 5.2 copy-start.6
  1092.3 5.2 copy-start.7
  1204.3 12.9 %copy-start.18 = (bf16[832,2048]{1,0:T(8,128)(2,1)S(1)}, bf16[832,2048]{1,0:T(8,128)(2,1)}, u32[]{:S(2)}) copy-start(bf16[832,2048]{1,0:T(8,128)(2,1)} %get-tuple-element.181) | copy-start | bytes 10223620
  (77 other events, 188.4 us)

commit v4 on v3

--- a/solution.py
+++ b/solution.py
@@ -65,17 +65,17 @@
 
 
 class Place:
-    def __init__(self, n, m, sent, arrived, row):
+    def __init__(self, n, m, sent, arrived, first):
         self.n, self.m = n, m
         self.me, self.col = lax.axis_index("dp"), lax.axis_index("mp")
-        self.sent, self.arrived, self.row = sent, arrived, row
+        self.sent, self.arrived, self.first = sent, arrived, first
 
     def remote(self, src, dst, slot, device):
         return pltpu.make_async_remote_copy(
             src_ref=src,
             dst_ref=dst,
-            send_sem=self.sent.at[self.row, slot],
-            recv_sem=self.arrived.at[self.row, slot],
+            send_sem=self.sent.at[self.first + slot],
+            recv_sem=self.arrived.at[self.first + slot],
             device_id=device,
             device_id_type=MESH,
         )
@@ -102,6 +102,9 @@
     reach = "dp"
     kept = False
 
+    def slots(self, n, m):
+        return max(n, m, 4)
+
     def result(self, shape, n, m):
         return shape
 
@@ -173,6 +176,21 @@
         loop(1, p.n, body)
 
 
+class EachRows(Each):
+    def result(self, shape, n, m):
+        return (n, shape[0] // n, shape[1])
+
+    def own(self, p, src, dst):
+        return src.at[at(p.me, dst.shape[1])], dst.at[p.me]
+
+    def each(self, p, src, dst, do):
+        def body(s):
+            target = p.over_dp(s)
+            do(p.remote(src.at[at(target[0], dst.shape[1])], dst.at[p.me], s, target))
+
+        loop(1, p.n, body)
+
+
 class Chips(Flow):
     def each(self, p, src, dst, do):
         loop(1, p.n // 2, lambda s: do(p.remote(src.at[s], dst.at[s], s, p.over_dp(2 * s))))
@@ -188,14 +206,11 @@
 
 
 class CoreRows(Flow):
-    axis = 0
-
     def result(self, shape, n, m):
-        return (shape[0] // 2, shape[1]) if self.axis == 0 else (shape[0], shape[1] // 2)
+        return (shape[0] // 2, shape[1])
 
     def cut(self, ref, i, count):
-        size = ref.shape[self.axis] // count
-        return ref.at[at(i, size)] if self.axis == 0 else ref.at[:, at(i, size)]
+        return ref.at[at(i, ref.shape[0] // count)]
 
     def each(self, p, src, dst, do):
         def body(c):
@@ -205,15 +220,9 @@
         loop(0, p.n // 2, body)
 
 
-class CoreColumns(CoreRows):
-    axis = 1
-
-
 class ChipRows(CoreRows):
     def result(self, shape, n, m):
-        if self.axis == 0:
-            return (n // 2, shape[0] // (n // 2), shape[1])
-        return (n // 2, shape[0], shape[1] // (n // 2))
+        return (n // 2, shape[0] // (n // 2), shape[1])
 
     def each(self, p, src, dst, do):
         def body(s):
@@ -221,10 +230,6 @@
             do(p.remote(self.cut(src, target[0] // 2, p.n // 2), dst.at[s], s, target))
 
         loop(1, p.n // 2, body)
-
-
-class ChipColumns(ChipRows):
-    axis = 1
 
 
 class Line(Flow):
@@ -233,6 +238,9 @@
         self.shape = result
         self.share = share
         self.reach = "both" if share else "dp"
+
+    def slots(self, n, m):
+        return 2 * n + (n * m if self.share else 0)
 
     def in_turn(ref, i, j):
         chips = lax.axis_size("dp") // 2
@@ -330,6 +338,9 @@
     def __init__(self, axis):
         self.axis = axis
 
+    def slots(self, n, m):
+        return max(4, m) * self.parts
+
     def result(self, shape, n, m):
         return (shape[0], m * shape[1]) if self.axis else (m * shape[0], shape[1])
 
@@ -448,6 +459,9 @@
 class World(Flow):
     reach = "world"
     kept = True
+
+    def slots(self, n, m):
+        return n * m
 
     def result(self, shape, n, m):
         return (n, m) + shape
@@ -527,10 +541,11 @@
         n, m = lax.axis_size("dp"), lax.axis_size("mp")
         takes, gives = len(self.inputs), len(self.outputs)
         flows, steps = self.flows, self.steps
-        count = max(len(flows), 1)
         rows = {flow[3]: row for row, flow in enumerate(flows)}
         reach = {flow[0].reach for flow in flows}
-        slots = max(2 * n + n * m, 4 * Pass.parts, Pass.parts * m)
+        firsts = [0]
+        for flow in flows:
+            firsts.append(firsts[-1] + flow[0].slots(n, m))
 
         def kernel(*refs):
             ins, outs = refs[:takes], refs[takes : takes + gives]
@@ -551,7 +566,7 @@
 
             def act(what, name, *rest):
                 kind, source, out, unused = flows[rows[name]]
-                place = Place(n, m, sent, arrived, rows[name])
+                place = Place(n, m, sent, arrived, firsts[rows[name]])
                 getattr(kind, what)(place, ref(source), outs[out], *rest)
 
             ended = set()
@@ -572,8 +587,8 @@
             in_specs=[HBM] * takes,
             out_specs=[HBM] * gives,
             scratch_shapes=[
-                pltpu.SemaphoreType.DMA((count, slots)),
-                pltpu.SemaphoreType.DMA((count, slots)),
+                pltpu.SemaphoreType.DMA((firsts[-1],)),
+                pltpu.SemaphoreType.DMA((firsts[-1],)),
             ],
             compiler_params=pltpu.CompilerParams(
                 collective_id=self.collective_id,
@@ -591,7 +606,7 @@
 def products_plain(inputs, outputs):
     a, b = inputs
     (rows, depth), width = a.shape, b.shape[1]
-    bm, bn = tile(rows, 416), tile(width, 512)
+    bm, bn = tile(rows, 832), tile(width, 512)
 
     def body(a_ref, b_ref, o_ref):
         o_ref[...] = dot_plain(a_ref[...], b_ref[...]).astype(BF)
@@ -610,7 +625,7 @@
 def products_right(inputs, outputs):
     pairs = len(inputs) // 2
     rows, width = inputs[0].shape[0], inputs[1].shape[0]
-    bm, bn = tile(rows, 416), tile(width, 512)
+    bm, bn = tile(rows, 832), tile(width, 512)
 
     def body(*refs):
         total = dot_right(refs[0][...], refs[1][...])
@@ -621,13 +636,13 @@
     specs = []
     for p in range(pairs):
         depth = inputs[2 * p].shape[1]
-        specs.append(pl.BlockSpec((bm, depth), lambda j, i: (i, 0)))
-        specs.append(pl.BlockSpec((bn, depth), lambda j, i: (j, 0)))
+        specs.append(pl.BlockSpec((bm, depth), lambda i, j: (i, 0)))
+        specs.append(pl.BlockSpec((bn, depth), lambda i, j: (j, 0)))
     pltpu.emit_pipeline(
         body,
-        grid=(width // bn, rows // bm),
+        grid=(rows // bm, width // bn),
         in_specs=specs,
-        out_specs=[pl.BlockSpec((bm, bn), lambda j, i: (i, j))],
+        out_specs=[pl.BlockSpec((bm, bn), lambda i, j: (i, j))],
     )(*inputs, outputs[0])
 
 
@@ -656,7 +671,7 @@
     cut = pl.ds(part * width, width)
     w_gate, w_up = w_gate.at[:, cut], w_up.at[:, cut]
     outputs = [o.at[:, cut] for o in outputs]
-    bm, bn = tile(rows, 416), tile(width, 512)
+    bm, bn = tile(rows, 832), tile(width, 512)
 
     def body(h_ref, gate_w, up_w, gate_ref, up_ref, hidden_ref):
         gate = dot_plain(h_ref[...], gate_w[...])
@@ -678,7 +693,7 @@
 def hidden_backward(inputs, outputs):
     gz, w_down, gate, upward = inputs
     (rows, depth), width = gz.shape, w_down.shape[0]
-    bm, bn = tile(rows, 416), tile(width, 512)
+    bm, bn = tile(rows, 832), tile(width, 512)
 
     def body(gz_ref, down_w, gate_ref, up_ref, dgate_ref, dup_ref):
         grad = dot_right(gz_ref[...], down_w[...])
@@ -1036,11 +1051,6 @@
 
     kernel = Kernel(2)
     gate_own = kernel.flow(Columns(), pre_gate)
-    if even:
-        act_own = [kernel.flow(Columns(), act_gate), kernel.flow(Columns(), act_up)]
-        act_own.append(kernel.flow(Rows(), act_down))
-    else:
-        act_own = [kernel.flow(Each(), act_weights)]
     up_own = kernel.flow(Columns(), pre_up, now=False)
     probs, mixed = [], []
     for h in range(heads):
@@ -1065,7 +1075,6 @@
     got = kernel.call("attend")
     probs, mixed = [got[p] for p in probs], [got[o] for o in mixed]
     up_own, down_own, w_gate = got[up_own], got[down_own], got[w_gate]
-    act_own = [got[a] for a in act_own]
 
     def summed(first, parts):
         value = first.astype(F32)
@@ -1080,23 +1089,69 @@
 
     kernel = Kernel(3)
     h2_pre = kernel.flow(Line(), h2_pre)
-    h2_act = kernel.flow(Line(), h2_act)
+    h2_act = kernel.flow(Line(by_lead, (n, aq, narrow)), h2_act)
     w_up = kernel.flow(Pass(1), up_own)
     if even:
-        act_all_w = [kernel.flow(Pass(axis), a) for axis, a in zip((1, 1, 0), act_own)]
+        act_own = [kernel.flow(Columns(), act_gate), kernel.flow(Columns(), act_up)]
+        act_own.append(kernel.flow(Rows(), act_down))
     else:
-        act_all_w = [kernel.flow(Pass(0), act_own[0].reshape(n * 3 * d_act, few))]
+        act_own = [kernel.flow(Each(), act_weights)]
     for k in range(1, half):
         kernel.relay(h2_pre, k)
         kernel.relay(h2_act, k)
         if k < 3:
             kernel.relay(w_up, k)
+    got = kernel.call("spread")
+    act_own = [got[a] for a in act_own]
+    h2_pre, h2_act = got[h2_pre].reshape(n * rq, wide), got[h2_act].reshape(n * aq, narrow)
+    w_up = got[w_up]
+    items, units = h2_pre.shape[0], w_gate.shape[1]
+    summing = Halves if m == 4 else Direct
+
+    kernel = Kernel(4)
+    gz_all = kernel.flow(Line(), gz_pre)
+    w_down = kernel.flow(Pass(0), down_own)
+    into = None
+    for piece in range(2):
+        into = kernel.job(
+            functools.partial(hidden_forward, piece, 2),
+            [h2_pre, w_gate, w_up],
+            [(items, units)] * 3,
+            into=into,
+        )
+        kernel.relay(gz_all, piece + 1)
+    kernel.relay(w_down, 1)
+    kernel.relay(w_down, 2)
+    for k in range(3, half):
+        kernel.relay(gz_all, k)
+    got = kernel.call("hidden")
+    gate, upward, hidden = [got[o] for o in into]
+    w_down, gz_pre_all = got[w_down], got[gz_all].reshape(n * rq, wide)
+
+    kernel = Kernel(5)
+    if even:
+        act_all_w = [kernel.flow(Pass(axis), a) for axis, a in zip((1, 1, 0), act_own)]
+    else:
+        act_all_w = [kernel.flow(Pass(0), act_own[0].reshape(n * 3 * d_act, few))]
+    g_down = kernel.job(products_left, [hidden, gz_pre_all], [(units, wide)])
+    first = kernel.flow(First(0), g_down) if m == 4 else None
+    z_p = kernel.job(products_plain, [hidden, w_down], [(items, wide)])
+    z_p_core = kernel.flow(Core(), z_p)
     for k in (1, 2):
         for a in act_all_w:
             kernel.relay(a, k)
-    got = kernel.call("spread")
-    h2_pre, h2_act = got[h2_pre].reshape(n * rq, wide), got[h2_act].reshape(n * aq, narrow)
-    w_up = got[w_up]
+    dgate, dup = kernel.job(
+        hidden_backward, [gz_pre_all, w_down, gate, upward], [(items, units)] * 2
+    )
+    got = kernel.call("hidden_grads")
+    dgate, dup = got[dgate], got[dup]
+    g_down = summing(got[g_down], 0)
+    g_down.take(got[first] if m == 4 else None)
+
+    def pair_sum(parts, other):
+        return add(parts[: other.shape[0]], other).reshape(half, -1, other.shape[1])
+
+    z_p = pair_sum(got[z_p], got[z_p_core])
     if even:
         act_gate_w, act_up_w, act_down_w = [got[a] for a in act_all_w]
     else:
@@ -1104,10 +1159,10 @@
         act_gate_w, act_up_w, act_down_w = act_all_w.reshape(3, narrow, m * few)
         act_down_w = act_down_w.T
 
-    match = (jnp.stack(turns)[:, None] == slot_all[None, :]).astype(BF)
+    match = (lax.broadcasted_iota(jnp.int32, (n, 1), 0) == slot_all[None, :]).astype(BF)
     cot_all = cot_all.reshape(n * slot_count, aq * narrow)
     gz_act_all = dot_plain(match, cot_all).astype(BF).reshape(n * aq, narrow)
-    gz_act = gz_act_all[:aq]
+    gz_act = lax.dynamic_slice_in_dim(gz_act_all, me * aq, aq, 0)
     gate_a = dot_plain(h2_act, act_gate_w)
     up_a = dot_plain(h2_act, act_up_w)
     hid_a = glu_value(gate_a, up_a).astype(BF)
@@ -1125,52 +1180,8 @@
     if even:
         act_back.append(g_down_a)
 
-    items, units = h2_pre.shape[0], w_gate.shape[1]
-    summing = Halves if m == 4 else Direct
-
-    kernel = Kernel(4)
-    gz_all = kernel.flow(Line(), gz_pre)
-    w_down = kernel.flow(Pass(0), down_own)
-    pieces = max(half - 1, m)
-    relays = [(gz_all, k) for k in range(1, half)]
-    turn = {pieces // 2: (w_down, 1), pieces - 1: (w_down, 2)}
-    into = None
-    for piece in range(pieces):
-        into = kernel.job(
-            functools.partial(hidden_forward, piece, pieces),
-            [h2_pre, w_gate, w_up],
-            [(items, units)] * 3,
-            into=into,
-        )
-        if piece in turn:
-            kernel.relay(*turn[piece])
-        if piece < len(relays):
-            kernel.relay(*relays[piece])
-    got = kernel.call("hidden")
-    gate, upward, hidden = [got[o] for o in into]
-    w_down, gz_pre_all = got[w_down], got[gz_all].reshape(n * rq, wide)
-
-    kernel = Kernel(5)
-    g_down = kernel.job(products_left, [hidden, gz_pre_all], [(units, wide)])
-    first = kernel.flow(First(0), g_down) if m == 4 else None
-    z_p = kernel.job(products_plain, [hidden, w_down], [(items, wide)])
-    z_p_core, z_a_core = kernel.flow(Core(), z_p), kernel.flow(Core(), z_a)
-    dgate, dup = kernel.job(
-        hidden_backward, [gz_pre_all, w_down, gate, upward], [(items, units)] * 2
-    )
-    got = kernel.call("hidden_grads")
-    dgate, dup = got[dgate], got[dup]
-    g_down = summing(got[g_down], 0)
-    g_down.take(got[first] if m == 4 else None)
-
-    def pair_sum(parts, other):
-        return add(parts[: other.shape[0]], other).reshape(half, -1, other.shape[1])
-
-    z_p = pair_sum(got[z_p], got[z_p_core])
-    z_a = pair_sum(z_a, got[z_a_core])
-
     kernel = Kernel(6)
-    z_p_parts, z_a_parts = kernel.flow(Chips(), z_p), kernel.flow(Chips(), z_a)
+    z_p_parts, z_a = kernel.flow(Chips(), z_p), kernel.flow(EachRows(), z_a)
     g_down.second(kernel)
     g_gate = kernel.job(products_left, [h2_pre, dgate], [(wide, units)])
     first = kernel.flow(First(1), g_gate) if m == 4 else None
@@ -1180,14 +1191,14 @@
     g_gate.take(got[first] if m == 4 else None)
     g_down = g_down.total(got)
     out_pre = (x2_pre + summed(z_p[0], got[z_p_parts])).astype(BF)
-    out_act = (x2_act + summed(z_a[0], got[z_a_parts])).astype(BF)
+    out_act = (x2_act + jnp.sum(got[z_a].astype(F32), axis=0)).astype(BF)
 
     kernel = Kernel(7)
     first = kernel.flow(First(1), g_up) if m == 4 else None
     grad_down = kernel.flow(Columns(), g_down)
     out_act = kernel.flow(Line(), out_act)
     dh2_p = kernel.job(products_right, [dgate, w_gate, dup, w_up], [(items, wide)])
-    dh2_p_core, dh2_a_core = kernel.flow(Core(), dh2_p), kernel.flow(Core(), dh2_a)
+    dh2_p_core = kernel.flow(Core(), dh2_p)
     for k in range(1, half):
         kernel.relay(out_act, k)
     got = kernel.call("row_grads")
@@ -1196,10 +1207,9 @@
     g_up.take(got[first] if m == 4 else None)
     grad_down = got[grad_down].astype(F32)
     dh2_p = pair_sum(got[dh2_p], got[dh2_p_core])
-    dh2_a = pair_sum(dh2_a, got[dh2_a_core])
 
     kernel = Kernel(8)
-    dh2_p_parts, dh2_a_parts = kernel.flow(Chips(), dh2_p), kernel.flow(Chips(), dh2_a)
+    dh2_p_parts, dh2_a = kernel.flow(Chips(), dh2_p), kernel.flow(EachRows(), dh2_a)
     g_gate.second(kernel)
     g_up.second(kernel)
     act_parts = [kernel.flow(Swaps(), a) for a in act_back]
@@ -1210,7 +1220,7 @@
         act_sum = jnp.concatenate(act_sum, axis=0).reshape(3, n, d_act, few)
         act_sum = [act_sum.transpose(1, 0, 2, 3).reshape(n, 3 * d_act, few)]
     gx2n_pre, g_gain_pf = norm_backward(x2_pre, gain_pf, summed(dh2_p[0], got[dh2_p_parts]))
-    gx2n_act, g_gain_af = norm_backward(x2_act, gain_af, summed(dh2_a[0], got[dh2_a_parts]))
+    gx2n_act, g_gain_af = norm_backward(x2_act, gain_af, jnp.sum(got[dh2_a].astype(F32), axis=0))
     gx2_pre = gz_pre.astype(F32) + gx2n_pre
     gx2_act = gz_act.astype(F32) + gx2n_act
 
@@ -1225,8 +1235,9 @@
         operands += [inputs[heads].at[pl.ds(first, count)], w_in.at[:, pl.ds(split, 2 * HD)]]
         products_right(operands, outputs)
 
-    def weight_grads(first, count, inputs, outputs):
-        products_left([a if a.shape[0] == count else a.at[pl.ds(first, count)] for a in inputs], outputs)
+    def weight_grads(first, count, cut, inputs, outputs):
+        inputs = [a if a.shape[0] == count else a.at[pl.ds(first, count)] for a in inputs]
+        products_left(inputs, [outputs[0].at[cut]])
 
     kernel = Kernel(9)
     gy_pre = kernel.flow(Whole(), gx2_pre.astype(BF))
@@ -1256,27 +1267,40 @@
     else:
         act_sum = [kernel.flow(Each(), act_sum[0])]
     out_act = kernel.flow(Whole(), out_act)
-    g_out_pre, g_out_act, g_q_pre, g_q_act = [], [], [], []
+    g_out_pre = g_out_act = g_q_pre = g_q_act = None
     for h in range(heads):
+        heads_columns = (slice(None), pl.ds(h * HD, HD))
         of_pre = functools.partial(weight_grads, 0, rows)
         of_act = functools.partial(weight_grads, rows, acts)
-        g_out_pre.append(kernel.job(of_pre, [mixed[h], gy_pre], [(HD, wide)]))
-        g_q_pre.append(kernel.job(of_pre, [h1_pre, gq[h]], [(wide, HD)]))
-        g_out_act.append(kernel.job(of_act, [mixed[h], gy_act], [(HD, narrow)]))
-        g_q_act.append(kernel.job(of_act, [h1_act, gq[h]], [(narrow, HD)]))
+
+        def grads(body, cut, pair, shape, into):
+            return [kernel.job(functools.partial(body, cut), pair, [shape], into=into)]
+
+        g_out_pre = grads(of_pre, heads_columns, [gy_pre, mixed[h]], (wide, split), g_out_pre)
+        g_q_pre = grads(of_pre, heads_columns, [h1_pre, gq[h]], (wide, split), g_q_pre)
+        g_out_act = grads(of_act, heads_columns, [gy_act, mixed[h]], (narrow, split), g_out_act)
+        g_q_act = grads(of_act, heads_columns, [h1_act, gq[h]], (narrow, split), g_q_act)
+    core_grads = [g[0] for g in (g_out_pre, g_q_pre, g_out_act, g_q_act)]
+    from_core = [kernel.flow(CoreRows(), g) for g in core_grads]
     got = kernel.call("heads")
     grad_gate, grad_up = got[grad_gate].astype(F32), got[grad_up].astype(F32)
-    g_out_pre, g_out_act, g_q_pre, g_q_act = [
-        [got[o] for o in group] for group in (g_out_pre, g_out_act, g_q_pre, g_q_act)
-    ]
+    here = lax.rem(me, 2)
+
+    def of_core(array, core):
+        size = array.shape[0] // n
+        blocks = array.reshape(half, 2, size, array.shape[1])
+        blocks = lax.dynamic_index_in_dim(blocks, core, 1, False)
+        return blocks.reshape(half * size, array.shape[1])
+
+    chip_grads = [add(of_core(got[g], here), got[f]) for g, f in zip(core_grads, from_core)]
     shares, gh1_pre, gh1_act, out_act = got[shares], got[gh1_pre], got[gh1_act], got[out_act]
     gkv_sum = summed(lax.dynamic_index_in_dim(shares, col, 0, False), got[share_parts])
     gh1_pre = summed(own(gh1_pre, rq), got[gh1_pre_parts])
     gh1_act = summed(own(gh1_act, aq), got[gh1_act_parts])
     act_sum = [got[a].astype(F32) for a in act_sum]
     gkv_sum = gkv_sum.astype(BF)
-    g_in_pre = g_q_pre + [dot_left(h1_pre, gkv_sum[:rows]).astype(BF)]
-    g_in_act = g_q_act + [dot_left(h1_act, gkv_sum[rows:]).astype(BF)]
+    g_kv_pre = dot_left(h1_pre, gkv_sum[:rows]).astype(BF)
+    g_kv_act = dot_left(h1_act, gkv_sum[rows:]).astype(BF)
     gxn_pre, g_gain_pa = norm_backward(own(x_pre, rq), gain_pa, gh1_pre)
     gxn_act, g_gain_aa = norm_backward(own(x_act, aq), gain_aa, gh1_act)
     grad_pre = (gx2_pre + gxn_pre).astype(BF)
@@ -1284,23 +1308,11 @@
     g_embed = dot_left(own(act_in, aq), gxa)
     act_grad = dot_right(gxa, embed).reshape(aq * dims_count // lanes, lanes)
 
-    def attn_block(item):
-        left = [lax.dynamic_slice_in_dim(g, item * d_pre, d_pre, 0) for g in g_in_pre]
-        out = [lax.dynamic_slice_in_dim(g, item * d_pre, d_pre, 1) for g in g_out_pre]
-        left_a = [lax.dynamic_slice_in_dim(g, item * d_act, d_act, 0) for g in g_in_act]
-        out_a = [lax.dynamic_slice_in_dim(g, item * d_act, d_act, 1) for g in g_out_act]
-
-        def aside(blocks, height):
-            return [p for b in blocks for p in jnp.split(b, b.shape[0] // height, axis=0)]
-
-        top = jnp.concatenate(left + aside(out, d_pre), axis=1)
-        low = jnp.concatenate(left_a + aside(out_a, d_act), axis=1)
-        return jnp.concatenate([top, low], axis=0)
-
-    parts = jnp.stack([attn_block(i) for i in turns])
-    swapped = lax.ppermute(parts[half:], "dp", [(i, i ^ 1) for i in range(n)])
-    parts = add(parts[:half], swapped)
-
+    swap = [(i, i ^ 1) for i in range(n)]
+    chip_grads += [
+        add(of_core(g, here), lax.ppermute(of_core(g, 1 - here), "dp", swap))
+        for g in (g_kv_pre, g_kv_act)
+    ]
     def by_index(vector):
         return vector.reshape(n, -1, narrow // n).transpose(1, 0, 2).reshape(-1, narrow)
 
@@ -1310,13 +1322,23 @@
     tiny = columns_first(pad_rows(tiny, round_up(tiny_rows, 16)).astype(BF))
 
     kernel = Kernel(11)
-    attn_parts = kernel.flow(Chips(), parts)
+    chip_parts = [kernel.flow(ChipRows(), g) for g in chip_grads]
     prefix_grad = kernel.flow(Whole(), grad_pre)
     prefix_output = kernel.flow(Whole(), out_pre)
     act_grad = kernel.flow(World(), act_grad)
     tiny = kernel.flow(Spread(), tiny)
     got = kernel.call("finish")
-    total = summed(parts[0], got[attn_parts])
+
+    def chip_sum(own_parts, parts):
+        size = own_parts.shape[0] // half
+        return summed(lax.dynamic_slice_in_dim(own_parts, me // 2 * size, size, 0), got[parts])
+
+    grad_out, grad_query, grad_out_a, grad_query_a, *both = [
+        chip_sum(g, f) for g, f in zip(chip_grads, chip_parts)
+    ]
+    grad_out, grad_out_a = grad_out.T, grad_out_a.T
+    both = jnp.concatenate(both, axis=0).astype(BF)
+    both = lax.all_gather(both, "mp", axis=1, tiled=True).astype(F32)
     prefix_grad = got[prefix_grad][:length].astype(F32)
     prefix_output = got[prefix_output][:length]
     act_grad = got[act_grad].reshape(n, acts, dims_count)[:, :steps]
@@ -1341,17 +1363,6 @@
         grad_gate_a = act_sum[:, :d_act].transpose(1, 0, 2).reshape(d_act, n * few)
         grad_up_a = act_sum[:, d_act : 2 * d_act].transpose(1, 0, 2).reshape(d_act, n * few)
         grad_down_a = act_sum[:, 2 * d_act :].transpose(0, 2, 1).reshape(n * few, d_act)
-    grad_query, grad_kv = total[:d_pre, :split], total[:d_pre, split : split + kvw]
-    grad_out = jnp.concatenate(
-        jnp.split(total[:d_pre, split + kvw :], split // d_pre, axis=1), axis=0
-    )
-    grad_query_a, grad_kv_a = total[d_pre:, :split], total[d_pre:, split : split + kvw]
-    grad_out_a = jnp.concatenate(
-        jnp.split(total[d_pre:, split + kvw :], split // d_act, axis=1), axis=0
-    )
-    both = jnp.concatenate([grad_kv, grad_kv_a], axis=0).astype(BF)
-    both = lax.all_gather(both, "mp", axis=1, tiled=True).astype(F32)
-
     return (
         prefix_output,
         action_output,

time: 1240 us -> 1160 us (0.935)
  Pallas kernels: 1010 us -> 925 us
    pallas_call x10, Pallas kernels: 1010 us -> 925 us  [call(): pl.pallas_call(kernel, out_shape=self.outputs, in_specs=[HBM] * takes, ou...]
    unnamed x239 -> x180, local copies, waits for them, and re-layouts: 29.7 us -> 22.6 us
    convert_element_type x11 -> x14, other arithmetic: 39.5 us -> 39 us  [add(): return (left.astype(F32) + right.astype(F32)).astype(BF)]
  transfers between devices with their start and end apart: 1 -> 2, of which waited for: 0 -> 0; matrix products, arithmetic and copies ran while one was open for 3% -> 4% of each run, Pallas kernels for 0% -> 0%
where the time goes in v4:
time: 1160 us; the launch traced here: 1150 us
  Pallas kernels  925 us (80%)
  other arithmetic  129 us (11%)
  local copies, waits for them, and re-layouts  55.9 us (5%)
  matrix products  25.8 us (2%)
    pallas_call x10, Pallas kernels, call(): pl.pallas_call(kernel, out_shape=self.outputs, in_specs=[HBM] * takes, ou...  925 us
    convert_element_type x14, other arithmetic, add(): return (left.astype(F32) + right.astype(F32)).astype(BF)  39 us
  transfers between devices with their start and end apart: 2, of which 0 were waited for; matrix products, arithmetic and copies ran while one was open for 4% of the time, Pallas kernels for 0%

profile of v4, /device:TPU:0, one launch (start us, length us, event | category | flops | bytes accessed | tf_op | source)
XLA Modules:
  0.0 1146.5 jit_solution(4665876944184405507)
XLA Ops:
  1.2 3.5 multiply_reduce_fusion
  4.7 3.7 pad_convert_fusion
  21.9 86.5 %gather.1 = (bf16[2048,1024]{1,0:T(8,128)(2,1)}, bf16[1024,1024]{1,0:T(8,128)(2,1)}, bf16[8,128,128]{2,1,0:T(8,128)(2,1)}, s32[8,8,128]{2,1,0:T(8,128)}, bf16[51...) custom-call(bf16[256,128]{1,0:T(8,128)(2,1)} %fusion.49.refs_0_, ...), custom_call_target="tpu_custom_call" | custom-call | tf_op jit(solution)/shard_map/gather/pallas_call | solution.py:584
  137.5 3.7 convolution_convert_fusion.2
  144.0 141.2 %attend.1 = (bf16[2048,512]{1,0:T(8,128)(2,1)}, bf16[2048,512]{1,0:T(8,128)(2,1)}, bf16[896,896]{1,0:T(8,128)(2,1)}, bf16[896,256]{1,0:T(8,128)(2,1)}, bf16[896,...) custom-call(bf16[256,4096]{1,0:T(8,128)(2,1)} %refs_0_.1, ...), custom_call_target="tpu_custom_call" | custom-call | tf_op jit(solution)/shard_map/attend/pallas_call | solution.py:584
  285.3 3.8 multiply_reduce_fusion.7
  292.4 85.5 %spread.1 = (bf16[8,208,2048]{2,1,0:T(8,128)(2,1)}, bf16[8,16,1024]{2,1,0:T(8,128)(2,1)}, bf16[2048,2048]{1,0:T(8,128)(2,1)}, bf16[1024,128]{1,0:T(8,128)(2,1)},...) custom-call(bf16[208,2048]{1,0:T(8,128)(2,1)} %multiply_convert_fusion.1.refs_0_, ...), custom_call_target="tpu_custom_call" | custom-call | tf_op jit(solution)/shard_map/spread/pallas_call | solution.py:584
  377.8 75.6 %hidden.1 = (bf16[8,208,2048]{2,1,0:T(8,128)(2,1)}, bf16[2048,2048]{1,0:T(8,128)(2,1)}, bf16[1664,2048]{1,0:T(8,128)(2,1)}, bf16[1664,2048]{1,0:T(8,128)(2,1)}, bf16[1664,2048]{1,0:T(8,128)(2,1)}) custom-call(bf16[208,2048]{1,0:T(8,128)(2,1)} %pad_dynamic-slice_fusion.refs_0_, bf16[512,2048]{1,0:T(8,128)(2,1)} %get-tuple-element.125.refs_1_, ...), custom_call_target="tpu_custom_call" | custom-call | tf_op jit(solution)/shard_map/hidden/pallas_call | solution.py:584
  453.4 84.0 %hidden_grads.1 = (bf16[1024,512]{1,0:T(8,128)(2,1)}, bf16[1024,512]{1,0:T(8,128)(2,1)}, bf16[512,1024]{1,0:T(8,128)(2,1)}, bf16[2048,2048]{1,0:T(8,128)(2,1)}, ...) custom-call(bf16[1024,128]{1,0:T(8,128)(2,1)} %get-tuple-element.122, ...), custom_call_target="tpu_custom_call" | custom-call | tf_op jit(solution)/shard_map/hidden_grads/pallas_call | solution.py:584
  547.7 2.6 fusion.20.refs_1_
  550.3 5.6 add_convert_fusion.1
  556.0 3.8 fusion.12
  559.8 82.2 %in_grads.1 = (bf16[4,208,2048]{2,1,0:T(8,128)(2,1)}, bf16[8,16,1024]{2,1,0:T(8,128)(2,1)}, bf16[512,1024]{1,0:T(8,128)(2,1)}, bf16[512,1024]{1,0:T(8,128)(2,1)}...) custom-call(bf16[4,208,2048]{2,1,0:T(8,128)(2,1)} %bitcast.411, ...), custom_call_target="tpu_custom_call" | custom-call | tf_op jit(solution)/shard_map/in_grads/pallas_call | solution.py:584
  643.6 4.3 add_convert_fusion.7
  649.4 59.8 %row_grads.1 = (bf16[4,1024,512]{2,1,0:T(8,128)(2,1)}, bf16[4096,256]{1,0:T(8,128)(2,1)}, bf16[8,16,1024]{2,1,0:T(8,128)(2,1)}, bf16[1664,2048]{1,0:T(8,128)(2,1)}, bf16[832,2048]{1,0:T(8,128)(2,1)}) custom-call(bf16[2048,2048]{1,0:T(8,128)(2,1)} %get-tuple-element.144.refs_0_, bf16[512,2048]{1,0:T(8,128)(2,1)} %pad_maximum_fusion.refs_1_, ...), custom_call_target="tpu_custom_call" | custom-call | tf_op jit(solution)/shard_map/row_grads/pallas_call | solution.py:584
  709.2 4.3 fusion.6
  715.5 3.2 add_convert_fusion
  718.8 3.5 fusion.8
  723.8 85.4 %sum_rows.1 = (bf16[4,208,2048]{2,1,0:T(8,128)(2,1)}, bf16[8,16,1024]{2,1,0:T(8,128)(2,1)}, bf16[1024,512]{1,0:T(8,128)(2,1)}, bf16[1024,512]{1,0:T(8,128)(2,1)}...) custom-call(bf16[4,208,2048]{2,1,0:T(8,128)(2,1)} %bitcast.410, ...), custom_call_target="tpu_custom_call" | custom-call | tf_op jit(solution)/shard_map/sum_rows/pallas_call | solution.py:584
  813.7 2.7 multiply_reduce_fusion.2
  819.1 3.8 add_convert_fusion.3
  825.9 2.6 add_convert_fusion.5
  831.8 3.7 fusion.18
  835.4 130.9 %heads.1 = (bf16[832,2048]{1,0:T(8,128)(2,1)}, bf16[64,1024]{1,0:T(8,128)(2,1)}, bf16[256,4096]{1,0:T(8,128)(2,1)}, bf16[256,4096]{1,0:T(8,128)(2,1)}, bf16[896,...) custom-call(bf16[208,2048]{1,0:T(8,128)(2,1)} %get-tuple-element.303, ...), custom_call_target="tpu_custom_call" | custom-call | tf_op jit(solution)/shard_map/heads/pallas_call | solution.py:584
  971.1 3.2 convolution_convert_fusion.1
  986.2 3.4 multiply_reduce_fusion.3
  989.8 4.0 fusion.16.refs_6_
  1009.2 2.5 convert_element_type.1075
  1017.6 93.8 %finish.1 = (bf16[4,256,512]{2,1,0:T(8,128)(2,1)}, bf16[4,256,512]{2,1,0:T(8,128)(2,1)}, bf16[4,128,512]{2,1,0:T(8,128)(2,1)}, bf16[4,128,512]{2,1,0:T(8,128)(2,...) custom-call(bf16[1024,512]{1,0:T(8,128)(2,1)} %fusion.1.refs_0_, ...), custom_call_target="tpu_custom_call" | custom-call | tf_op jit(solution)/shard_map/finish/pallas_call | solution.py:584
  1116.1 8.8 all_gather.3
  1133.9 4.3 slice.381
  1141.8 3.7 slice_convert_fusion
  (310 shorter events, 135.2 us)
Async XLA Ops:
  4.7 7.9 copy-start.48
  12.7 101.0 %copy-start.59 = (f32[832]{0:T(1024)S(1)}, f32[832]{0:T(1024)}, u32[]{:S(2)}) copy-start(f32[832]{0:T(1024)} %multiply_reduce_fusion) | copy-start | bytes 9988
  112.9 14.5 %copy-start.34 = (bf16[8,4,8,128]{3,2,1,0:T(8,128)(2,1)}, bf16[8,4,8,128]{3,2,1,0:T(8,128)(2,1)S(1)}, u32[]{:S(2)}) copy-start(bf16[8,4,8,128]{3,2,1,0:T(8,128)(2,1)S(1)} %get-tuple-element.323) | copy-start | bytes 196612
  119.0 12.2 %copy-start.61 = (s32[832]{0:T(1024)S(1)}, s32[832]{0:T(1024)}, u32[]{:S(2)}) copy-start(s32[832]{0:T(1024)} %get-tuple-element.328) | copy-start | bytes 9988
  119.0 12.1 %copy-start.81 = (s32[64]{0:T(128)S(1)}, s32[64]{0:T(128)}, u32[]{:S(2)}) copy-start(s32[64]{0:T(128)} %compare_select_fusion.1) | copy-start | bytes 772
  119.1 12.2 %copy-start.60 = (s32[832]{0:T(1024)S(1)}, s32[832]{0:T(1024)}, u32[]{:S(2)}) copy-start(s32[832]{0:T(1024)} %get-tuple-element.329) | copy-start | bytes 9988
  119.7 7.8 copy-start.76
  123.9 9.8 copy-start.49
  135.2 6.0 copy-start
  285.3 5.3 copy-start.50
  289.1 524.0 %copy-start.56 = (f32[208]{0:T(256)}, f32[208]{0:T(256)S(1)}, u32[]{:S(2)}) copy-start(f32[208]{0:T(256)S(1)} %fusion.64) | copy-start | bytes 2500
  290.5 87.3 %copy-start.78 = (f32[16]{0:T(128)}, f32[16]{0:T(128)S(1)}, u32[]{:S(2)}) copy-start(f32[16]{0:T(128)S(1)} %get-tuple-element.277) | copy-start | bytes 196
  290.5 87.3 %copy-start.67 = (f32[16]{0:T(128)}, f32[16]{0:T(128)S(1)}, u32[]{:S(2)}) copy-start(f32[16]{0:T(128)S(1)} %fusion.66) | copy-start | bytes 196
  453.4 84.1 %copy-start.11 = (bf16[8,16,1024]{2,1,0:T(8,128)(2,1)S(1)}, bf16[8,16,1024]{2,1,0:T(8,128)(2,1)}, u32[]{:S(2)}) copy-start(bf16[8,16,1024]{2,1,0:T(8,128)(2,1)} %get-tuple-element.136) | copy-start | bytes 786436
  550.3 5.6 copy-start.8
  709.2 4.8 copy-start.23
  813.7 4.2 copy-start.68
  813.7 4.9 copy-start.79
  819.1 5.3 copy-start.30
  819.1 5.3 copy-start.31
  825.9 5.9 copy-start.22
  835.4 133.0 %copy-start.16 = (bf16[64,1024]{1,0:T(8,128)(2,1)S(1)}, bf16[64,1024]{1,0:T(8,128)(2,1)}, u32[]{:S(2)}) copy-start(bf16[64,1024]{1,0:T(8,128)(2,1)} %copy-done.15) | copy-start | bytes 393220
  971.1 43.2 %collective-permute-start.1 = (bf16[512,128]{1,0:T(8,128)(2,1)}, bf16[512,128]{1,0:T(8,128)(2,1)}, u32[]{:S(2)}, u32[]{:S(2)}) collective-permute-start(bf16[512,128]{1,0:T(8,128)(2,1)} %bitcast.65), channel_id=1, source_target_pairs={{0,4},{4,0},{8,12},{12,8},{16,20},{20,16},{24,28},{28,24},{1,5},{5... | collective-permute-start | bytes 393224 | tf_op jit(solution)/shard_map/ppermute | solution.py:1313
  975.1 40.8 %collective-permute-start = (bf16[1024,128]{1,0:T(8,128)(2,1)}, bf16[1024,128]{1,0:T(8,128)(2,1)}, u32[]{:S(2)}, u32[]{:S(2)}) collective-permute-start(bf16[1024,128]{1,0:T(8,128)(2,1)} %bitcast.61), channel_id=1, source_target_pairs={{0,4},{4,0},{8,12},{12,8},{16,20},{20,16},{24,28},{28,24},{1,5},{5... | collective-permute-start | bytes 786440 | tf_op jit(solution)/shard_map/ppermute | solution.py:1313
  984.7 5.0 copy-start.5
  1002.8 4.7 copy-start.42
  1111.4 15.1 %copy-start.40 = (bf16[4,128,512]{2,1,0:T(8,128)(2,1)S(1)}, bf16[4,128,512]{2,1,0:T(8,128)(2,1)}, u32[]{:S(2)}) copy-start(bf16[4,128,512]{2,1,0:T(8,128)(2,1)} %get-tuple-element.195) | copy-start | bytes 1572868
  1112.6 15.8 %copy-start.39 = (bf16[4,128,512]{2,1,0:T(8,128)(2,1)S(1)}, bf16[4,128,512]{2,1,0:T(8,128)(2,1)}, u32[]{:S(2)}) copy-start(bf16[4,128,512]{2,1,0:T(8,128)(2,1)} %get-tuple-element.194) | copy-start | bytes 1572868
  1116.1 13.9 %copy-start.33 = (bf16[4,256,512]{2,1,0:T(8,128)(2,1)S(1)}, bf16[4,256,512]{2,1,0:T(8,128)(2,1)}, u32[]{:S(2)}) copy-start(bf16[4,256,512]{2,1,0:T(8,128)(2,1)} %get-tuple-element.190) | copy-start | bytes 3145732
  1127.5 4.6 copy-start.32
  1133.9 4.3 copy-start.55
  1133.9 7.8 copy-start.14
  (53 other events, 143.3 us)

commit v5 on v4

--- a/solution.py
+++ b/solution.py
@@ -390,41 +390,120 @@
                 self.turned(p, src, dst, c).wait()
 
 
+def by_way(rows, m):
+    return round_up(rows // 2, 16) if m == 4 and rows >= 64 else 0
+
+
 class Parts(Flow):
     reach = "mp"
 
     def result(self, shape, n, m):
-        return shape if len(shape) == 3 else (m, shape[0] // m, shape[1])
+        rows = shape[-2] if len(shape) == 3 else shape[0] // m
+        return (m + 1, rows, shape[-1])
+
+    def block(self, p, src, k):
+        i = self.index(p, k)
+        return src.at[i] if len(src.shape) == 3 else src.at[at(i, src.shape[0] // p.m)]
+
+    def index(self, p, k):
+        return p.col ^ k
+
+    def halves(self, p, dst):
+        first = by_way(dst.shape[1], p.m)
+        return [(1, pl.ds(0, first)), (2, pl.ds(first, dst.shape[1] - first))] if first else []
 
     def each(self, p, src, dst, do):
-        for k in range(1, p.m):
-            target = p.over_mp(k)
-            if len(src.shape) == 3:
-                block = src.at[target[1]]
-            else:
-                block = src.at[at(target[1], src.shape[0] // p.m)]
-            do(p.remote(block, dst.at[k], k, target))
+        halves = self.halves(p, dst)
+        for k in range(1, 3 if halves else p.m):
+            do(p.remote(self.block(p, src, k), dst.at[k], k, p.over_mp(k)))
+
+    def sideways(self, p, src, dst, via, cut):
+        block = self.block(p, src, 3).at[cut]
+        return p.remote(block, dst.at[p.m, cut], p.m + via, p.over_mp(via))
+
+    def onward(self, p, dst, via, cut):
+        return p.remote(dst.at[p.m, cut], dst.at[3, cut], p.m + 2 + via, p.over_mp(3 - via))
+
+    def slots(self, n, m):
+        return m + 5
+
+    def start(self, p, src, dst):
+        for via, cut in self.halves(p, dst):
+            self.sideways(p, src, dst, via, cut).start()
+        self.each(p, src, dst, lambda c: c.start())
+
+    def relay(self, p, src, dst, k):
+        for via, cut in self.halves(p, dst):
+            self.sideways(p, src, dst, via, cut).wait_recv()
+            self.onward(p, dst, via, cut).start()
+
+    def wait(self, p, src, dst):
+        self.each(p, src, dst, lambda c: c.wait())
+        for via, cut in self.halves(p, dst):
+            self.sideways(p, src, dst, via, cut).wait_send()
+            self.onward(p, dst, via, cut).wait()
 
 
 class Swaps(Parts):
-    def each(self, p, src, dst, do):
-        for k in range(1, p.m):
-            do(p.remote(src.at[k], dst.at[k], k, p.over_mp(k)))
+    def __init__(self, axis=0):
+        self.axis = axis
+
+    def result(self, shape, n, m):
+        if len(shape) == 3:
+            return (m + 1,) + shape[1:]
+        return (m + 1, shape[0], shape[1] // m) if self.axis else (m + 1, shape[0] // m, shape[1])
+
+    def block(self, p, src, k):
+        if len(src.shape) == 3:
+            return src.at[k]
+        size = src.shape[self.axis] // p.m
+        cut = pl.ds(k * size, size)
+        return src.at[:, cut] if self.axis else src.at[cut]
 
 
 class Whole(Flow):
     reach = "mp"
-    kept = True
 
     def result(self, shape, n, m):
         return (m * shape[0], shape[1])
 
-    def own(self, p, src, dst):
-        return src, dst.at[at(p.col, src.shape[0])]
-
-    def each(self, p, src, dst, do):
-        for k in range(1, p.m):
-            do(p.remote(src, dst.at[at(p.col, src.shape[0])], k, p.over_mp(k)))
+    def slots(self, n, m):
+        return m + 3
+
+    def spot(self, src, dst, i, cut=None):
+        rows = src.shape[0]
+        if cut is None:
+            return dst.at[at(i, rows)]
+        return dst.at[pl.ds(pl.multiple_of(i * rows + cut[0], 16), cut[1])]
+
+    def halves(self, p, src):
+        first = by_way(src.shape[0], p.m)
+        return [(1, (0, first)), (2, (first, src.shape[0] - first))] if first else []
+
+    def direct(self, p, src, dst, k):
+        return p.remote(src, self.spot(src, dst, p.col), k, p.over_mp(k))
+
+    def onward(self, p, src, dst, via, cut):
+        block = self.spot(src, dst, p.col ^ via, cut)
+        return p.remote(block, block, p.m + via, p.over_mp(3 - via))
+
+    def start(self, p, src, dst):
+        for k in range(1, 3 if self.halves(p, src) else p.m):
+            self.direct(p, src, dst, k).start()
+        p.keep(src, self.spot(src, dst, p.col))
+
+    def relay(self, p, src, dst, k):
+        for via, cut in self.halves(p, src):
+            self.direct(p, src, dst, via).wait_recv()
+            self.onward(p, src, dst, via, cut).start()
+
+    def wait(self, p, src, dst):
+        halves = self.halves(p, src)
+        for k in range(1, 3 if halves else p.m):
+            copy = self.direct(p, src, dst, k)
+            (copy.wait_send if halves else copy.wait)()
+        for via, cut in halves:
+            self.onward(p, src, dst, via, cut).wait()
 
 
 class Swap(Flow):
@@ -715,6 +794,30 @@
     )(gz, w_down, gate, upward, *outputs)
 
 
+def act_feed_forward(inputs, outputs):
+    def body(h_ref, gz_ref, gate_w, up_w, down_w, z, dh2, g_gate, g_up, g_down):
+        h, gz = h_ref[...], gz_ref[...]
+        gate, upward = dot_plain(h, gate_w[...]), dot_plain(h, up_w[...])
+        hidden = glu_value(gate, upward).astype(BF)
+        z[...] = dot_plain(hidden, down_w[...]).astype(BF)
+        g_down[...] = dot_left(hidden, gz).astype(BF)
+        dgate, dup = glu_backward(gate, upward, dot_right(gz, down_w[...]))
+        dgate, dup = dgate.astype(BF), dup.astype(BF)
+        dh2[...] = (dot_right(dgate, gate_w[...]) + dot_right(dup, up_w[...])).astype(BF)
+        g_gate[...] = dot_left(h, dgate).astype(BF)
+        g_up[...] = dot_left(h, dup).astype(BF)
+
+    def whole(ref):
+        return pl.BlockSpec(ref.shape, lambda i: (0, 0))
+
+    pltpu.emit_pipeline(
+        body,
+        grid=(1,),
+        in_specs=[whole(r) for r in inputs],
+        out_specs=[whole(r) for r in outputs],
+    )(*inputs, *outputs)
+
+
 def attend_forward(inputs, outputs):
     query, keys, values, seg_q, seg_k = inputs
     probs, mixed = outputs
@@ -804,43 +907,115 @@
     return lambda inputs, outputs: body([inputs[0].at[pl.ds(first, count)]] + inputs[1:], outputs)
 
 
+def add_pairs(pairs, outputs):
+    (rows, width), count = outputs[0].shape, len(outputs)
+
+    def body(*refs):
+        for k in range(count):
+            refs[2 * count + k][...] = add(refs[2 * k][...], refs[2 * k + 1][...])
+
+    block = pl.BlockSpec((tile(rows, 256), width), lambda i: (i, 0))
+    pltpu.emit_pipeline(
+        body,
+        grid=(rows // tile(rows, 256),),
+        in_specs=[block] * (2 * count),
+        out_specs=[block] * count,
+    )(*[ref for pair in pairs for ref in pair], *outputs)
+
+
 class Halves:
-    def __init__(self, whole, axis):
-        self.whole, self.axis = whole, axis
-
-    def take(self, got):
-        top, low = jnp.split(self.whole, 2, axis=1 - self.axis)
-        t, b = jnp.split(top, 4, axis=self.axis), jnp.split(low, 4, axis=self.axis)
-        self.top, self.next_y = add(t[0], got[0]), add(t[2], got[1])
-        self.low, self.next_x = add(b[0], got[2]), add(b[1], got[3])
+    def __init__(self, axis):
+        self.axis = axis
+
+    def settle(self, got):
+        for name, value in vars(self).items():
+            if name != "axis" and isinstance(value, int):
+                setattr(self, name, got[value])
+
+    def first(self, kernel, whole):
+        self.whole = whole
+        self.parts = kernel.flow(First(self.axis), whole)
 
     def second(self, kernel):
-        self.from_y = kernel.flow(Swap(2), self.next_y)
-        self.from_x = kernel.flow(Swap(1), self.next_x)
-
-    def total(self, got):
-        return jnp.concatenate(
-            [add(self.top, got[self.from_y]), add(self.low, got[self.from_x])], axis=1 - self.axis
-        )
+        axis = self.axis
+
+        def take(inputs, outputs):
+            whole, parts = inputs
+            width, deep = whole.shape[axis] // 4, whole.shape[1 - axis] // 2
+
+            def part(half, k):
+                block, deeps = pl.ds(k * width, width), pl.ds(half * deep, deep)
+                return whole.at[deeps, block] if axis else whole.at[block, deeps]
+
+            own = [part(0, 0), part(0, 2), part(1, 0), part(1, 1)]
+            add_pairs([(own[k], parts.at[k]) for k in range(4)], outputs)
+
+        like = kernel.shape_of(self.parts).shape[1:]
+        self.top, next_y, self.low, next_x = kernel.job(take, [self.whole, self.parts], [like] * 4)
+        self.from_y = kernel.flow(Swap(2), next_y)
+        self.from_x = kernel.flow(Swap(1), next_x)
+
+    def total(self, kernel):
+        axis = self.axis
+        rows, width = kernel.shape_of(self.top).shape
+
+        def join(inputs, outputs):
+            top, low, from_y, from_x = inputs
+            halves = [(top, from_y), (low, from_x)]
+            for k, pair in enumerate(halves):
+                spot = pl.ds(k * rows, rows) if axis else (slice(None), pl.ds(k * width, width))
+                add_pairs([pair], [outputs[0].at[spot]])
+
+        shape = (2 * rows, width) if axis else (rows, 2 * width)
+        return kernel.job(join, [self.top, self.low, self.from_y, self.from_x], [shape])
 
 
 class Direct:
-    def __init__(self, whole, axis):
-        parts = jnp.split(whole, lax.axis_size("mp"), axis=axis)
+    def __init__(self, axis):
+        self.axis = axis
+
+    def settle(self, got):
+        if isinstance(self.whole, int):
+            self.whole = got[self.whole]
+
+    def first(self, kernel, whole):
+        self.whole = whole
+
+    def second(self, kernel):
+        return None
+
+    def total(self, kernel):
+        parts = jnp.split(self.whole, lax.axis_size("mp"), axis=self.axis)
         total = parts[0].astype(F32)
         for k in range(1, len(parts)):
             pairs = [(i, i ^ k) for i in range(len(parts))]
             total = total + lax.ppermute(parts[k], "mp", pairs).astype(F32)
-        self.sum = total.astype(BF)
-
-    def take(self, got):
-        return None
-
-    def second(self, kernel):
-        return None
-
-    def total(self, got):
-        return self.sum
+        return total.astype(BF)
+
+
+def project_rows(first, heads, inputs, outputs):
+    x, gain, w_in = inputs
+    rows, depth = x.shape
+    block = tile(rows, 416)
+
+    def body(x_ref, gain_ref, w_ref, normed_ref, *refs):
+        normed = rms_gain(x_ref[...].astype(F32), gain_ref[:1]).astype(BF)
+        normed_ref[...] = normed
+        for k in range(heads + 2):
+            refs[k][...] = dot_plain(normed, w_ref[:, k * HD : (k + 1) * HD]).astype(BF)
+
+    spots = [o.at[pl.ds(first, rows)] for o in outputs[1:]]
+    pltpu.emit_pipeline(
+        body,
+        grid=(rows // block,),
+        in_specs=[
+            pl.BlockSpec((block, depth), lambda i: (i, 0)),
+            pl.BlockSpec(gain.shape, lambda i: (0, 0)),
+            pl.BlockSpec(w_in.shape, lambda i: (0, 0)),
+        ],
+        out_specs=[pl.BlockSpec((block, depth), lambda i: (i, 0))]
+        + [pl.BlockSpec((block, HD), lambda i: (i, 0))] * (heads + 2),
+    )(x, gain, w_in, outputs[0], *spots)
 
 
 def local(
@@ -906,6 +1081,8 @@
     def columns_first(array):
         return array.reshape(array.shape[0], n, -1).transpose(1, 0, 2)
 
+    even = few % lanes == 0 and d_act % lanes == 0
+
     smalls = [pre_gain_attn, pre_gain_ffn, act_gain_attn, act_gain_ffn, act_embed, action_input]
     small = jnp.concatenate([lane_rows(a) for a in smalls], axis=0)
     ints = jnp.pad(jnp.stack([slot_item, valid_dims]), ((0, 6), (0, lanes - slot_count)))
@@ -958,7 +1135,10 @@
         w_q_pre = kernel.flow(Line(by_rows(d_pre), (wide, split)), pre_query)
         w_q_act = kernel.flow(Line(by_rows(d_act), (narrow, split)), act_query)
     w_out_pre = kernel.flow(Line(by_columns(d_pre), (split, wide)), pre_output)
-    w_out_act = kernel.flow(Line(by_lead, (n, split, d_act)), act_output)
+    if even:
+        w_out_act = kernel.flow(Line(by_columns(d_act), (split, narrow)), act_output)
+    else:
+        w_out_act = kernel.flow(Line(by_lead, (n, split, d_act)), act_output)
     cot_all = kernel.flow(Line(by_lead, (n, slot_count * aq, narrow)), cot_rows)
     lines += [small, ints, w_q_pre, w_q_act, w_out_pre, w_out_act, cot_all]
     for k in range(1, half):
@@ -983,7 +1163,8 @@
     act_all = smalls_all[5].reshape(n * slot_count, steps, dims_count)
     slot_all = ints[:, 0, :slot_count].reshape(-1)
     valid_all = ints[:, 1, :slot_count].reshape(-1)
-    w_out_act = w_out_act.transpose(1, 0, 2).reshape(split, narrow)
+    if not even:
+        w_out_act = w_out_act.transpose(1, 0, 2).reshape(split, narrow)
 
     mine = (slot_all == me).astype(F32)
     valid = jnp.sum(mine * valid_all.astype(F32))
@@ -991,15 +1172,8 @@
     act_in = jnp.sum(mine[:, None, None] * act_all.astype(F32), axis=0).astype(BF) * dims_mask
     act_in = pad_rows(act_in, acts)
 
-    x_pre = pad_rows(prefix_input, rows).astype(F32)
-    h1_pre = rms_gain(x_pre, gain_pa).astype(BF)
+    x_pre = pad_rows(prefix_input, rows)
     x_act = dot_plain(act_in, embed)
-    h1_act = rms_gain(x_act, gain_aa).astype(BF)
-    into = jnp.concatenate(
-        [dot_plain(h1_pre, w_in_pre).astype(BF), dot_plain(h1_act, w_in_act).astype(BF)], axis=0
-    )
-    query = [into[:, h * HD : (h + 1) * HD] for h in range(heads)]
-    keys, values = into[:, split : split + HD], into[:, split + HD :]
     last, never = 1 << 10, 1 << 20
     seg = jnp.pad(segments[0], (0, rows - length), constant_values=never)
     seg_q = jnp.concatenate([jnp.minimum(seg, last), jnp.full((acts,), last, jnp.int32)])
@@ -1009,7 +1183,6 @@
     seg_k = jnp.broadcast_to(seg_k[None, :], (8, total_rows))
 
     gz_pre = own(pad_rows(prefix_cotangent, rows), rq)
-    even = few % lanes == 0 and d_act % lanes == 0
     if not even:
         act_weights = jnp.concatenate(
             [
@@ -1052,6 +1225,19 @@
     kernel = Kernel(2)
     gate_own = kernel.flow(Columns(), pre_gate)
     up_own = kernel.flow(Columns(), pre_up, now=False)
+    h1_pre, *into = kernel.job(
+        functools.partial(project_rows, 0, heads),
+        [x_pre, jnp.broadcast_to(gain_pa, (8, wide)), w_in_pre],
+        [(rows, wide)] + [(total_rows, HD)] * (heads + 2),
+    )
+    h1_act = kernel.new_output((acts, narrow), BF)
+    kernel.job(
+        functools.partial(project_rows, rows, heads),
+        [x_act, jnp.broadcast_to(gain_aa, (8, narrow)), w_in_act],
+        [],
+        into=[h1_act] + into,
+    )
+    query, keys, values = into[:heads], into[heads], into[heads + 1]
     probs, mixed = [], []
     for h in range(heads):
         p, o = kernel.job(
@@ -1061,29 +1247,32 @@
         )
         probs.append(p)
         mixed.append(o)
-        if h == 0:
-            kernel.go(up_own)
     y_pre = kernel.job(project(0, rows), mixed + [w_out_pre], [(rows, wide)])
     y_act = kernel.job(project(rows, acts), mixed + [w_out_act], [(acts, narrow)])
     y_pre_parts = kernel.flow(Parts(), y_pre)
     y_act_parts = kernel.flow(Parts(), y_act)
     kernel.ready(gate_own)
+    kernel.go(up_own)
     w_gate = kernel.flow(Pass(1), gate_own)
+    kernel.relay(y_pre_parts, 1)
+    kernel.relay(y_act_parts, 1)
+    kernel.relay(w_gate, 1)
     down_own = kernel.flow(Rows(), pre_down)
-    kernel.relay(w_gate, 1)
     kernel.relay(w_gate, 2)
     got = kernel.call("attend")
     probs, mixed = [got[p] for p in probs], [got[o] for o in mixed]
+    query, keys, values = [got[q] for q in query], got[keys], got[values]
+    h1_pre, h1_act = got[h1_pre], got[h1_act]
     up_own, down_own, w_gate = got[up_own], got[down_own], got[w_gate]
 
-    def summed(first, parts):
+    def summed(first, parts, count=None):
         value = first.astype(F32)
-        for k in range(1, parts.shape[0]):
+        for k in range(1, count or parts.shape[0]):
             value = value + parts[k].astype(F32)
         return value
 
-    x2_pre = own(x_pre, rq) + summed(own(got[y_pre], rq), got[y_pre_parts])
-    x2_act = own(x_act, aq) + summed(own(got[y_act], aq), got[y_act_parts])
+    x2_pre = own(x_pre, rq).astype(F32) + summed(own(got[y_pre], rq), got[y_pre_parts], m)
+    x2_act = own(x_act, aq) + summed(own(got[y_act], aq), got[y_act_parts], m)
     h2_pre = rms_gain(x2_pre, gain_pf).astype(BF)
     h2_act = rms_gain(x2_act, gain_af).astype(BF)
 
@@ -1134,7 +1323,8 @@
     else:
         act_all_w = [kernel.flow(Pass(0), act_own[0].reshape(n * 3 * d_act, few))]
     g_down = kernel.job(products_left, [hidden, gz_pre_all], [(units, wide)])
-    first = kernel.flow(First(0), g_down) if m == 4 else None
+    down_sum, gate_sum, up_sum = summing(0), summing(1), summing(1)
+    down_sum.first(kernel, g_down)
     z_p = kernel.job(products_plain, [hidden, w_down], [(items, wide)])
     z_p_core = kernel.flow(Core(), z_p)
     for k in (1, 2):
@@ -1145,8 +1335,7 @@
     )
     got = kernel.call("hidden_grads")
     dgate, dup = got[dgate], got[dup]
-    g_down = summing(got[g_down], 0)
-    g_down.take(got[first] if m == 4 else None)
+    down_sum.settle(got)
 
     def pair_sum(parts, other):
         return add(parts[: other.shape[0]], other).reshape(half, -1, other.shape[1])
@@ -1163,39 +1352,33 @@
     cot_all = cot_all.reshape(n * slot_count, aq * narrow)
     gz_act_all = dot_plain(match, cot_all).astype(BF).reshape(n * aq, narrow)
     gz_act = lax.dynamic_slice_in_dim(gz_act_all, me * aq, aq, 0)
-    gate_a = dot_plain(h2_act, act_gate_w)
-    up_a = dot_plain(h2_act, act_up_w)
-    hid_a = glu_value(gate_a, up_a).astype(BF)
-    z_a = dot_plain(hid_a, act_down_w).astype(BF)
-    dgate_a, dup_a = glu_backward(gate_a, up_a, dot_right(gz_act_all, act_down_w))
-    dgate_a, dup_a = dgate_a.astype(BF), dup_a.astype(BF)
-    dh2_a = (dot_right(dgate_a, act_gate_w) + dot_right(dup_a, act_up_w)).astype(BF)
-    act_back = [dot_left(h2_act, dgate_a), dot_left(h2_act, dup_a)]
-    if even:
-        g_down_a = dot_left(hid_a, gz_act_all).astype(BF).reshape(m, few, narrow)
-    else:
-        act_back.append(dot_left(gz_act_all, hid_a))
-    act_back = [jnp.concatenate(act_back, axis=0).astype(BF)]
-    act_back = [jnp.stack(jnp.split(a, m, axis=1)) for a in act_back]
-    if even:
-        act_back.append(g_down_a)
-
     kernel = Kernel(6)
-    z_p_parts, z_a = kernel.flow(Chips(), z_p), kernel.flow(EachRows(), z_a)
-    g_down.second(kernel)
+    z_p_parts = kernel.flow(Chips(), z_p)
+    down_sum.second(kernel)
     g_gate = kernel.job(products_left, [h2_pre, dgate], [(wide, units)])
-    first = kernel.flow(First(1), g_gate) if m == 4 else None
+    gate_sum.first(kernel, g_gate)
+    z_a, dh2_a, g_gate_a, g_up_a, g_down_a = kernel.job(
+        act_feed_forward,
+        [h2_act, gz_act_all, act_gate_w, act_up_w, act_down_w],
+        [(n * aq, narrow)] * 2 + [(narrow, m * few)] * 2 + [(m * few, narrow)],
+    )
+    z_a = kernel.flow(EachRows(), z_a)
     g_up = kernel.job(products_left, [h2_pre, dup], [(wide, units)])
     got = kernel.call("in_grads")
-    g_gate, g_up = summing(got[g_gate], 1), got[g_up]
-    g_gate.take(got[first] if m == 4 else None)
-    g_down = g_down.total(got)
+    dh2_a, g_gate_a, g_up_a, g_down_a = [got[o] for o in (dh2_a, g_gate_a, g_up_a, g_down_a)]
+    act_back = [g_gate_a, g_up_a, g_down_a]
+    if not even:
+        act_back = jnp.concatenate([g_gate_a, g_up_a, g_down_a.T], axis=0)
+        act_back = [jnp.stack(jnp.split(act_back, m, axis=1))]
+    down_sum.settle(got)
+    gate_sum.settle(got)
+    g_up = got[g_up]
     out_pre = (x2_pre + summed(z_p[0], got[z_p_parts])).astype(BF)
     out_act = (x2_act + jnp.sum(got[z_a].astype(F32), axis=0)).astype(BF)
 
     kernel = Kernel(7)
-    first = kernel.flow(First(1), g_up) if m == 4 else None
-    grad_down = kernel.flow(Columns(), g_down)
+    up_sum.first(kernel, g_up)
+    grad_down = kernel.flow(Columns(), down_sum.total(kernel))
     out_act = kernel.flow(Line(), out_act)
     dh2_p = kernel.job(products_right, [dgate, w_gate, dup, w_up], [(items, wide)])
     dh2_p_core = kernel.flow(Core(), dh2_p)
@@ -1203,19 +1386,25 @@
         kernel.relay(out_act, k)
     got = kernel.call("row_grads")
     out_act = got[out_act].reshape(n * aq, narrow)
-    g_up = summing(g_up, 1)
-    g_up.take(got[first] if m == 4 else None)
+    up_sum.settle(got)
     grad_down = got[grad_down].astype(F32)
     dh2_p = pair_sum(got[dh2_p], got[dh2_p_core])
 
     kernel = Kernel(8)
     dh2_p_parts, dh2_a = kernel.flow(Chips(), dh2_p), kernel.flow(EachRows(), dh2_a)
-    g_gate.second(kernel)
-    g_up.second(kernel)
-    act_parts = [kernel.flow(Swaps(), a) for a in act_back]
+    act_parts = [kernel.flow(Swaps(axis), a) for axis, a in zip((1, 1, 0), act_back)]
+    gate_sum.second(kernel)
+    up_sum.second(kernel)
+    for flow in act_parts:
+        kernel.relay(flow, 1)
     got = kernel.call("sum_rows")
-    g_gate, g_up = g_gate.total(got), g_up.total(got)
-    act_sum = [summed(a[0], got[b]).astype(BF) for a, b in zip(act_back, act_parts)]
+    gate_sum.settle(got)
+    up_sum.settle(got)
+    if even:
+        act_back = [g_gate_a[:, :few], g_up_a[:, :few], g_down_a[:few]]
+    else:
+        act_back = [act_back[0][0]]
+    act_sum = [summed(a, got[b], m).astype(BF) for a, b in zip(act_back, act_parts)]
     if not even:
         act_sum = jnp.concatenate(act_sum, axis=0).reshape(3, n, d_act, few)
         act_sum = [act_sum.transpose(1, 0, 2, 3).reshape(n, 3 * d_act, few)]
@@ -1242,10 +1431,12 @@
     kernel = Kernel(9)
     gy_pre = kernel.flow(Whole(), gx2_pre.astype(BF))
     gy_act = kernel.flow(Whole(), gx2_act.astype(BF))
-    grad_gate = kernel.flow(Rows(), g_gate)
+    grad_gate = kernel.flow(Rows(), gate_sum.total(kernel))
+    kernel.relay(gy_pre, 1)
+    kernel.relay(gy_act, 1)
     kernel.ready(gy_pre)
     kernel.ready(gy_act)
-    grad_up = kernel.flow(Rows(), g_up)
+    grad_up = kernel.flow(Rows(), up_sum.total(kernel))
     gmix = kernel.job(both_rows, [gy_pre, w_out_pre, gy_act, w_out_act], [(total_rows, split)])
     *gq, gkv, shares = kernel.job(
         functools.partial(attend_backward, heads),
@@ -1262,11 +1453,10 @@
     )
     gh1_act_parts = kernel.flow(Parts(), gh1_act)
     if even:
-        both = [kernel.flow(Rows(), act_sum[0][k * narrow : (k + 1) * narrow]) for k in (0, 1)]
-        act_sum = both + [kernel.flow(Columns(), act_sum[1])]
+        act_sum = [kernel.flow(k(), a) for k, a in zip((Rows, Rows, Columns), act_sum)]
     else:
         act_sum = [kernel.flow(Each(), act_sum[0])]
-    out_act = kernel.flow(Whole(), out_act)
+    late = [share_parts, gh1_pre_parts, gh1_act_parts]
     g_out_pre = g_out_act = g_q_pre = g_q_act = None
     for h in range(heads):
         heads_columns = (slice(None), pl.ds(h * HD, HD))
@@ -1280,6 +1470,9 @@
         g_q_pre = grads(of_pre, heads_columns, [h1_pre, gq[h]], (wide, split), g_q_pre)
         g_out_act = grads(of_act, heads_columns, [gy_act, mixed[h]], (narrow, split), g_out_act)
         g_q_act = grads(of_act, heads_columns, [h1_act, gq[h]], (narrow, split), g_q_act)
+        if h == 0:
+            for flow in late:
+                kernel.relay(flow, 1)
     core_grads = [g[0] for g in (g_out_pre, g_q_pre, g_out_act, g_q_act)]
     from_core = [kernel.flow(CoreRows(), g) for g in core_grads]
     got = kernel.call("heads")
@@ -1293,15 +1486,15 @@
         return blocks.reshape(half * size, array.shape[1])
 
     chip_grads = [add(of_core(got[g], here), got[f]) for g, f in zip(core_grads, from_core)]
-    shares, gh1_pre, gh1_act, out_act = got[shares], got[gh1_pre], got[gh1_act], got[out_act]
-    gkv_sum = summed(lax.dynamic_index_in_dim(shares, col, 0, False), got[share_parts])
-    gh1_pre = summed(own(gh1_pre, rq), got[gh1_pre_parts])
-    gh1_act = summed(own(gh1_act, aq), got[gh1_act_parts])
+    shares, gh1_pre, gh1_act = got[shares], got[gh1_pre], got[gh1_act]
+    gkv_sum = summed(lax.dynamic_index_in_dim(shares, col, 0, False), got[share_parts], m)
+    gh1_pre = summed(own(gh1_pre, rq), got[gh1_pre_parts], m)
+    gh1_act = summed(own(gh1_act, aq), got[gh1_act_parts], m)
     act_sum = [got[a].astype(F32) for a in act_sum]
     gkv_sum = gkv_sum.astype(BF)
     g_kv_pre = dot_left(h1_pre, gkv_sum[:rows]).astype(BF)
     g_kv_act = dot_left(h1_act, gkv_sum[rows:]).astype(BF)
-    gxn_pre, g_gain_pa = norm_backward(own(x_pre, rq), gain_pa, gh1_pre)
+    gxn_pre, g_gain_pa = norm_backward(own(x_pre, rq).astype(F32), gain_pa, gh1_pre)
     gxn_act, g_gain_aa = norm_backward(own(x_act, aq), gain_aa, gh1_act)
     grad_pre = (gx2_pre + gxn_pre).astype(BF)
     gxa = (gx2_act + gxn_act).astype(BF)
@@ -1325,9 +1518,14 @@
     chip_parts = [kernel.flow(ChipRows(), g) for g in chip_grads]
     prefix_grad = kernel.flow(Whole(), grad_pre)
     prefix_output = kernel.flow(Whole(), out_pre)
+    out_act = kernel.flow(Whole(), out_act)
     act_grad = kernel.flow(World(), act_grad)
     tiny = kernel.flow(Spread(), tiny)
+    kernel.relay(prefix_grad, 1)
+    kernel.relay(prefix_output, 1)
+    kernel.relay(out_act, 1)
     got = kernel.call("finish")
+    out_act = got[out_act]
 
     def chip_sum(own_parts, parts):
         size = own_parts.shape[0] // half

time: 1160 us -> 1100 us (0.948)
  other arithmetic: 129 us -> 94.5 us
  matrix products: 25.8 us -> 6.2 us
  local copies, waits for them, and re-layouts: 55.9 us -> 37.6 us
  Pallas kernels: 925 us -> 938 us
    convert_element_type x14 -> x8, other arithmetic: 39 us -> 21 us  [add(): return (left.astype(F32) + right.astype(F32)).astype(BF)]
    pallas_call x10, Pallas kernels: 925 us -> 938 us  [call(): pl.pallas_call(kernel, out_shape=self.outputs, in_specs=[HBM] * takes, ou...]
  transfers between devices with their start and end apart: 2 -> 2, of which waited for: 0 -> 0; matrix products, arithmetic and copies ran while one was open for 4% -> 3% of each run, Pallas kernels for 0% -> 0%
where the time goes in v5:
time: 1100 us; the launch traced here: 1090 us
  Pallas kernels  938 us (85%)
  other arithmetic  94.5 us (9%)
  local copies, waits for them, and re-layouts  37.6 us (3%)
    pallas_call x10, Pallas kernels, call(): pl.pallas_call(kernel, out_shape=self.outputs, in_specs=[HBM] * takes, ou...  938 us
  transfers between devices with their start and end apart: 2, of which 0 were waited for; matrix products, arithmetic and copies ran while one was open for 3% of the time, Pallas kernels for 0%

profile of v5, /device:TPU:0, one launch (start us, length us, event | category | flops | bytes accessed | tf_op | source)
XLA Modules:
  0.0 1088.2 jit_solution(16381548686186835304)
XLA Ops:
  10.7 86.5 %gather.1 = (bf16[2048,1024]{1,0:T(8,128)(2,1)}, bf16[1024,1024]{1,0:T(8,128)(2,1)}, bf16[8,128,128]{2,1,0:T(8,128)(2,1)}, s32[8,8,128]{2,1,0:T(8,128)}, bf16[51...) custom-call(bf16[256,128]{1,0:T(8,128)(2,1)} %fusion.24.refs_0_, ...), custom_call_target="tpu_custom_call" | custom-call | tf_op jit(solution)/shard_map/gather/pallas_call | solution.py:663
  105.5 2.3 pad_dynamic-slice_fusion.refs_0_
  107.8 2.0 pad.48.refs_2_
  113.6 156.6 %attend.1 = (bf16[2048,512]{1,0:T(8,128)(2,1)}, bf16[2048,512]{1,0:T(8,128)(2,1)}, bf16[832,2048]{1,0:T(8,128)(2,1)}, bf16[896,256]{1,0:T(8,128)(2,1)}, bf16[896...) custom-call(bf16[256,4096]{1,0:T(8,128)(2,1)} %refs_0_.1, ...), custom_call_target="tpu_custom_call" | custom-call | tf_op jit(solution)/shard_map/attend/pallas_call | solution.py:663
  270.3 3.4 multiply_reduce_fusion.3
  277.1 85.5 %spread.1 = (bf16[8,208,2048]{2,1,0:T(8,128)(2,1)}, bf16[8,16,1024]{2,1,0:T(8,128)(2,1)}, bf16[2048,2048]{1,0:T(8,128)(2,1)}, bf16[1024,128]{1,0:T(8,128)(2,1)},...) custom-call(bf16[208,2048]{1,0:T(8,128)(2,1)} %multiply_convert_fusion.refs_0_, ...), custom_call_target="tpu_custom_call" | custom-call | tf_op jit(solution)/shard_map/spread/pallas_call | solution.py:663
  362.7 75.6 %hidden.1 = (bf16[8,208,2048]{2,1,0:T(8,128)(2,1)}, bf16[2048,2048]{1,0:T(8,128)(2,1)}, bf16[1664,2048]{1,0:T(8,128)(2,1)}, bf16[1664,2048]{1,0:T(8,128)(2,1)}, bf16[1664,2048]{1,0:T(8,128)(2,1)}) custom-call(bf16[208,2048]{1,0:T(8,128)(2,1)} %pad_dynamic-slice_fusion.refs_0_, bf16[512,2048]{1,0:T(8,128)(2,1)} %get-tuple-element.142.refs_1_, ...), custom_call_target="tpu_custom_call" | custom-call | tf_op jit(solution)/shard_map/hidden/pallas_call | solution.py:663
  438.3 84.1 %hidden_grads.1 = (bf16[1024,512]{1,0:T(8,128)(2,1)}, bf16[1024,512]{1,0:T(8,128)(2,1)}, bf16[512,1024]{1,0:T(8,128)(2,1)}, bf16[2048,2048]{1,0:T(8,128)(2,1)}, ...) custom-call(bf16[1024,128]{1,0:T(8,128)(2,1)} %get-tuple-element.139, ...), custom_call_target="tpu_custom_call" | custom-call | tf_op jit(solution)/shard_map/hidden_grads/pallas_call | solution.py:663
  522.3 6.5 add_convert_fusion.1
  528.9 82.1 %in_grads.1 = (bf16[4,208,2048]{2,1,0:T(8,128)(2,1)}, bf16[512,1024]{1,0:T(8,128)(2,1)}, bf16[512,1024]{1,0:T(8,128)(2,1)}, bf16[512,1024]{1,0:T(8,128)(2,1)}, b...) custom-call(bf16[4,208,2048]{2,1,0:T(8,128)(2,1)} %bitcast.344, ...), custom_call_target="tpu_custom_call" | custom-call | tf_op jit(solution)/shard_map/in_grads/pallas_call | solution.py:663
  612.5 64.7 %row_grads.1 = (bf16[4,1024,512]{2,1,0:T(8,128)(2,1)}, bf16[512,2048]{1,0:T(8,128)(2,1)}, bf16[4096,256]{1,0:T(8,128)(2,1)}, bf16[8,16,1024]{2,1,0:T(8,128)(2,1)...) custom-call(bf16[2048,2048]{1,0:T(8,128)(2,1)} %get-tuple-element.162.refs_0_.refs_7_, ...), custom_call_target="tpu_custom_call" | custom-call | tf_op jit(solution)/shard_map/row_grads/pallas_call | solution.py:663
  677.3 6.5 add_convert_fusion
  683.8 84.7 %sum_rows.1 = (bf16[4,208,2048]{2,1,0:T(8,128)(2,1)}, bf16[8,16,1024]{2,1,0:T(8,128)(2,1)}, bf16[5,1024,128]{2,1,0:T(8,128)(2,1)}, bf16[5,1024,128]{2,1,0:T(8,12...) custom-call(bf16[4,208,2048]{2,1,0:T(8,128)(2,1)} %bitcast.345, ...), custom_call_target="tpu_custom_call" | custom-call | tf_op jit(solution)/shard_map/sum_rows/pallas_call | solution.py:663
  768.6 2.2 fusion.15.refs_22_
  770.8 2.0 fusion.16.refs_21_
  772.8 2.0 fusion.17.refs_20_
  774.9 3.6 multiply_reduce_fusion.1
  781.8 5.6 fusion.10
  787.4 124.4 %heads.1 = (bf16[832,2048]{1,0:T(8,128)(2,1)}, bf16[64,1024]{1,0:T(8,128)(2,1)}, bf16[2048,512]{1,0:T(8,128)(2,1)}, bf16[256,4096]{1,0:T(8,128)(2,1)}, bf16[2048...) custom-call(bf16[208,2048]{1,0:T(8,128)(2,1)} %get-tuple-element.317, ...), custom_call_target="tpu_custom_call" | custom-call | tf_op jit(solution)/shard_map/heads/pallas_call | solution.py:663
  916.9 3.2 convolution_convert_fusion.1
  928.8 3.0 fusion.8
  932.8 4.4 fusion.4.refs_6_
  944.7 2.3 convert_element_type.805
  950.2 2.5 convert_element_type.803
  952.7 2.5 convert_element_type.804
  958.6 93.9 %finish.1 = (bf16[4,256,512]{2,1,0:T(8,128)(2,1)}, bf16[4,256,512]{2,1,0:T(8,128)(2,1)}, bf16[4,128,512]{2,1,0:T(8,128)(2,1)}, bf16[4,128,512]{2,1,0:T(8,128)(2,...) custom-call(bf16[1024,512]{1,0:T(8,128)(2,1)} %fusion.1.refs_0_, ...), custom_call_target="tpu_custom_call" | custom-call | tf_op jit(solution)/shard_map/finish/pallas_call | solution.py:663
  1057.2 9.7 all_gather.3
  1071.9 2.3 fusion.13
  1074.1 2.0 copy.88
  1076.2 2.1 convert_add_fusion.20
  1078.3 2.0 slice.316
  1083.5 3.7 slice_convert_fusion
  (209 shorter events, 72.8 us)
Async XLA Ops:
  0.7 100.5 %copy-start.44 = (s32[1,816]{1,0:T(1,128)S(1)}, s32[1,816]{1,0:T(1,128)}, u32[]{:S(2)}) copy-start(s32[1,816]{1,0:T(1,128)} %param.30) | copy-start | bytes 9796
  7.8 2.9 copy-start.35
  104.3 171.0 %copy-start.30 = (f32[1024]{0:T(1024)}, f32[1024]{0:T(1024)S(1)}, u32[]{:S(2)}) copy-start(f32[1024]{0:T(1024)S(1)} %fusion.36) | copy-start | bytes 12292
  104.4 8.0 copy-start.32
  110.0 160.3 %copy-start.29 = (bf16[50,32]{1,0:T(8,128)(2,1)}, bf16[50,32]{1,0:T(8,128)(2,1)S(1)}, u32[]{:S(2)}) copy-start(bf16[50,32]{1,0:T(8,128)(2,1)S(1)} %convert_multiply_fusion.4) | copy-start | bytes 9604
  270.3 3.4 copy-start.34
  273.7 501.1 %copy-start.1 = (f32[208,2048]{1,0:T(8,128)}, f32[208,2048]{1,0:T(8,128)S(1)}, u32[]{:S(2)}) copy-start(f32[208,2048]{1,0:T(8,128)S(1)} %get-tuple-element.314) | copy-start | bytes 5111812
  273.7 501.1 %copy-start.36 = (f32[208]{0:T(256)}, f32[208]{0:T(256)S(1)}, u32[]{:S(2)}) copy-start(f32[208]{0:T(256)S(1)} %fusion.39) | copy-start | bytes 2500
  275.3 503.7 %copy-start.41 = (f32[16]{0:T(128)}, f32[16]{0:T(128)S(1)}, u32[]{:S(2)}) copy-start(f32[16]{0:T(128)S(1)} %fusion.41) | copy-start | bytes 196
  768.5 6.3 copy-start.10
  774.8 4.2 copy-start.26
  774.8 4.2 copy-start.31
  787.4 126.5 %copy-start.12 = (bf16[64,1024]{1,0:T(8,128)(2,1)S(1)}, bf16[64,1024]{1,0:T(8,128)(2,1)}, u32[]{:S(2)}) copy-start(bf16[64,1024]{1,0:T(8,128)(2,1)} %get-tuple-element.198.refs_26_.refs_30_) | copy-start | bytes 393220
  916.5 38.7 %collective-permute-start.1 = (bf16[512,128]{1,0:T(8,128)(2,1)}, bf16[512,128]{1,0:T(8,128)(2,1)}, u32[]{:S(2)}, u32[]{:S(2)}) collective-permute-start(bf16[512,128]{1,0:T(8,128)(2,1)} %bitcast.49), channel_id=1, source_target_pairs={{0,4},{4,0},{8,12},{12,8},{16,20},{20,16},{24,28},{28,24},{1,5},{5... | collective-permute-start | bytes 393224 | tf_op jit(solution)/shard_map/ppermute | solution.py:1506
  920.9 36.0 %collective-permute-start = (bf16[1024,128]{1,0:T(8,128)(2,1)}, bf16[1024,128]{1,0:T(8,128)(2,1)}, u32[]{:S(2)}, u32[]{:S(2)}) collective-permute-start(bf16[1024,128]{1,0:T(8,128)(2,1)} %bitcast.45), channel_id=1, source_target_pairs={{0,4},{4,0},{8,12},{12,8},{16,20},{20,16},{24,28},{28,24},{1,5},{5... | collective-permute-start | bytes 786440 | tf_op jit(solution)/shard_map/ppermute | solution.py:1506
  928.8 3.1 copy-start.40
  928.8 3.1 copy-start.2
  928.8 3.5 copy-start.3
  928.8 4.0 copy-start.4
  928.8 4.0 copy-start.37
  928.8 4.0 copy-start.39
  932.8 4.4 copy-start.18
  941.7 3.0 copy-start.7
  944.7 3.0 copy-start.25
  944.7 3.9 copy-start.24
  944.7 4.7 copy-start.23
  947.0 3.2 copy-start.9
  952.7 4.1 copy-start.15
  1052.5 15.9 %copy-start.21 = (bf16[4,128,512]{2,1,0:T(8,128)(2,1)S(1)}, bf16[4,128,512]{2,1,0:T(8,128)(2,1)}, u32[]{:S(2)}) copy-start(bf16[4,128,512]{2,1,0:T(8,128)(2,1)} %get-tuple-element.229) | copy-start | bytes 1572868
  1053.6 16.6 %copy-start.20 = (bf16[4,128,512]{2,1,0:T(8,128)(2,1)S(1)}, bf16[4,128,512]{2,1,0:T(8,128)(2,1)}, u32[]{:S(2)}) copy-start(bf16[4,128,512]{2,1,0:T(8,128)(2,1)} %get-tuple-element.228) | copy-start | bytes 1572868
  1071.9 6.4 copy-start.6
  1080.5 2.9 copy-start.5
  (16 other events, 30.1 us)

commit v6 on v5

--- a/solution.py
+++ b/solution.py
@@ -921,6 +921,32 @@
         in_specs=[block] * (2 * count),
         out_specs=[block] * count,
     )(*[ref for pair in pairs for ref in pair], *outputs)
+
+
+def second_norm(count, inputs, outputs):
+    x, y, parts, gain = inputs
+    m, width = parts.shape[0] - 1, parts.shape[2]
+    rows = at(lax.axis_index("mp"), count)
+
+    def body(x_ref, y_ref, parts_ref, gain_ref, sum_ref, normed_ref):
+        total = x_ref[...].astype(F32) + y_ref[...].astype(F32)
+        for k in range(m - 1):
+            total = total + parts_ref[k].astype(F32)
+        sum_ref[...] = total
+        normed_ref[...] = rms_gain(total, gain_ref[:1]).astype(BF)
+
+    block = pl.BlockSpec((count, width), lambda i: (0, 0))
+    pltpu.emit_pipeline(
+        body,
+        grid=(1,),
+        in_specs=[
+            block,
+            block,
+            pl.BlockSpec((m - 1, count, width), lambda i: (0, 0, 0)),
+            pl.BlockSpec(gain.shape, lambda i: (0, 0)),
+        ],
+        out_specs=[block, block],
+    )(x.at[rows], y.at[rows], parts.at[pl.ds(1, m - 1)], gain, *outputs)
 
 
 class Halves:
@@ -1253,17 +1279,51 @@
     y_act_parts = kernel.flow(Parts(), y_act)
     kernel.ready(gate_own)
     kernel.go(up_own)
-    w_gate = kernel.flow(Pass(1), gate_own)
     kernel.relay(y_pre_parts, 1)
     kernel.relay(y_act_parts, 1)
+    w_gate = kernel.flow(Pass(1), gate_own)
+    kernel.ready(y_pre_parts)
+    kernel.ready(y_act_parts)
+    x2_pre, h2_pre = kernel.new_output((rq, wide), F32), kernel.new_output((rq, wide), BF)
+    x2_act, h2_act = kernel.new_output((aq, narrow), F32), kernel.new_output((aq, narrow), BF)
+    kernel.job(
+        functools.partial(second_norm, rq),
+        [x_pre, y_pre, y_pre_parts, jnp.broadcast_to(gain_pf, (8, wide))],
+        [],
+        into=[x2_pre, h2_pre],
+    )
+    kernel.job(
+        functools.partial(second_norm, aq),
+        [x_act, y_act, y_act_parts, jnp.broadcast_to(gain_af, (8, narrow))],
+        [],
+        into=[x2_act, h2_act],
+    )
+    h2_pre = kernel.flow(Line(), h2_pre)
+    h2_act = kernel.flow(Line(by_lead, (n, aq, narrow)), h2_act)
     kernel.relay(w_gate, 1)
+    kernel.relay(h2_pre, 1)
+    kernel.relay(h2_act, 1)
+    kernel.relay(w_gate, 2)
     down_own = kernel.flow(Rows(), pre_down)
-    kernel.relay(w_gate, 2)
+    if even:
+        act_own = [kernel.flow(Columns(), act_gate), kernel.flow(Columns(), act_up)]
+        act_own.append(kernel.flow(Rows(), act_down))
+    else:
+        act_own = [kernel.flow(Each(), act_weights)]
+    kernel.ready(up_own)
+    w_up = kernel.flow(Pass(1), up_own)
+    for k in range(2, half):
+        kernel.relay(h2_pre, k)
+        kernel.relay(h2_act, k)
+        if k < 4:
+            kernel.relay(w_up, k - 1)
     got = kernel.call("attend")
     probs, mixed = [got[p] for p in probs], [got[o] for o in mixed]
     query, keys, values = [got[q] for q in query], got[keys], got[values]
     h1_pre, h1_act = got[h1_pre], got[h1_act]
-    up_own, down_own, w_gate = got[up_own], got[down_own], got[w_gate]
+    down_own, w_gate, w_up = got[down_own], got[w_gate], got[w_up]
+    x2_pre, x2_act = got[x2_pre], got[x2_act]
+    h2_pre, h2_act = got[h2_pre].reshape(n * rq, wide), got[h2_act].reshape(n * aq, narrow)
 
     def summed(first, parts, count=None):
         value = first.astype(F32)
@@ -1271,34 +1331,16 @@
             value = value + parts[k].astype(F32)
         return value
 
-    x2_pre = own(x_pre, rq).astype(F32) + summed(own(got[y_pre], rq), got[y_pre_parts], m)
-    x2_act = own(x_act, aq) + summed(own(got[y_act], aq), got[y_act_parts], m)
-    h2_pre = rms_gain(x2_pre, gain_pf).astype(BF)
-    h2_act = rms_gain(x2_act, gain_af).astype(BF)
-
-    kernel = Kernel(3)
-    h2_pre = kernel.flow(Line(), h2_pre)
-    h2_act = kernel.flow(Line(by_lead, (n, aq, narrow)), h2_act)
-    w_up = kernel.flow(Pass(1), up_own)
-    if even:
-        act_own = [kernel.flow(Columns(), act_gate), kernel.flow(Columns(), act_up)]
-        act_own.append(kernel.flow(Rows(), act_down))
-    else:
-        act_own = [kernel.flow(Each(), act_weights)]
-    for k in range(1, half):
-        kernel.relay(h2_pre, k)
-        kernel.relay(h2_act, k)
-        if k < 3:
-            kernel.relay(w_up, k)
-    got = kernel.call("spread")
     act_own = [got[a] for a in act_own]
-    h2_pre, h2_act = got[h2_pre].reshape(n * rq, wide), got[h2_act].reshape(n * aq, narrow)
-    w_up = got[w_up]
     items, units = h2_pre.shape[0], w_gate.shape[1]
     summing = Halves if m == 4 else Direct
 
+    def in_turn_rows(ref, i, j):
+        chip = lax.rem(i // 2 - j // 2 + half, half)
+        return ref.at[at(chip + half * lax.rem(i + j, 2), rq)]
+
     kernel = Kernel(4)
-    gz_all = kernel.flow(Line(), gz_pre)
+    gz_all = kernel.flow(Line(in_turn_rows, (items, wide)), gz_pre)
     w_down = kernel.flow(Pass(0), down_own)
     into = None
     for piece in range(2):
@@ -1309,31 +1351,29 @@
             into=into,
         )
         kernel.relay(gz_all, piece + 1)
+    gate, upward, hidden = into
     kernel.relay(w_down, 1)
     kernel.relay(w_down, 2)
     for k in range(3, half):
         kernel.relay(gz_all, k)
-    got = kernel.call("hidden")
-    gate, upward, hidden = [got[o] for o in into]
-    w_down, gz_pre_all = got[w_down], got[gz_all].reshape(n * rq, wide)
-
-    kernel = Kernel(5)
     if even:
         act_all_w = [kernel.flow(Pass(axis), a) for axis, a in zip((1, 1, 0), act_own)]
     else:
         act_all_w = [kernel.flow(Pass(0), act_own[0].reshape(n * 3 * d_act, few))]
-    g_down = kernel.job(products_left, [hidden, gz_pre_all], [(units, wide)])
+    kernel.ready(gz_all)
+    g_down = kernel.job(products_left, [hidden, gz_all], [(units, wide)])
     down_sum, gate_sum, up_sum = summing(0), summing(1), summing(1)
     down_sum.first(kernel, g_down)
+    kernel.ready(w_down)
     z_p = kernel.job(products_plain, [hidden, w_down], [(items, wide)])
     z_p_core = kernel.flow(Core(), z_p)
     for k in (1, 2):
         for a in act_all_w:
             kernel.relay(a, k)
     dgate, dup = kernel.job(
-        hidden_backward, [gz_pre_all, w_down, gate, upward], [(items, units)] * 2
+        hidden_backward, [gz_all, w_down, gate, upward], [(items, units)] * 2
     )
-    got = kernel.call("hidden_grads")
+    got = kernel.call("hidden")
     dgate, dup = got[dgate], got[dup]
     down_sum.settle(got)
 

time: 1100 us -> 1080 us (0.982)
  Pallas kernels: 938 us -> 916 us
    pallas_call x10 -> x8, Pallas kernels: 938 us -> 916 us  [call(): pl.pallas_call(kernel, out_shape=self.outputs, in_specs=[HBM] * takes, ou...]
where the time goes in v6:
time: 1080 us; the launch traced here: 1070 us
  Pallas kernels  916 us (85%)
  other arithmetic  87.2 us (8%)
  local copies, waits for them, and re-layouts  45.4 us (4%)
    pallas_call x8, Pallas kernels, call(): pl.pallas_call(kernel, out_shape=self.outputs, in_specs=[HBM] * takes, ou...  916 us
  transfers between devices with their start and end apart: 2, of which 0 were waited for; matrix products, arithmetic and copies ran while one was open for 3% of the time, Pallas kernels for 0%

profile of v6, /device:TPU:0, one launch (start us, length us, event | category | flops | bytes accessed | tf_op | source)
XLA Modules:
  0.0 1066.6 jit_solution(12627086125552683204)
XLA Ops:
  11.2 86.5 %gather.1 = (bf16[2048,1024]{1,0:T(8,128)(2,1)}, bf16[1024,1024]{1,0:T(8,128)(2,1)}, bf16[8,128,128]{2,1,0:T(8,128)(2,1)}, s32[8,8,128]{2,1,0:T(8,128)}, bf16[51...) custom-call(bf16[256,128]{1,0:T(8,128)(2,1)} %fusion.24.refs_0_, ...), custom_call_target="tpu_custom_call" | custom-call | tf_op jit(solution)/shard_map/gather/pallas_call | solution.py:663
  103.1 2.1 reshape.511
  106.9 2.0 convolution_convert_fusion
  108.9 1.8 reshape.512.refs_6_
  114.1 2.2 pad.48.refs_2_.refs_14_
  122.0 225.7 %attend.1 = (bf16[2048,512]{1,0:T(8,128)(2,1)}, bf16[2048,512]{1,0:T(8,128)(2,1)}, bf16[832,2048]{1,0:T(8,128)(2,1)}, bf16[896,256]{1,0:T(8,128)(2,1)}, bf16[896...) custom-call(bf16[256,4096]{1,0:T(8,128)(2,1)} %refs_0_.1, ...), custom_call_target="tpu_custom_call" | custom-call | tf_op jit(solution)/shard_map/attend/pallas_call | solution.py:663
  349.3 2.2 pad_dynamic-slice_fusion.refs_0_
  351.5 153.4 %hidden.1 = (bf16[1664,2048]{1,0:T(8,128)(2,1)}, bf16[2048,2048]{1,0:T(8,128)(2,1)}, bf16[1664,2048]{1,0:T(8,128)(2,1)}, bf16[1664,2048]{1,0:T(8,128)(2,1)}, bf1...) custom-call(bf16[208,2048]{1,0:T(8,128)(2,1)} %pad_dynamic-slice_fus, ...), custom_call_target="tpu_custom_call" | custom-call | tf_op jit(solution)/shard_map/hidden/pallas_call | solution.py:663
  504.9 6.5 add_convert_fusion.1
  511.4 82.1 %in_grads.1 = (bf16[4,208,2048]{2,1,0:T(8,128)(2,1)}, bf16[512,1024]{1,0:T(8,128)(2,1)}, bf16[512,1024]{1,0:T(8,128)(2,1)}, bf16[512,1024]{1,0:T(8,128)(2,1)}, b...) custom-call(bf16[4,208,2048]{2,1,0:T(8,128)(2,1)} %bitcast.317, ...), custom_call_target="tpu_custom_call" | custom-call | tf_op jit(solution)/shard_map/in_grads/pallas_call | solution.py:663
  595.2 64.2 %row_grads.1 = (bf16[4,1024,512]{2,1,0:T(8,128)(2,1)}, bf16[512,2048]{1,0:T(8,128)(2,1)}, bf16[4096,256]{1,0:T(8,128)(2,1)}, bf16[8,16,1024]{2,1,0:T(8,128)(2,1)...) custom-call(bf16[2048,2048]{1,0:T(8,128)(2,1)} %get-tuple-element.144.refs_0_.refs_7_, ...), custom_call_target="tpu_custom_call" | custom-call | tf_op jit(solution)/shard_map/row_grads/pallas_call | solution.py:663
  659.5 6.5 add_convert_fusion
  666.0 85.5 %sum_rows.1 = (bf16[4,208,2048]{2,1,0:T(8,128)(2,1)}, bf16[8,16,1024]{2,1,0:T(8,128)(2,1)}, bf16[5,1024,128]{2,1,0:T(8,128)(2,1)}, bf16[5,1024,128]{2,1,0:T(8,12...) custom-call(bf16[4,208,2048]{2,1,0:T(8,128)(2,1)} %bitcast.318, ...), custom_call_target="tpu_custom_call" | custom-call | tf_op jit(solution)/shard_map/sum_rows/pallas_call | solution.py:663
  751.5 2.2 fusion.15.refs_22_
  753.7 2.0 fusion.16.refs_21_
  755.7 2.0 fusion.17.refs_20_
  757.8 4.6 multiply_reduce_fusion.1
  765.7 3.7 fusion.45.refs_0_
  769.4 124.4 %heads.1 = (bf16[832,2048]{1,0:T(8,128)(2,1)}, bf16[64,1024]{1,0:T(8,128)(2,1)}, bf16[2048,512]{1,0:T(8,128)(2,1)}, bf16[256,4096]{1,0:T(8,128)(2,1)}, bf16[2048...) custom-call(bf16[208,2048]{1,0:T(8,128)(2,1)} %fusion.45.refs_0_, ...), custom_call_target="tpu_custom_call" | custom-call | tf_op jit(solution)/shard_map/heads/pallas_call | solution.py:663
  896.8 1.7 constant_dynamic-slice_fusion.1
  898.9 3.2 convolution_convert_fusion.1
  908.9 3.0 fusion.8
  912.9 4.3 fusion.4.refs_6_
  925.0 2.3 convert_element_type.740
  930.5 2.5 convert_element_type.738
  933.1 2.5 convert_element_type.739
  937.2 1.7 fusion.14.refs_4_
  938.9 93.9 %finish.1 = (bf16[4,256,512]{2,1,0:T(8,128)(2,1)}, bf16[4,256,512]{2,1,0:T(8,128)(2,1)}, bf16[4,128,512]{2,1,0:T(8,128)(2,1)}, bf16[4,128,512]{2,1,0:T(8,128)(2,...) custom-call(bf16[1024,512]{1,0:T(8,128)(2,1)} %fusion.1.refs_0_, ...), custom_call_target="tpu_custom_call" | custom-call | tf_op jit(solution)/shard_map/finish/pallas_call | solution.py:663
  1037.5 8.8 all_gather.3
  1053.4 1.9 convert_add_fusion.16
  1055.3 4.2 slice.292
  1061.8 3.7 slice_convert_fusion
  (232 shorter events, 71.7 us)
Async XLA Ops:
  0.7 101.8 %copy-start.53 = (s32[1,816]{1,0:T(1,128)S(1)}, s32[1,816]{1,0:T(1,128)}, u32[]{:S(2)}) copy-start(s32[1,816]{1,0:T(1,128)} %param.30) | copy-start | bytes 9796
  8.3 2.9 copy-start.42
  97.8 16.3 %copy-start = (bf16[816,2048]{1,0:T(8,128)(2,1)S(1)}, bf16[816,2048]{1,0:T(8,128)(2,1)}, u32[]{:S(2)}) copy-start(bf16[816,2048]{1,0:T(8,128)(2,1)} %param.26) | copy-start | bytes 10027012
  110.7 8.7 copy-start.36
  111.6 9.1 copy-start.39
  349.3 408.4 %copy-start.45 = (f32[208]{0:T(256)}, f32[208]{0:T(256)S(1)}, u32[]{:S(2)}) copy-start(f32[208]{0:T(256)S(1)} %fusion.38) | copy-start | bytes 2500
  511.4 83.1 %copy-start.17 = (f32[16,1024]{1,0:T(8,128)S(1)}, f32[16,1024]{1,0:T(8,128)}, u32[]{:S(2)}) copy-start(f32[16,1024]{1,0:T(8,128)} %get-tuple-element.149) | copy-start | bytes 196612
  666.0 91.8 %copy-start.10 = (bf16[4,208,2048]{2,1,0:T(8,128)(2,1)S(1)}, bf16[4,208,2048]{2,1,0:T(8,128)(2,1)}, u32[]{:S(2)}) copy-start(bf16[4,208,2048]{2,1,0:T(8,128)(2,1)} %get-tuple-element.196) | copy-start | bytes 10223620
  751.5 6.3 copy-start.2
  757.7 5.2 copy-start.30
  757.7 5.2 copy-start.37
  769.4 126.5 %copy-start.12 = (bf16[64,1024]{1,0:T(8,128)(2,1)S(1)}, bf16[64,1024]{1,0:T(8,128)(2,1)}, u32[]{:S(2)}) copy-start(bf16[64,1024]{1,0:T(8,128)(2,1)} %get-tuple-element.182.refs_26_.refs_30_) | copy-start | bytes 393220
  898.5 37.0 %collective-permute-start.1 = (bf16[512,128]{1,0:T(8,128)(2,1)}, bf16[512,128]{1,0:T(8,128)(2,1)}, u32[]{:S(2)}, u32[]{:S(2)}) collective-permute-start(bf16[512,128]{1,0:T(8,128)(2,1)} %bitcast.43), channel_id=1, source_target_pairs={{0,4},{4,0},{8,12},{12,8},{16,20},{20,16},{24,28},{28,24},{1,5},{5... | collective-permute-start | bytes 393224 | tf_op jit(solution)/shard_map/ppermute | solution.py:1546
  902.9 34.3 %collective-permute-start = (bf16[1024,128]{1,0:T(8,128)(2,1)}, bf16[1024,128]{1,0:T(8,128)(2,1)}, u32[]{:S(2)}, u32[]{:S(2)}) collective-permute-start(bf16[1024,128]{1,0:T(8,128)(2,1)} %bitcast.39), channel_id=1, source_target_pairs={{0,4},{4,0},{8,12},{12,8},{16,20},{20,16},{24,28},{28,24},{1,5},{5... | collective-permute-start | bytes 786440 | tf_op jit(solution)/shard_map/ppermute | solution.py:1546
  908.9 3.1 copy-start.48
  908.9 3.1 copy-start.1
  908.9 3.5 copy-start.3
  908.9 4.0 copy-start.4
  908.9 4.0 copy-start.46
  908.9 4.0 copy-start.47
  912.9 4.3 copy-start.22
  921.8 3.2 copy-start.7
  925.0 3.0 copy-start.29
  925.0 3.9 copy-start.28
  925.0 4.7 copy-start.27
  933.1 4.1 copy-start.16
  1032.8 15.0 %copy-start.25 = (bf16[4,128,512]{2,1,0:T(8,128)(2,1)S(1)}, bf16[4,128,512]{2,1,0:T(8,128)(2,1)}, u32[]{:S(2)}) copy-start(bf16[4,128,512]{2,1,0:T(8,128)(2,1)} %get-tuple-element.213) | copy-start | bytes 1572868
  1034.0 15.7 %copy-start.24 = (bf16[4,128,512]{2,1,0:T(8,128)(2,1)S(1)}, bf16[4,128,512]{2,1,0:T(8,128)(2,1)}, u32[]{:S(2)}) copy-start(bf16[4,128,512]{2,1,0:T(8,128)(2,1)} %get-tuple-element.212) | copy-start | bytes 1572868
  1037.5 13.8 %copy-start.19 = (bf16[4,256,512]{2,1,0:T(8,128)(2,1)S(1)}, bf16[4,256,512]{2,1,0:T(8,128)(2,1)}, u32[]{:S(2)}) copy-start(bf16[4,256,512]{2,1,0:T(8,128)(2,1)} %get-tuple-element.208) | copy-start | bytes 3145732
  1048.8 4.6 copy-start.18
  1055.3 4.2 copy-start.41
  1055.3 4.5 copy-start.15
  (28 other events, 48.8 us)

commit v7 on v6

--- a/solution.py
+++ b/solution.py
@@ -1373,14 +1373,18 @@
     dgate, dup = kernel.job(
         hidden_backward, [gz_all, w_down, gate, upward], [(items, units)] * 2
     )
+
+    def pair_sum(inputs, outputs):
+        parts, other = inputs
+        add_pairs([(parts.at[pl.ds(0, other.shape[0])], other)], outputs)
+
+    kernel.ready(z_p_core)
+    z_p = kernel.job(pair_sum, [z_p, z_p_core], [(items // 2, wide)])
     got = kernel.call("hidden")
     dgate, dup = got[dgate], got[dup]
     down_sum.settle(got)
 
-    def pair_sum(parts, other):
-        return add(parts[: other.shape[0]], other).reshape(half, -1, other.shape[1])
-
-    z_p = pair_sum(got[z_p], got[z_p_core])
+    z_p = got[z_p].reshape(half, rq, wide)
     if even:
         act_gate_w, act_up_w, act_down_w = [got[a] for a in act_all_w]
     else:
@@ -1388,9 +1392,11 @@
         act_gate_w, act_up_w, act_down_w = act_all_w.reshape(3, narrow, m * few)
         act_down_w = act_down_w.T
 
-    match = (lax.broadcasted_iota(jnp.int32, (n, 1), 0) == slot_all[None, :]).astype(BF)
-    cot_all = cot_all.reshape(n * slot_count, aq * narrow)
-    gz_act_all = dot_plain(match, cot_all).astype(BF).reshape(n * aq, narrow)
+    to_rows = lax.broadcasted_iota(jnp.int32, (n * aq, 1), 0)
+    from_rows = lax.broadcasted_iota(jnp.int32, (1, n * slot_count * aq), 1)
+    match = (to_rows // aq == jnp.repeat(slot_all, aq)[None, :]) & (to_rows % aq == from_rows % aq)
+    cot_all = cot_all.reshape(n * slot_count * aq, narrow)
+    gz_act_all = dot_plain(match.astype(BF), cot_all).astype(BF)
     gz_act = lax.dynamic_slice_in_dim(gz_act_all, me * aq, aq, 0)
     kernel = Kernel(6)
     z_p_parts = kernel.flow(Chips(), z_p)
@@ -1424,11 +1430,13 @@
     dh2_p_core = kernel.flow(Core(), dh2_p)
     for k in range(1, half):
         kernel.relay(out_act, k)
+    kernel.ready(dh2_p_core)
+    dh2_p = kernel.job(pair_sum, [dh2_p, dh2_p_core], [(items // 2, wide)])
     got = kernel.call("row_grads")
     out_act = got[out_act].reshape(n * aq, narrow)
     up_sum.settle(got)
     grad_down = got[grad_down].astype(F32)
-    dh2_p = pair_sum(got[dh2_p], got[dh2_p_core])
+    dh2_p = got[dh2_p].reshape(half, rq, wide)
 
     kernel = Kernel(8)
     dh2_p_parts, dh2_a = kernel.flow(Chips(), dh2_p), kernel.flow(EachRows(), dh2_a)

time: 1080 us -> 1070 us (level)
  other arithmetic: 87.2 us -> 75.3 us
    convert_element_type x8 -> x6, other arithmetic: 20.9 us -> 7.91 us  [add(): return (left.astype(F32) + right.astype(F32)).astype(BF)]
where the time goes in v7:
time: 1070 us; the launch traced here: 1060 us
  Pallas kernels  926 us (87%)
  other arithmetic  75.3 us (7%)
  local copies, waits for them, and re-layouts  42.1 us (4%)
    pallas_call x8, Pallas kernels, call(): pl.pallas_call(kernel, out_shape=self.outputs, in_specs=[HBM] * takes, ou...  926 us
  transfers between devices with their start and end apart: 2, of which 0 were waited for; matrix products, arithmetic and copies ran while one was open for 3% of the time, Pallas kernels for 0%

profile of v7, /device:TPU:0, one launch (start us, length us, event | category | flops | bytes accessed | tf_op | source)
XLA Modules:
  0.0 1061.2 jit_solution(8287708497564355096)
XLA Ops:
  10.8 1.5 fusion.27.refs_0_
  12.3 86.5 %gather.1 = (bf16[2048,1024]{1,0:T(8,128)(2,1)}, bf16[1024,1024]{1,0:T(8,128)(2,1)}, bf16[8,128,128]{2,1,0:T(8,128)(2,1)}, s32[8,8,128]{2,1,0:T(8,128)}, bf16[51...) custom-call(bf16[256,128]{1,0:T(8,128)(2,1)} %fusion.27.refs_0_, ...), custom_call_target="tpu_custom_call" | custom-call | tf_op jit(solution)/shard_map/gather/pallas_call | solution.py:663
  109.9 2.2 pad.48.refs_2_.refs_14_
  117.8 225.7 %attend.1 = (bf16[2048,512]{1,0:T(8,128)(2,1)}, bf16[2048,512]{1,0:T(8,128)(2,1)}, bf16[832,2048]{1,0:T(8,128)(2,1)}, bf16[896,256]{1,0:T(8,128)(2,1)}, bf16[896...) custom-call(bf16[256,4096]{1,0:T(8,128)(2,1)} %refs_0_.1, ...), custom_call_target="tpu_custom_call" | custom-call | tf_op jit(solution)/shard_map/attend/pallas_call | solution.py:663
  343.5 1.6 multiply_reduce_fusion.3
  345.3 2.2 pad_dynamic-slice_fusion.refs_0_
  348.5 158.8 %hidden.1 = (bf16[1664,2048]{1,0:T(8,128)(2,1)}, bf16[2048,2048]{1,0:T(8,128)(2,1)}, bf16[1664,2048]{1,0:T(8,128)(2,1)}, bf16[1664,2048]{1,0:T(8,128)(2,1)}, bf1...) custom-call(bf16[208,2048]{1,0:T(8,128)(2,1)} %pad_dynamic-slice_fus, ...), custom_call_target="tpu_custom_call" | custom-call | tf_op jit(solution)/shard_map/hidden/pallas_call | solution.py:663
  507.3 82.2 %in_grads.1 = (bf16[4,208,2048]{2,1,0:T(8,128)(2,1)}, bf16[512,1024]{1,0:T(8,128)(2,1)}, bf16[512,1024]{1,0:T(8,128)(2,1)}, bf16[512,1024]{1,0:T(8,128)(2,1)}, b...) custom-call(bf16[4,208,2048]{2,1,0:T(8,128)(2,1)} %bitcast.318, ...), custom_call_target="tpu_custom_call" | custom-call | tf_op jit(solution)/shard_map/in_grads/pallas_call | solution.py:663
  591.2 68.4 %row_grads.1 = (bf16[4,1024,512]{2,1,0:T(8,128)(2,1)}, bf16[512,2048]{1,0:T(8,128)(2,1)}, bf16[4096,256]{1,0:T(8,128)(2,1)}, bf16[8,16,1024]{2,1,0:T(8,128)(2,1)...) custom-call(bf16[2048,2048]{1,0:T(8,128)(2,1)} %get-tuple-element.141.refs_0_.refs_7_, ...), custom_call_target="tpu_custom_call" | custom-call | tf_op jit(solution)/shard_map/row_grads/pallas_call | solution.py:663
  659.7 84.5 %sum_rows.1 = (bf16[4,208,2048]{2,1,0:T(8,128)(2,1)}, bf16[8,16,1024]{2,1,0:T(8,128)(2,1)}, bf16[5,1024,128]{2,1,0:T(8,128)(2,1)}, bf16[5,1024,128]{2,1,0:T(8,12...) custom-call(bf16[4,208,2048]{2,1,0:T(8,128)(2,1)} %bitcast.319, ...), custom_call_target="tpu_custom_call" | custom-call | tf_op jit(solution)/shard_map/sum_rows/pallas_call | solution.py:663
  744.2 2.2 fusion.15.refs_22_
  746.3 2.0 fusion.16.refs_21_
  748.4 2.0 fusion.17.refs_20_
  750.4 4.7 multiply_reduce_fusion.1
  757.0 1.5 fusion.50.refs_1_
  758.5 3.7 fusion.51.refs_0_
  762.2 125.8 %heads.1 = (bf16[832,2048]{1,0:T(8,128)(2,1)}, bf16[64,1024]{1,0:T(8,128)(2,1)}, bf16[2048,512]{1,0:T(8,128)(2,1)}, bf16[256,4096]{1,0:T(8,128)(2,1)}, bf16[2048...) custom-call(bf16[208,2048]{1,0:T(8,128)(2,1)} %fusion.51.refs_0_, ...), custom_call_target="tpu_custom_call" | custom-call | tf_op jit(solution)/shard_map/heads/pallas_call | solution.py:663
  891.1 1.7 constant_dynamic-slice_fusion.1
  893.1 3.2 convolution_convert_fusion
  903.2 3.0 fusion.8
  907.1 4.3 fusion.4.refs_6_
  919.0 2.3 convert_element_type.716
  924.5 2.5 convert_element_type.714
  927.0 2.5 convert_element_type.715
  929.6 1.6 fusion.19.refs_5_
  931.2 1.7 fusion.14.refs_4_
  932.9 93.9 %finish.1 = (bf16[4,256,512]{2,1,0:T(8,128)(2,1)}, bf16[4,256,512]{2,1,0:T(8,128)(2,1)}, bf16[4,128,512]{2,1,0:T(8,128)(2,1)}, bf16[4,128,512]{2,1,0:T(8,128)(2,...) custom-call(bf16[1024,512]{1,0:T(8,128)(2,1)} %fusion.1.refs_0_, ...), custom_call_target="tpu_custom_call" | custom-call | tf_op jit(solution)/shard_map/finish/pallas_call | solution.py:663
  1031.5 9.1 all_gather.3
  1044.0 1.7 convert_add_fusion.32
  1047.7 1.9 convert_add_fusion.16
  1049.6 4.2 slice.284
  1056.2 3.7 slice_convert_fusion
  (242 shorter events, 66.2 us)
Async XLA Ops:
  0.7 102.7 %copy-start.55 = (s32[1,816]{1,0:T(1,128)S(1)}, s32[1,816]{1,0:T(1,128)}, u32[]{:S(2)}) copy-start(s32[1,816]{1,0:T(1,128)} %param.30) | copy-start | bytes 9796
  0.7 109.2 %copy-start = (bf16[816,2048]{1,0:T(8,128)(2,1)S(1)}, bf16[816,2048]{1,0:T(8,128)(2,1)}, u32[]{:S(2)}) copy-start(bf16[816,2048]{1,0:T(8,128)(2,1)} %param.26) | copy-start | bytes 10027012
  9.4 2.9 copy-start.43
  106.5 8.7 copy-start.37
  107.4 9.1 copy-start.40
  345.2 405.2 %copy-start.46 = (f32[208]{0:T(256)}, f32[208]{0:T(256)S(1)}, u32[]{:S(2)}) copy-start(f32[208]{0:T(256)S(1)} %fusion.44) | copy-start | bytes 2500
  507.3 83.2 %copy-start.17 = (f32[16,1024]{1,0:T(8,128)S(1)}, f32[16,1024]{1,0:T(8,128)}, u32[]{:S(2)}) copy-start(f32[16,1024]{1,0:T(8,128)} %get-tuple-element.146) | copy-start | bytes 196612
  659.6 90.7 %copy-start.10 = (bf16[4,208,2048]{2,1,0:T(8,128)(2,1)S(1)}, bf16[4,208,2048]{2,1,0:T(8,128)(2,1)}, u32[]{:S(2)}) copy-start(bf16[4,208,2048]{2,1,0:T(8,128)(2,1)} %get-tuple-element.192) | copy-start | bytes 10223620
  744.1 6.3 copy-start.2
  750.4 5.3 copy-start.31
  750.4 5.4 copy-start.38
  762.2 127.9 %copy-start.12 = (bf16[64,1024]{1,0:T(8,128)(2,1)S(1)}, bf16[64,1024]{1,0:T(8,128)(2,1)}, u32[]{:S(2)}) copy-start(bf16[64,1024]{1,0:T(8,128)(2,1)} %get-tuple-element.178.refs_26_.refs_30_) | copy-start | bytes 393220
  892.8 36.8 %collective-permute-start.1 = (bf16[512,128]{1,0:T(8,128)(2,1)}, bf16[512,128]{1,0:T(8,128)(2,1)}, u32[]{:S(2)}, u32[]{:S(2)}) collective-permute-start(bf16[512,128]{1,0:T(8,128)(2,1)} %bitcast.44), channel_id=1, source_target_pairs={{0,4},{4,0},{8,12},{12,8},{16,20},{20,16},{24,28},{28,24},{1,5},{5... | collective-permute-start | bytes 393224 | tf_op jit(solution)/shard_map/ppermute | solution.py:1554
  897.1 34.0 %collective-permute-start = (bf16[1024,128]{1,0:T(8,128)(2,1)}, bf16[1024,128]{1,0:T(8,128)(2,1)}, u32[]{:S(2)}, u32[]{:S(2)}) collective-permute-start(bf16[1024,128]{1,0:T(8,128)(2,1)} %bitcast.40), channel_id=1, source_target_pairs={{0,4},{4,0},{8,12},{12,8},{16,20},{20,16},{24,28},{28,24},{1,5},{5... | collective-permute-start | bytes 786440 | tf_op jit(solution)/shard_map/ppermute | solution.py:1554
  903.1 3.1 copy-start.49
  903.1 3.1 copy-start.1
  903.1 3.5 copy-start.3
  903.1 4.0 copy-start.4
  903.1 4.0 copy-start.47
  903.2 4.0 copy-start.48
  907.1 4.4 copy-start.22
  916.0 3.0 copy-start.7
  919.0 3.0 copy-start.30
  919.0 3.9 copy-start.29
  919.0 4.7 copy-start.28
  927.0 4.1 copy-start.16
  1026.8 15.3 %copy-start.26 = (bf16[4,128,512]{2,1,0:T(8,128)(2,1)S(1)}, bf16[4,128,512]{2,1,0:T(8,128)(2,1)}, u32[]{:S(2)}) copy-start(bf16[4,128,512]{2,1,0:T(8,128)(2,1)} %get-tuple-element.209) | copy-start | bytes 1572868
  1028.0 16.0 %copy-start.25 = (bf16[4,128,512]{2,1,0:T(8,128)(2,1)S(1)}, bf16[4,128,512]{2,1,0:T(8,128)(2,1)}, u32[]{:S(2)}) copy-start(bf16[4,128,512]{2,1,0:T(8,128)(2,1)} %get-tuple-element.208) | copy-start | bytes 1572868
  1031.5 14.2 %copy-start.19 = (bf16[4,256,512]{2,1,0:T(8,128)(2,1)S(1)}, bf16[4,256,512]{2,1,0:T(8,128)(2,1)}, u32[]{:S(2)}) copy-start(bf16[4,256,512]{2,1,0:T(8,128)(2,1)} %get-tuple-element.204) | copy-start | bytes 3145732
  1043.1 4.6 copy-start.18
  1049.6 4.2 copy-start.42
  1049.6 4.5 copy-start.15
  (33 other events, 60.0 us)
